TPU v7x, 32 devices: a whole 2x2x4 slice. The times are simulated.
32 devices in a mesh: ent: 8 (over z, x), rep: 4 (over y, core).
Axes of the slice: x: 2, y: 2, z: 4, core: 2. Of those that a mesh axis runs over, the one named last changes fastest.
Arguments:
- entity_table: float32 [8192, 200], P('ent'), may hold values from -1.8 to 1.8
- entity_state: float32 [8192], P('ent'), may hold values from 1e-05 to 1
- operators: float32 [16, 200, 200], P('ent'), may hold values from -0.4375 to 0.4375
- operator_state: float32 [16, 200, 200], P('ent'), may hold values from 1 to 100
- sources: int32 [8192], P(('ent', 'rep')), may hold values from 0 to 1023
- destinations: int32 [8192], P(('ent', 'rep')), may hold values from 0 to 1023
- relations: int32 [8192, 1], P(('ent', 'rep')), may hold values from 0 to 15; in each aligned block of 256 rows (0 to 255, 256 to 511, ...) at most 32 rows name the same one
- negatives: int32 [32, 1000], P(('ent', 'rep')), may hold values from 0 to 1023
Outputs:
- new_table: float32 [8192, 200], P('ent')
- new_entity_state: float32 [8192], P('ent')
- new_operators: float32 [16, 200, 200], P('ent')
- new_operator_state: float32 [16, 200, 200], P('ent')
Inputs may be any that keep to these rules, and one draw needn't show every extreme that they name: `relations`: among the 256 edges of one device no relation occurs more than 32 times, and some relation occurs exactly 32 times.
All inputs are finite; a program needn't handle non-finite values.
Results may differ from a plain program's by a relative error of at most 0.0019.
Values may be sent and summed in bfloat16 or wider, within the bound.
No kernel may reach another device: no remote copies, remote signals or barrier semaphores. Data moves between devices by JAX's collectives and lax.ppermute only.
A program may use at most 64 MiB of HBM per device.

v0:
```python
import jax
import jax.numpy as jnp
from jax import lax
from jax.sharding import PartitionSpec as P

SPAN = 256
EDGE_DEV = 256
REL_DEV = 2


entity_rate = 0.1
operator_rate = 0.02
epsilon = 1e-06


def passed_along(array, axis, by):
    peers = lax.axis_size(axis)
    return lax.ppermute(array, axis, [(i, (i + by) % peers) for i in range(peers)])


def place_slots(relation_ids, capacity):
    count_edges = relation_ids.shape[0]
    ordering = jnp.argsort(relation_ids, stable=True)
    ranked = relation_ids[ordering]
    leading = jnp.searchsorted(ranked, ranked, side="left")
    within = jnp.arange(count_edges, dtype=jnp.int32) - leading
    position = jnp.zeros((count_edges,), jnp.int32).at[ordering].set(within)
    return relation_ids * capacity + position


def score_grads(transformed, target_ids, negative_ids, table_rows):
    target_rows = jnp.take(table_rows, target_ids, axis=0)
    positive = jnp.sum(transformed.astype(jnp.float32) * target_rows.astype(jnp.float32), axis=-1)
    positive_grad = -jax.nn.sigmoid(-positive)
    width = transformed.shape[1]
    blocks = transformed.reshape(-1, SPAN, width)
    negative_count = negative_ids.shape[1]

    def span_step(running, pieces):
        query_block, negative_block = pieces
        negative_rows = jnp.take(table_rows, negative_block, axis=0)
        scores = lax.dot_general(
            query_block, negative_rows, (((1,), (1,)), ((), ())), preferred_element_type=jnp.float32
        )
        negative_grad = (jax.nn.sigmoid(scores) / negative_count).astype(jnp.bfloat16)
        query_part = jnp.dot(negative_grad, negative_rows, preferred_element_type=jnp.float32)
        row_update = lax.dot_general(
            negative_grad, query_block, (((0,), (0,)), ((), ())), preferred_element_type=jnp.float32
        )
        return (running.at[negative_block].add(row_update), query_part)

    starting = jnp.zeros((table_rows.shape[0], width), jnp.float32)
    negative_total, query_parts = lax.scan(span_step, starting, (blocks, negative_ids))
    query_grad = (
        positive_grad[:, None] * target_rows.astype(jnp.float32) + query_parts.reshape(-1, width)
    ).astype(jnp.bfloat16)
    target_grad = negative_total.at[target_ids].add(
        positive_grad[:, None] * transformed.astype(jnp.float32)
    )
    return (query_grad, target_grad)


def row_adagrad(weights, moments, gradient):
    fresh_moments = moments + jnp.mean(gradient * gradient, axis=-1)
    updated = weights - entity_rate * gradient / (jnp.sqrt(fresh_moments)[:, None] + epsilon)
    return (updated, fresh_moments)


def dense_adagrad(weights, moments, gradient):
    fresh_moments = moments + gradient * gradient
    updated = weights - operator_rate * gradient / (jnp.sqrt(fresh_moments) + epsilon)
    return (updated, fresh_moments)


def shards(
    entity_table,
    entity_state,
    operators,
    operator_state,
    sources,
    destinations,
    relations,
    negatives,
):
    groups = lax.axis_size("ent")
    relation_count = REL_DEV * groups
    capacity = max(2, (2 * EDGE_DEV + relation_count - 1) // relation_count)
    width = entity_table.shape[1]
    table_half = entity_table.astype(jnp.bfloat16)
    operators_half = operators.astype(jnp.bfloat16)
    slot_index = place_slots(relations[:, 0], capacity)
    source_rows = jnp.take(table_half, sources, axis=0)
    outgoing = (
        jnp.zeros((relation_count * capacity, width), jnp.bfloat16).at[slot_index].set(source_rows)
    )
    outgoing = outgoing.reshape(groups, REL_DEV, capacity, width)
    arrived = lax.all_to_all(outgoing, "ent", split_axis=0, concat_axis=0, tiled=True)
    result = jnp.einsum(
        "srmd,rdk->srmk", arrived, operators_half, preferred_element_type=jnp.float32
    ).astype(jnp.bfloat16)
    returned = lax.all_to_all(result, "ent", split_axis=0, concat_axis=0, tiled=True)
    transformed_slots = returned
    transformed = jnp.take(transformed_slots.reshape(-1, width), slot_index, axis=0)
    neighbour_table = passed_along(table_half, "ent", -1)
    query_grad, target_grad = score_grads(transformed, destinations, negatives, neighbour_table)
    home_grad = passed_along(target_grad, "ent", 1)
    grad_slots = (
        jnp.zeros((relation_count * capacity, width), jnp.bfloat16).at[slot_index].set(query_grad)
    )
    grad_slots = grad_slots.reshape(groups, REL_DEV, capacity, width)
    arrived_grads = lax.all_to_all(grad_slots, "ent", split_axis=0, concat_axis=0, tiled=True)
    source_grads = jnp.einsum(
        "srmk,rdk->srmd", arrived_grads, operators_half, preferred_element_type=jnp.float32
    ).astype(jnp.bfloat16)
    returned = lax.all_to_all(source_grads, "ent", split_axis=0, concat_axis=0, tiled=True)
    operator_grad = jnp.einsum(
        "srmd,srmk->rdk", arrived, arrived_grads, preferred_element_type=jnp.float32
    )
    source_grad = jnp.take(returned.reshape(-1, width), slot_index, axis=0)
    entity_grad = (
        jnp.zeros(entity_table.shape, jnp.float32).at[sources].add(source_grad.astype(jnp.float32))
        + home_grad
    )
    total_grad, total_operator = lax.psum((entity_grad, operator_grad), "rep")
    new_table, new_entity_state = row_adagrad(entity_table, entity_state, total_grad)
    new_operators, new_operator_state = dense_adagrad(operators, operator_state, total_operator)
    return (new_table, new_entity_state, new_operators, new_operator_state)


def solution(mesh):
    placed = (
        P("ent", None),
        P("ent"),
        P("ent", None, None),
        P("ent", None, None),
        P(("ent", "rep")),
        P(("ent", "rep")),
        P(("ent", "rep"), None),
        P(("ent", "rep"), None),
    )
    return jax.shard_map(
        shards,
        mesh=mesh,
        in_specs=placed,
        out_specs=(P("ent", None), P("ent"), P("ent", None, None), P("ent", None, None)),
        check_vma=False,
    )
```

profile of v0, /device:TPU:0, one launch (start us, length us, event | category | flops | bytes accessed | tf_op | source)
XLA Modules:
  0.0 174.4 jit_solution(13409637041813159841)
XLA Ops:
  8.7 6.0 %collective-permute-start = (bf16[1024,200]{1,0:T(8,128)(2,1)S(1)}, bf16[1024,200]{1,0:T(8,128)(2,1)S(1)}, u32[]{:S(2)}, u32[]{:S(2)}) collective-permute-start(bf16[1024,200]{1,0:T(8,128)(2,1)S(1)} %convert_element_type.48), channel_id=1, source_target_pairs={{0,28},{4,0},{8,4},{12,8},{16,12},{20,16},{24,20},{28,24},{1,29},{... | collective-permute-start | bytes 1228808 | tf_op jit(solution)/shard_map/ppermute | solution.py:18
  15.5 3.2 %sort.17 = (s32[256]{0:T(256)}, s32[256]{0:T(256)S(1)}) sort(s32[256]{0:T(256)S(1)} %bitcast.29, s32[256]{0:T(256)S(1)} %iota.7), dimensions={0}, to_apply=%region_0.0 | sort | flops 2048 | bytes 4096 | tf_op jit(solution)/shard_map/jit(argsort)/sort | solution.py:23
  20.6 18.4 %while.30 = (s32[]{:T(128)}, u32[256]{0:T(256)S(1)}, u32[256]{0:T(256)S(1)}, s32[256]{0:T(256)S(1)}, s32[]{:T(128)}, /*index=5*/s32[]{:T(128)}, s32[]{}) while((s32[]{:T(128)}, u32[256]{0:T(256)S(1)}, u32[256]{0:T(256)S(1)}, s32[256]{0:T(256)S(1)}, s32[]{:T(128)}, /*index=5*/s32[]{:T(128)}, s32[]{}) %tuple.50), condition=%wide.region_2.3_spmd.clone, body=%wide.region_1.2_spmd.clone.sunk | while | flops 5636 | bytes 22117 | solution.py:25
  20.6 1.9 %gather_fusion = s32[256]{0:T(256)S(1)} fusion(s32[256]{0:T(256)S(1)} %get-tuple-element.182, u32[1024]{0:T(1024)S(1)} %pad_clamp_fusion.7), kind=kCustom, calls=%fused_computation.clone.clone.1 | custom fusion | bytes 3072 | tf_op jit(solution)/shard_map/jit(searchsorted)/jit(_searchsorted_scan_impl)/vmap(jit(_searchsorted_scan_impl))/while/body/eval_jaxpr/gather | solution.py:25
  22.7 1.9 %gather_fusion = s32[256]{0:T(256)S(1)} fusion(s32[256]{0:T(256)S(1)} %get-tuple-element.182, u32[1024]{0:T(1024)S(1)} %pad_clamp_fusion.7), kind=kCustom, calls=%fused_computation.clone.clone.1 | custom fusion | bytes 3072 | tf_op jit(solution)/shard_map/jit(searchsorted)/jit(_searchsorted_scan_impl)/vmap(jit(_searchsorted_scan_impl))/while/body/eval_jaxpr/gather | solution.py:25
  24.7 1.9 %gather_fusion = s32[256]{0:T(256)S(1)} fusion(s32[256]{0:T(256)S(1)} %get-tuple-element.182, u32[1024]{0:T(1024)S(1)} %pad_clamp_fusion.7), kind=kCustom, calls=%fused_computation.clone.clone.1 | custom fusion | bytes 3072 | tf_op jit(solution)/shard_map/jit(searchsorted)/jit(_searchsorted_scan_impl)/vmap(jit(_searchsorted_scan_impl))/while/body/eval_jaxpr/gather | solution.py:25
  26.8 1.9 %gather_fusion = s32[256]{0:T(256)S(1)} fusion(s32[256]{0:T(256)S(1)} %get-tuple-element.182, u32[1024]{0:T(1024)S(1)} %pad_clamp_fusion.7), kind=kCustom, calls=%fused_computation.clone.clone.1 | custom fusion | bytes 3072 | tf_op jit(solution)/shard_map/jit(searchsorted)/jit(_searchsorted_scan_impl)/vmap(jit(_searchsorted_scan_impl))/while/body/eval_jaxpr/gather | solution.py:25
  28.8 1.9 %gather_fusion = s32[256]{0:T(256)S(1)} fusion(s32[256]{0:T(256)S(1)} %get-tuple-element.182, u32[1024]{0:T(1024)S(1)} %pad_clamp_fusion.7), kind=kCustom, calls=%fused_computation.clone.clone.1 | custom fusion | bytes 3072 | tf_op jit(solution)/shard_map/jit(searchsorted)/jit(_searchsorted_scan_impl)/vmap(jit(_searchsorted_scan_impl))/while/body/eval_jaxpr/gather | solution.py:25
  30.8 1.9 %gather_fusion = s32[256]{0:T(256)S(1)} fusion(s32[256]{0:T(256)S(1)} %get-tuple-element.182, u32[1024]{0:T(1024)S(1)} %pad_clamp_fusion.7), kind=kCustom, calls=%fused_computation.clone.clone.1 | custom fusion | bytes 3072 | tf_op jit(solution)/shard_map/jit(searchsorted)/jit(_searchsorted_scan_impl)/vmap(jit(_searchsorted_scan_impl))/while/body/eval_jaxpr/gather | solution.py:25
  41.1 2.9 %scatter_custom_fusion.1 = bf16[512,200]{1,0:T(8,128)(2,1)} fusion(s32[256]{0:T(256)S(1)} %get-tuple-element.134, bf16[]{:T(256)} %constant.105.clone.1, pred[256]{0:T(512)(128)(4,1)S(1)} %compare_and_fusion.3, bf16[]{:T(256)} %constant.112.clone.1, bf16[1024,200]{1,0:T(8,128)(2,1)S(1)} %convert_element_type.48, s32[1024]{0:T(1024)S(1)} %pad_clamp_fusion.4), kind=kCustom, calls=%fused_computation.51 | custom fusion | flops 51200 | bytes 733700 | tf_op jit(solution)/shard_map/scatter | solution.py:94
  44.0 3.5 %all-to-all-start = ((bf16[8,2,32,200]{3,2,1,0:T(8,128)(2,1)}), bf16[8,2,32,200]{3,2,1,0:T(8,128)(2,1)S(1)}, u32[]{:S(2)}, u32[]{:S(2)}) async-start(bf16[8,2,32,200]{3,2,1,0:T(8,128)(2,1)} %bitcast.3), calls=%async_computation | async-start | bytes 524288 | tf_op jit(solution)/shard_map/all_to_all | solution.py:97
  48.3 8.2 %all-to-all-done = bf16[8,2,32,200]{3,2,1,0:T(8,128)(2,1)S(1)} async-done(((bf16[8,2,32,200]{3,2,1,0:T(8,128)(2,1)}), bf16[8,2,32,200]{3,2,1,0:T(8,128)(2,1)S(1)}, u32[]{:S(2)}, u32[]{:S(2)}) %all-to-all-start) | async-done | bytes 204832 | tf_op jit(solution)/shard_map/all_to_all | solution.py:97
  57.4 3.5 %all-to-all-start.1 = ((bf16[8,2,32,200]{3,2,1,0:T(8,128)(2,1)}), bf16[8,2,32,200]{3,2,1,0:T(8,128)(2,1)S(1)}, u32[]{:S(2)}, u32[]{:S(2)}) async-start(bf16[8,2,32,200]{3,2,1,0:T(8,128)(2,1)} %copy.29), calls=%async_computation.1 | async-start | bytes 524288 | tf_op jit(solution)/shard_map/all_to_all | solution.py:101
  62.2 5.0 %gather_fusion.2 = bf16[1000,200]{1,0:T(8,128)(2,1)} fusion(bf16[1024,200]{1,0:T(8,128)(2,1)S(1)} %collective-permute-done, s32[1024]{0:T(1024)S(1)} %pad_clamp_fusion.2), kind=kCustom, calls=%fused_computation.6 | custom fusion | bytes 804000 | tf_op jit(solution)/shard_map/while/body/eval_jaxpr/jit(_take)/gather | solution.py:41
  67.2 2.3 %all-to-all-done.1 = bf16[8,2,32,200]{3,2,1,0:T(8,128)(2,1)S(1)} async-done(((bf16[8,2,32,200]{3,2,1,0:T(8,128)(2,1)}), bf16[8,2,32,200]{3,2,1,0:T(8,128)(2,1)S(1)}, u32[]{:S(2)}, u32[]{:S(2)}) %all-to-all-start.1) | async-done | bytes 204832 | tf_op jit(solution)/shard_map/all_to_all | solution.py:101
  73.7 2.1 %scatter_custom_fusion.4 = bf16[512,200]{1,0:T(8,128)(2,1)} fusion(s32[256]{0:T(256)S(1)} %get-tuple-element.134, bf16[256,200]{1,0:T(8,128)(2,1)S(1)} %copy.35, bf16[]{:T(256)} %constant.105.clone.1), kind=kCustom, calls=%fused_computation.53 | custom fusion | bytes 204802 | tf_op jit(solution)/shard_map/scatter | solution.py:108
  75.9 3.7 %all-to-all-start.2 = ((bf16[8,2,32,200]{3,2,1,0:T(8,128)(2,1)}), bf16[8,2,32,200]{3,2,1,0:T(8,128)(2,1)S(1)}, u32[]{:S(2)}, u32[]{:S(2)}) async-start(bf16[8,2,32,200]{3,2,1,0:T(8,128)(2,1)} %bitcast.9), calls=%async_computation.2 | async-start | bytes 524288 | tf_op jit(solution)/shard_map/all_to_all | solution.py:111
  80.9 6.4 %scatter_custom_fusion.2 = f32[1024,200]{1,0:T(8,128)S(1)} fusion(s32[1000]{0:T(1024)S(1)} %bitcast.36, f32[1000,200]{1,0:T(8,128)} %fusion.33, f32[]{:T(128)} %constant.101.clone.1), kind=kCustom, calls=%fused_computation.32 | custom fusion | flops 200000 | bytes 819712 | tf_op jit(solution)/shard_map/while/body/eval_jaxpr/scatter-add | solution.py:50
  87.3 2.4 %scatter_fusion = f32[1024,200]{1,0:T(8,128)S(1)} fusion(f32[1024,200]{1,0:T(8,128)S(1)} %scatter_custom_fusion.2, s32[256]{0:T(256)S(1)} %compare_select_fusion.4, f32[256,200]{1,0:T(8,128)S(1)} %copy.33), kind=kCustom, calls=%fused_computation.10 | custom fusion | flops 51200 | bytes 615424 | tf_op jit(solution)/shard_map/scatter-add | solution.py:57
  90.9 2.0 %collective-permute-start.1 = (f32[1024,200]{0,1:T(8,128)}, f32[1024,200]{0,1:T(8,128)}, u32[]{:S(2)}, u32[]{:S(2)}) collective-permute-start(f32[1024,200]{0,1:T(8,128)} %copy.34), channel_id=1, source_target_pairs={{0,4},{4,8},{8,12},{12,16},{16,20},{20,24},{24,28},{28,0},{1,5},{5... | collective-permute-start | bytes 2457608 | tf_op jit(solution)/shard_map/ppermute | solution.py:18
  93.9 4.6 %all-to-all-start.3 = ((bf16[8,2,32,200]{3,2,1,0:T(8,128)(2,1)}), bf16[8,2,32,200]{3,2,1,0:T(8,128)(2,1)S(1)}, u32[]{:S(2)}, u32[]{:S(2)}) async-start(bf16[8,2,32,200]{3,2,1,0:T(8,128)(2,1)} %copy.37), calls=%async_computation.3 | async-start | bytes 524288 | tf_op jit(solution)/shard_map/all_to_all | solution.py:115
  99.5 15.7 %collective-permute-done.1 = f32[1024,200]{0,1:T(8,128)} collective-permute-done((f32[1024,200]{0,1:T(8,128)}, f32[1024,200]{0,1:T(8,128)}, u32[]{:S(2)}, u32[]{:S(2)}) %collective-permute-start.1) | collective-permute-done | bytes 819232 | tf_op jit(solution)/shard_map/ppermute | solution.py:18
  116.9 3.2 %scatter_custom_fusion.5 = f32[1024,200]{1,0:T(8,128)S(1)} fusion(f32[1024,200]{1,0:T(8,128)S(1)} %copy.38, s32[256]{0:T(256)S(1)} %compare_select_fusion.3, pred[256]{0:T(512)(128)(4,1)S(1)} %get-tuple-element.133, bf16[]{:T(256)} %constant.112.clone.1, bf16[512,200]{1,0:T(8,128)(2,1)S(1)} %bitcast.33, s32[1024]{0:T(1024)S(1)} %pad_clamp_fusion.3), kind=kCustom, calls=%fused_computation.39 | custom fusion | flops 153600 | bytes 1085954 | tf_op jit(solution)/shard_map/scatter-add | solution.py:121
  121.1 41.7 %all-reduce.3.cloned.1.call-done = (f32[1024,200]{1,0:T(8,128)}, f32[2,200,200]{2,1,0:T(8,128)}) async-done(((f32[1024,200]{1,0:T(8,128)}, f32[2,200,200]{2,1,0:T(8,128)}), (f32[1024,200]{1,0:T(8,128)}, f32[2,200,200]{2,1,0:T(8,128)})) %all-reduce.3.cloned.1.call-update) | async-done | bytes 1139216 | tf_op jit(solution)/shard_map/psum | solution.py:124
  (123 shorter events, 31.4 us)
Async XLA Ops:
  8.6 6.1 %copy-start.12 = (s32[256]{0:T(256)S(1)}, s32[256]{0:T(256)}, u32[]{:S(2)}) copy-start(s32[256]{0:T(256)} %param.18) | copy-start | bytes 3076
  8.7 52.2 %collective-permute-start = (bf16[1024,200]{1,0:T(8,128)(2,1)S(1)}, bf16[1024,200]{1,0:T(8,128)(2,1)S(1)}, u32[]{:S(2)}, u32[]{:S(2)}) collective-permute-start(bf16[1024,200]{1,0:T(8,128)(2,1)S(1)} %convert_element_type.48), channel_id=1, source_target_pairs={{0,28},{4,0},{8,4},{12,8},{16,12},{20,16},{24,20},{28,24},{1,29},{... | collective-permute-start | bytes 1228808 | tf_op jit(solution)/shard_map/ppermute | solution.py:18
  14.8 0.7 copy-start
  40.4 0.7 copy-start.10
  44.0 12.4 %copy-start.3 = (f32[2,200,200]{2,1,0:T(8,128)S(1)}, f32[2,200,200]{2,1,0:T(8,128)}, u32[]{:S(2)}) copy-start(f32[2,200,200]{2,1,0:T(8,128)} %param.16) | copy-start | bytes 960004
  44.0 12.4 %all-to-all-start = ((bf16[8,2,32,200]{3,2,1,0:T(8,128)(2,1)}), bf16[8,2,32,200]{3,2,1,0:T(8,128)(2,1)S(1)}, u32[]{:S(2)}, u32[]{:S(2)}) async-start(bf16[8,2,32,200]{3,2,1,0:T(8,128)(2,1)} %bitcast.3), calls=%async_computation | async-start | bytes 524288 | tf_op jit(solution)/shard_map/all_to_all | solution.py:97
  47.6 0.7 copy-start.9
  57.4 12.2 %all-to-all-start.1 = ((bf16[8,2,32,200]{3,2,1,0:T(8,128)(2,1)}), bf16[8,2,32,200]{3,2,1,0:T(8,128)(2,1)S(1)}, u32[]{:S(2)}, u32[]{:S(2)}) async-start(bf16[8,2,32,200]{3,2,1,0:T(8,128)(2,1)} %copy.29), calls=%async_computation.1 | async-start | bytes 524288 | tf_op jit(solution)/shard_map/all_to_all | solution.py:101
  70.8 1.0 copy-start.4
  72.3 0.8 copy-start.5
  73.6 5.9 %copy-start.6 = (bf16[256,1000]{0,1:T(8,128)(2,1)S(1)}, bf16[256,1000]{0,1:T(8,128)(2,1)}, u32[]{:S(2)}) copy-start(bf16[256,1000]{0,1:T(8,128)(2,1)} %copy-done.5) | copy-start | bytes 1536004
  75.9 17.0 %all-to-all-start.2 = ((bf16[8,2,32,200]{3,2,1,0:T(8,128)(2,1)}), bf16[8,2,32,200]{3,2,1,0:T(8,128)(2,1)S(1)}, u32[]{:S(2)}, u32[]{:S(2)}) async-start(bf16[8,2,32,200]{3,2,1,0:T(8,128)(2,1)} %bitcast.9), calls=%async_computation.2 | async-start | bytes 524288 | tf_op jit(solution)/shard_map/all_to_all | solution.py:111
  90.9 24.3 %collective-permute-start.1 = (f32[1024,200]{0,1:T(8,128)}, f32[1024,200]{0,1:T(8,128)}, u32[]{:S(2)}, u32[]{:S(2)}) collective-permute-start(f32[1024,200]{0,1:T(8,128)} %copy.34), channel_id=1, source_target_pairs={{0,4},{4,8},{8,12},{12,16},{16,20},{20,24},{24,28},{28,0},{1,5},{5... | collective-permute-start | bytes 2457608 | tf_op jit(solution)/shard_map/ppermute | solution.py:18
  93.9 23.0 %all-to-all-start.3 = ((bf16[8,2,32,200]{3,2,1,0:T(8,128)(2,1)}), bf16[8,2,32,200]{3,2,1,0:T(8,128)(2,1)S(1)}, u32[]{:S(2)}, u32[]{:S(2)}) async-start(bf16[8,2,32,200]{3,2,1,0:T(8,128)(2,1)} %copy.37), calls=%async_computation.3 | async-start | bytes 524288 | tf_op jit(solution)/shard_map/all_to_all | solution.py:115
  98.5 64.4 %all-reduce.3.cloned.1.call-start = ((), (), s32[]{:S(2)}) async-start(), calls=%async_computation.4 | async-start | bytes 2916352 | tf_op jit(solution)/shard_map/psum | solution.py:124
  120.1 1.0 copy-start.1
  162.8 2.1 %copy-start.2 = (f32[1024,200]{1,0:T(8,128)S(1)}, f32[1024,200]{1,0:T(8,128)}, u32[]{:S(2)}) copy-start(f32[1024,200]{1,0:T(8,128)} %get-tuple-element.125) | copy-start | bytes 2457604
  162.8 1.5 copy-start.11
  165.2 1.2 copy-start.7
  165.2 1.2 copy-start.8
Sparse Core Ops, SparseCore 0:
  121.3 41.5 all-reduce.2
where the time goes:
time: 175 us; the launch traced here: 174 us
  waiting for transfers between devices  68.1 us (39%)
  local copies, waits for them, and re-layouts  42.1 us (24%)
  starting transfers between devices  23.4 us (13%)
  other arithmetic  22.1 us (13%)
  between operations  14.4 us (8%)
  matrix products  3.77 us (2%)
    psum x1, waiting for transfers between devices, shards(): total_grad, total_operator = lax.psum((entity_grad, operator_grad), 'rep')  41.7 us
    gather x9, local copies, waits for them, and re-layouts, place_slots(): leading = jnp.searchsorted(ranked, ranked, side='left')  17.5 us
    ppermute x2, waiting for transfers between devices, passed_along(): lax.ppermute(array, axis, [(i, (i + by) % peers) for i in range(peers)])  15.7 us
    all_to_all x1, waiting for transfers between devices, shards(): lax.all_to_all(outgoing, 'ent', split_axis=0, concat_axis=0, tiled=True)  8.16 us
    ppermute x2, starting transfers between devices, passed_along(): lax.ppermute(array, axis, [(i, (i + by) % peers) for i in range(peers)])  8.04 us
    unnamed x28, local copies, waits for them, and re-layouts  7.28 us
    scatter-add x1, other arithmetic, span_step(): return (running.at[negative_block].add(row_update), query_part)  6.45 us
    gather x1, local copies, waits for them, and re-layouts, span_step(): negative_rows = jnp.take(table_rows, negative_block, axis=0)  4.98 us
  transfers between devices with their start and end apart: 7, of which 5 were waited for; matrix products, arithmetic and copies ran while one was open for 28% of the time, Pallas kernels for 0%

commit v1 on v0

--- a/solution.py
+++ b/solution.py
@@ -1,6 +1,10 @@
+import functools
+
 import jax
 import jax.numpy as jnp
 from jax import lax
+from jax.experimental import pallas as pl
+from jax.experimental.pallas import tpu as pltpu
 from jax.sharding import PartitionSpec as P
 
 SPAN = 256
@@ -72,7 +76,7 @@
     return (updated, fresh_moments)
 
 
-def shards(
+def exchanged_shards(
     entity_table,
     entity_state,
     operators,
@@ -127,6 +131,383 @@
     return (new_table, new_entity_state, new_operators, new_operator_state)
 
 
+bf16 = jnp.bfloat16
+f32 = jnp.float32
+CORES = 2
+LANES = 128
+RING = (0, 2, 4, 6, 7, 5, 3, 1)
+PLACE = tuple(RING.index(e) for e in range(8))
+SLOTS = 32
+QUARTER = 64
+VMEM = pltpu.VMEM
+SMEM = pltpu.SMEM
+NT = (((1,), (1,)), ((), ()))
+TN = (((0,), (0,)), ((), ()))
+
+
+def dot(a, b, dims=(((1,), (0,)), ((), ()))):
+    return lax.dot_general(a, b, dims, preferred_element_type=f32)
+
+
+def lanes_of(shape):
+    return lax.broadcasted_iota(jnp.int32, shape, 1)
+
+
+def rows_of(shape):
+    return lax.broadcasted_iota(jnp.int32, shape, 0)
+
+
+def one_hot(mask):
+    return jnp.where(mask, 1.0, 0.0).astype(bf16)
+
+
+def call(body, outs, name, flops, size, operands, scratch=(), grid=None, in_specs=None, out_specs=None):
+    spaces = [pl.BlockSpec(memory_space=SMEM)] + [pl.BlockSpec(memory_space=VMEM)] * (len(operands) - 1)
+    extra = {} if grid is None else {"grid": grid}
+    return pl.pallas_call(
+        body,
+        out_shape=outs,
+        in_specs=spaces if in_specs is None else in_specs,
+        out_specs=[pl.BlockSpec(memory_space=VMEM)] * len(outs) if out_specs is None else out_specs,
+        scratch_shapes=list(scratch),
+        name=name,
+        cost_estimate=pl.CostEstimate(flops=flops, bytes_accessed=size, transcendentals=0),
+        compiler_params=pltpu.CompilerParams(vmem_limit_bytes=44 * 2**20),
+        **extra,
+    )(*operands)
+
+
+def slot_kernel(count, scalars, own, near, far, across, table, slotted, turned, columns, rows, counts):
+    reps, _, edges = columns.shape[0], None, columns.shape[1]
+    buffers = (own, near, far, across)
+    places = slotted.shape[1]
+    me = scalars[1]
+    before = one_hot(rows_of((edges, edges)) > lanes_of((edges, edges)))
+    for m in range(reps):
+        block = lax.bitwise_xor(me, m)
+        ids = buffers[m][...]
+        relation = ids[2:3]
+        local = jnp.zeros_like(relation)
+        for r in range(count):
+            local = jnp.where(relation == r, scalars[11 + r], local)
+        stacked = jnp.concatenate([ids[0:2], local, ids[3:8]], axis=0).astype(f32)
+        standing = stacked.T
+        local_column = standing[:, 2:3].astype(jnp.int32)
+        named = lanes_of((edges, LANES)) == local_column
+        ahead = dot(before, one_hot(named))
+        slot = local_column.astype(f32) * SLOTS + jnp.sum(
+            jnp.where(named, ahead, 0.0), axis=1, keepdims=True
+        )
+        standing = jnp.where(lanes_of(standing.shape) == 2, slot, standing)
+        lying = standing.T
+        columns[block] = standing
+        rows[block] = lying
+        picked = one_hot(
+            lanes_of((edges, table.shape[0])) == standing[:, 0:1].astype(jnp.int32)
+        )
+        source_rows = dot(picked, table[...]).astype(bf16)
+        into = one_hot(rows_of((places * SLOTS, edges)) == lying[2:3].astype(jnp.int32))
+        slotted[block] = dot(into, source_rows).astype(bf16).reshape(places, SLOTS, -1)
+        tally = jnp.zeros((8, LANES), f32)
+        for k in range(3, 7):
+            drawn = ids[k : k + 1]
+            high = one_hot(rows_of((8, edges)) == lax.shift_right_arithmetic(drawn, 7))
+            low = one_hot(rows_of((LANES, edges)) == lax.bitwise_and(drawn, LANES - 1))
+            tally = tally + dot(high, low, NT)
+        counts[block] = jnp.concatenate([tally[k : k + 1] for k in range(8)], axis=1)
+    for m in range(places // 2):
+        pair = slotted[:, 2 * m : 2 * m + 2].reshape(reps * 2 * SLOTS, -1)
+        turned[m] = pair.astype(f32).T.astype(bf16)
+
+
+def score_kernel(
+    negative_count, scalars, o0, a1, a2, a3, a4, b4, b3, b2, b1, slotted, turned, columns, rows, counts,
+    mine, other, outgoing, transformed, weights, scaled, scaled_rest, query, table, moved,
+):
+    step = pl.program_id(0)
+    core, me = scalars[0], scalars[1]
+    reps = slotted.shape[0]
+    places = slotted.shape[1]
+    width = table.shape[1]
+    half = mine.shape[0]
+    edges = columns.shape[1]
+    entities = table.shape[0]
+
+    @pl.when(step == 0)
+    def _():
+        table[pl.ds(pl.multiple_of(core * half, half), half)] = mine[...]
+        table[pl.ds(pl.multiple_of((1 - core) * half, half), half)] = other[...]
+        for place, op in enumerate(operator_list(o0, a1, a2, a3, a4, b4, b3, b2, b1)):
+            given = slotted[:, place].reshape(reps * SLOTS, width)
+            moved[:, place] = dot(given, op()).astype(bf16).reshape(reps, SLOTS, width)
+
+    standing = columns[step].astype(jnp.int32)
+    out_of = one_hot(lanes_of((edges, places * SLOTS)) == standing[:, 2:3])
+    made = dot(out_of, moved[step].reshape(places * SLOTS, width))
+    made_half = made.astype(bf16)
+    scores = dot(made_half, table[...], NT)
+    aimed = lanes_of((edges, entities)) == standing[:, 1:2]
+    positive = jnp.sum(jnp.where(aimed, scores, 0.0), axis=1, keepdims=True)
+    positive_grad = -(0.5 * jnp.tanh(-0.5 * positive) + 0.5)
+    share = (0.5 * jnp.tanh(0.5 * scores) + 0.5) * (1.0 / negative_count)
+    weighted = (share.astype(bf16).astype(f32) * counts[step]).astype(bf16)
+    target_rows = dot(one_hot(aimed), table[...])
+    asked = (positive_grad * target_rows + dot(weighted, table[...])).astype(bf16)
+    push = positive_grad * made
+    push_half = push.astype(bf16)
+    transformed[0] = made_half
+    weights[0] = weighted
+    scaled[0] = push_half
+    scaled_rest[0] = (push - push_half.astype(f32)).astype(bf16)
+    query[0] = asked
+    chosen_lane = lanes_of((width, LANES)) % QUARTER
+    quarter = width // reps
+    chosen = one_hot(
+        (rows_of((width, LANES)) == chosen_lane + me * quarter) & (chosen_lane < quarter)
+    )
+    part = dot(asked, chosen).astype(bf16)
+    into = one_hot(
+        rows_of((places * SLOTS, edges)) == rows[step][2:3].astype(jnp.int32)
+    )
+    moved[step, :, :, 0:LANES] = dot(into, part).astype(bf16).reshape(places, SLOTS, LANES)
+
+    @pl.when(step == reps - 1)
+    def _():
+        size = reps * 2 * SLOTS
+        parity = lax.bitwise_and(lax.shift_right_logical(rows_of((size, LANES)), 5), 1)
+        side = lax.shift_right_logical(lanes_of((size, LANES)), 6)
+        for m in range(places // 2):
+            pair = moved[:, 2 * m : 2 * m + 2, :, 0:LANES].reshape(size, LANES)
+            kept = side == (lax.bitwise_xor(parity, core) if m == places // 4 else parity)
+            pair = jnp.where(kept, pair.astype(f32), 0.0).astype(bf16)
+            outgoing[scalars[3 + m]] = dot(turned[m], pair).astype(bf16)
+
+
+def operator_list(o0, a1, a2, a3, a4, b4, b3, b2, b1):
+    listed = [(o0, 0), (o0, 1)]
+    for ref in (a1, a2, a3):
+        listed += [(ref, 0), (ref, 1)]
+    listed += [(a4, 0), (b4, 0)]
+    for ref in (b3, b2, b1):
+        listed += [(ref, 0), (ref, 1)]
+    return [lambda ref=ref, i=i: ref[i] for ref, i in listed]
+
+
+def return_kernel(
+    scalars, o0, a1, a2, a3, a4, b4, b3, b2, b1, columns, rows, transformed, weights, scaled, scaled_rest,
+    query, target_half, source_total, held, total,
+):
+    step = pl.program_id(0)
+    core = scalars[0]
+    reps, places = pl.num_programs(0), held.shape[1]
+    width = query.shape[2]
+    edges = columns.shape[1]
+    entities = source_total.shape[0]
+    half = target_half.shape[0]
+    lying = rows[step].astype(jnp.int32)
+    standing = columns[step].astype(jnp.int32)
+    aimed = one_hot(lanes_of((edges, entities)) == standing[:, 1:2])
+    sides = jnp.concatenate([transformed[0], scaled[0], scaled_rest[0]], axis=0)
+    faces = jnp.concatenate([weights[0], aimed, aimed], axis=0)
+    grown = dot(sides, faces, TN)
+
+    @pl.when(step == 0)
+    def _():
+        total[...] = grown
+
+    @pl.when(step > 0)
+    def _():
+        total[...] += grown
+
+    into = one_hot(rows_of((places * SLOTS, edges)) == lying[2:3])
+    held[step] = dot(into, query[0]).astype(bf16).reshape(places, SLOTS, width)
+
+    @pl.when(step == held.shape[0] - 1)
+    def _():
+        whole = total[...].T
+        target_half[...] = jnp.where(core == 0, whole[:half], whole[half:]).astype(bf16)
+        for place, op in enumerate(operator_list(o0, a1, a2, a3, a4, b4, b3, b2, b1)):
+            given = held[:, place].reshape(-1, width)
+            held[:, place] = dot(given, op(), NT).astype(bf16).reshape(-1, SLOTS, width)
+        summed = jnp.zeros((entities, width), f32)
+        for b in range(held.shape[0]):
+            out_of = one_hot(
+                lanes_of((edges, places * SLOTS)) == columns[b][:, 2:3].astype(jnp.int32)
+            )
+            back = dot(out_of, held[b].reshape(places * SLOTS, width)).astype(bf16)
+            spread = one_hot(rows_of((entities, edges)) == rows[b][0:1].astype(jnp.int32))
+            summed = summed + dot(spread, back)
+        source_total[...] = summed
+
+
+def entity_kernel(scalars, source_total, mine, other, table, state, new_table, new_state, gradient):
+    core = scalars[0]
+    half = mine.shape[0]
+    width = table.shape[1]
+    for ref, side in ((mine, core), (other, 1 - core)):
+        at = pl.ds(pl.multiple_of(side * half, half), half)
+        gradient[at] = source_total[at] + ref[...].astype(f32)
+    old = state[...].T
+    fresh = []
+    for k in range(table.shape[0] // LANES):
+        at = slice(k * LANES, (k + 1) * LANES)
+        g = gradient[at]
+        moments = old[:, k : k + 1] + jnp.sum(g * g, axis=1, keepdims=True) * (1.0 / width)
+        fresh.append(moments)
+        new_table[at] = table[at] - g * (entity_rate / (jnp.sqrt(moments) + epsilon))
+    new_state[...] = jnp.concatenate(fresh, axis=1).T
+
+
+def operator_kernel(scalars, own, near, far, across, operators, state, new_operators, new_state):
+    me = scalars[1]
+    width = operators.shape[1]
+    quarter = width // 4
+    buffers = (own, near, far, across)
+    lane = rows_of((LANES, width))
+    inside = lane % QUARTER
+    for i in range(operators.shape[0]):
+        g = jnp.zeros((width, width), f32)
+        for m in range(4):
+            starting = lax.bitwise_xor(me, m) * quarter
+            put = one_hot(
+                (lane // QUARTER == i)
+                & (inside < quarter)
+                & (inside + starting == lanes_of((LANES, width)))
+            )
+            g = g + dot(buffers[m][...], put)
+        moments = state[i] + g * g
+        new_state[i] = moments
+        new_operators[i] = operators[i] - operator_rate * g / (jnp.sqrt(moments) + epsilon)
+
+
+def rep_swapped(array, by):
+    peers = lax.axis_size("rep")
+    return lax.ppermute(array, "rep", [(i, i ^ by) for i in range(peers)])
+
+
+def ring_step(array):
+    groups, reps = lax.axis_size("ent"), lax.axis_size("rep")
+    pairs = []
+    for e in range(groups):
+        for r in range(reps):
+            to = RING[(PLACE[e] + (1 if r % CORES == 0 else -1)) % groups]
+            pairs.append((e * reps + r, to * reps + r))
+    return lax.ppermute(array, ("ent", "rep"), pairs)
+
+
+def gathered_shards(
+    entity_table, entity_state, operators, operator_state, sources, destinations, relations, negatives
+):
+    groups, reps = lax.axis_size("ent"), lax.axis_size("rep")
+    entities, width = entity_table.shape
+    edges = sources.shape[0]
+    relation_count = groups * operators.shape[0]
+    half = entities // CORES
+    ent, rep = lax.axis_index("ent"), lax.axis_index("rep")
+    core = rep % CORES
+    sign = jnp.where(core == 0, -1, 1)
+    place = jnp.asarray(PLACE, jnp.int32)
+    here = place[ent]
+    owner_at = jnp.asarray(RING, jnp.int32)[(here + sign * jnp.arange(groups)) % groups]
+    offset_of = (sign * (jnp.repeat(place, operators.shape[0]) - here)) % groups
+    parity = jnp.arange(relation_count) % 2
+    local_of = 2 * offset_of + jnp.where(offset_of == groups // 2, parity ^ core, parity)
+    scalars = jnp.concatenate(
+        [jnp.stack([core, rep, sign]), owner_at, local_of]
+    ).astype(jnp.int32)
+
+    operators_half = operators.astype(bf16)
+    table_half = entity_table.astype(bf16)
+    ids = jnp.concatenate(
+        [
+            sources,
+            destinations,
+            relations[:, 0],
+            negatives[0],
+            jnp.full((5 * edges - negatives.shape[1],), -1, jnp.int32),
+        ]
+    ).reshape(8, edges)
+    others = [rep_swapped(ids, by) for by in (1, 2, 3)]
+    a1 = ring_step(operators_half)
+    own_half = lax.dynamic_slice_in_dim(table_half, core * half, half, 0)
+    mine = passed_along(own_half, "ent", -1)
+    b1 = rep_swapped(a1, 1)
+    a2 = ring_step(a1)
+    other = rep_swapped(mine, 1)
+    b2 = rep_swapped(a2, 1)
+    a3 = ring_step(a2)
+    b3 = rep_swapped(a3, 1)
+    a4 = ring_step(lax.dynamic_slice_in_dim(a3, core, 1, 0))
+    b4 = rep_swapped(a4, 1)
+    gathered = (operators_half, a1, a2, a3, a4, b4, b3, b2, b1)
+
+    places = relation_count
+    slot_out = [
+        jax.ShapeDtypeStruct((reps, places, SLOTS, width), bf16),
+        jax.ShapeDtypeStruct((places // 2, width, reps * 2 * SLOTS), bf16),
+        jax.ShapeDtypeStruct((reps, edges, 8), f32),
+        jax.ShapeDtypeStruct((reps, 8, edges), f32),
+        jax.ShapeDtypeStruct((reps, 1, entities), f32),
+    ]
+    slotted, turned, columns, rows, counts = call(
+        functools.partial(slot_kernel, relation_count), slot_out, "slots", 10**9, 10**7,
+        (scalars, ids, *others, table_half),
+    )
+    whole = pl.BlockSpec(memory_space=VMEM)
+    by_block = lambda a, b: pl.BlockSpec((1, a, b), lambda i: (i, 0, 0))
+    score_out = [
+        jax.ShapeDtypeStruct((groups, width, LANES), bf16),
+        jax.ShapeDtypeStruct((reps, edges, width), bf16),
+        jax.ShapeDtypeStruct((reps, edges, entities), bf16),
+        jax.ShapeDtypeStruct((reps, edges, width), bf16),
+        jax.ShapeDtypeStruct((reps, edges, width), bf16),
+        jax.ShapeDtypeStruct((reps, edges, width), bf16),
+    ]
+    operands = (scalars, *gathered, slotted, turned, columns, rows, counts, mine, other)
+    rowwise = by_block(edges, width)
+    outgoing, *kept = call(
+        functools.partial(score_kernel, negatives.shape[1]), score_out, "scores", 3 * 10**9, 2 * 10**7,
+        operands,
+        scratch=[VMEM((entities, width), bf16), VMEM((reps, places, SLOTS, width), bf16)],
+        grid=(reps,),
+        in_specs=[pl.BlockSpec(memory_space=SMEM)] + [whole] * (len(operands) - 1),
+        out_specs=[whole, rowwise, by_block(edges, entities), rowwise, rowwise, rowwise],
+    )
+    arrived = lax.all_to_all(outgoing, "ent", split_axis=0, concat_axis=0, tiled=True)
+    operands = (scalars, *gathered, columns, rows, *kept)
+    target_half, source_total = call(
+        return_kernel,
+        [jax.ShapeDtypeStruct((half, width), bf16), jax.ShapeDtypeStruct((entities, width), f32)],
+        "returns", 3 * 10**9, 2 * 10**7, operands,
+        scratch=[VMEM((reps, places, SLOTS, width), bf16), VMEM((width, entities), f32)],
+        grid=(reps,),
+        in_specs=[pl.BlockSpec(memory_space=SMEM)] + [whole] * (len(operands) - 6)
+        + [rowwise, by_block(edges, entities), rowwise, rowwise, rowwise],
+        out_specs=[whole, whole],
+    )
+    home_mine = passed_along(target_half, "ent", 1)
+    home_other = rep_swapped(home_mine, 1)
+    quarter = jnp.sum(arrived.astype(f32), axis=0).astype(bf16)
+    quarters = [rep_swapped(quarter, by) for by in (1, 2, 3)]
+    new_table, new_state = call(
+        entity_kernel,
+        [
+            jax.ShapeDtypeStruct((entities, width), f32),
+            jax.ShapeDtypeStruct((entities // LANES, LANES), f32),
+        ],
+        "entity_update", 10**7, 4 * 10**6,
+        (scalars, source_total, home_mine, home_other, entity_table, entity_state.reshape(-1, LANES)),
+        scratch=[VMEM((entities, width), f32)],
+    )
+    new_operators, new_operator_state = call(
+        operator_kernel,
+        [jax.ShapeDtypeStruct(operators.shape, f32)] * 2,
+        "operator_update", 10**7, 2 * 10**6,
+        (scalars, quarter, *quarters, operators, operator_state),
+    )
+    return (new_table, new_state.reshape(-1), new_operators, new_operator_state)
+
+
 def solution(mesh):
     placed = (
         P("ent", None),
@@ -138,8 +519,9 @@
         P(("ent", "rep"), None),
         P(("ent", "rep"), None),
     )
+    small = mesh.shape["ent"] == len(RING) and mesh.shape["rep"] == 2 * CORES
     return jax.shard_map(
-        shards,
+        gathered_shards if small else exchanged_shards,
         mesh=mesh,
         in_specs=placed,
         out_specs=(P("ent", None), P("ent"), P("ent", None, None), P("ent", None, None)),

time: 175 us -> 104 us (0.59)
  waiting for transfers between devices: 68.1 us -> 17.9 us
  Pallas kernels: 0 us -> 24.5 us
  other arithmetic: 22.1 us -> 3.69 us
  between operations: 14.4 us -> 0.97 us
  local copies, waits for them, and re-layouts: 42.1 us -> 30.9 us
  matrix products: 3.77 us -> 0 us
    psum x1 -> x0, waiting for transfers between devices: 41.7 us -> none  [shards(): total_grad, total_operator = lax.psum((entity_grad, operator_grad), 'rep')]
    gather x15 -> x1, local copies, waits for them, and re-layouts: 26.9 us -> 1.16 us  [gathered_shards(): jnp.asarray(RING, jnp.int32)[(here + sign * jnp.arange(groups)) % groups]]
    pallas_call x0 -> x5, Pallas kernels: none -> 24.5 us  [call(): pl.pallas_call(body, out_shape=outs, in_specs=spaces if in_specs is None...]
    unnamed x28 -> x86, local copies, waits for them, and re-layouts: 7.28 us -> 26.8 us
    ppermute x0 -> x16, starting transfers between devices: none -> 13.1 us  [the longest x4 8.04 us: ring_step(): return lax.ppermute(array, ('ent', 'rep'), pairs)]
    scatter-add x3 -> x0, other arithmetic: 12 us -> none  [the longest x1 6.45 us: span_step(): return (running.at[negative_block].add(row_update), query_part)]
    all_to_all x4 -> x1, waiting for transfers between devices: 10.7 us -> 0.01 us  [gathered_shards(): lax.all_to_all(outgoing, 'ent', split_axis=0, concat_axis=0, tiled=True)]
    all_to_all x4 -> x1, starting transfers between devices: 15.3 us -> 5.79 us  [gathered_shards(): lax.all_to_all(outgoing, 'ent', split_axis=0, concat_axis=0, tiled=True)]
  transfers between devices with their start and end apart: 7 -> 19, of which waited for: 5 -> 3; matrix products, arithmetic and copies ran while one was open for 28% -> 9% of each run, Pallas kernels for 0% -> 13%
where the time goes in v1:
time: 104 us; the launch traced here: 102 us
  local copies, waits for them, and re-layouts  30.9 us (30%)
  starting transfers between devices  24.5 us (24%)
  Pallas kernels  24.5 us (24%)
  waiting for transfers between devices  17.9 us (17%)
  other arithmetic  3.69 us (4%)
    unnamed x86, local copies, waits for them, and re-layouts  26.8 us
    pallas_call x5, Pallas kernels, call(): pl.pallas_call(body, out_shape=outs, in_specs=spaces if in_specs is None...  24.5 us
    ppermute x2, waiting for transfers between devices, passed_along(): lax.ppermute(array, axis, [(i, (i + by) % peers) for i in range(peers)])  9.15 us
    ppermute x4, waiting for transfers between devices, ring_step(): return lax.ppermute(array, ('ent', 'rep'), pairs)  8.75 us
    ppermute x4, starting transfers between devices, ring_step(): return lax.ppermute(array, ('ent', 'rep'), pairs)  8.04 us
    all_to_all x1, starting transfers between devices, gathered_shards(): lax.all_to_all(outgoing, 'ent', split_axis=0, concat_axis=0, tiled=True)  5.79 us
    ppermute x2, starting transfers between devices, passed_along(): lax.ppermute(array, axis, [(i, (i + by) % peers) for i in range(peers)])  5.52 us
    ppermute x12, starting transfers between devices, rep_swapped(): return lax.ppermute(array, 'rep', [(i, i ^ by) for i in range(peers)])  5.11 us
  transfers between devices with their start and end apart: 19, of which 3 were waited for; matrix products, arithmetic and copies ran while one was open for 9% of the time, Pallas kernels for 13%

profile of v1, /device:TPU:0, one launch (start us, length us, event | category | flops | bytes accessed | tf_op | source)
XLA Modules:
  0.0 102.5 jit_solution(3656850038977143424)
XLA Ops:
  1.7 3.1 %collective-permute-start = (bf16[2,200,200]{2,1,0:T(8,128)(2,1)S(1)}, bf16[2,200,200]{2,1,0:T(8,128)(2,1)S(1)}, u32[]{:S(2)}, u32[]{:S(2)}) collective-permute-start(bf16[2,200,200]{2,1,0:T(8,128)(2,1)S(1)} %convert_element_type.8.o0), channel_id=1, source_target_pairs={{0,8},{1,5},{2,10},{3,7},{4,0},{5,13},{6,2},{7,15},{8,16},{9,1},{1... | collective-permute-start | bytes 480008 | tf_op jit(solution)/shard_map/ppermute | solution.py:395
  7.4 1.5 %copy.17.table = f32[1024,200]{1,0:T(8,128)S(1)} copy(f32[1024,200]{0,1:T(8,128)} %param.10) | data formatting | bytes 1638400 | tf_op args[0]
  9.0 3.5 %collective-permute-start.11 = (bf16[512,200]{1,0:T(8,128)(2,1)S(1)}, bf16[512,200]{1,0:T(8,128)(2,1)S(1)}, u32[]{:S(2)}, u32[]{:S(2)}) collective-permute-start(bf16[512,200]{1,0:T(8,128)(2,1)S(1)} %constant_dynamic-slice_fusion), channel_id=1, source_target_pairs={{0,28},{4,0},{8,4},{12,8},{16,12},{20,16},{24,20},{28,24},{1,29},{... | collective-permute-start | bytes 614408 | tf_op jit(solution)/shard_map/ppermute | solution.py:22
  13.9 6.8 %collective-permute-done.1.a2 = bf16[2,200,200]{2,1,0:T(8,128)(2,1)S(1)} collective-permute-done((bf16[2,200,200]{2,1,0:T(8,128)(2,1)S(1)}, bf16[2,200,200]{2,1,0:T(8,128)(2,1)S(1)}, u32[]{:S(2)}, u32[]{:S(2)}) %collective-permute-start.1) | collective-permute-done | bytes 160032 | tf_op jit(solution)/shard_map/ppermute | solution.py:395
  20.7 2.5 %collective-permute-start.2 = (bf16[2,200,200]{2,1,0:T(8,128)(2,1)S(1)}, bf16[2,200,200]{2,1,0:T(8,128)(2,1)S(1)}, u32[]{:S(2)}, u32[]{:S(2)}) collective-permute-start(bf16[2,200,200]{2,1,0:T(8,128)(2,1)S(1)} %collective-permute-done.1.a2), channel_id=1, source_target_pairs={{0,8},{1,5},{2,10},{3,7},{4,0},{5,13},{6,2},{7,15},{8,16},{9,1},{1... | collective-permute-start | bytes 480008 | tf_op jit(solution)/shard_map/ppermute | solution.py:395
  24.5 1.9 %collective-permute-done.2.a3 = bf16[2,200,200]{2,1,0:T(8,128)(2,1)S(1)} collective-permute-done((bf16[2,200,200]{2,1,0:T(8,128)(2,1)S(1)}, bf16[2,200,200]{2,1,0:T(8,128)(2,1)S(1)}, u32[]{:S(2)}, u32[]{:S(2)}) %collective-permute-start.2) | collective-permute-done | bytes 160032 | tf_op jit(solution)/shard_map/ppermute | solution.py:395
  28.2 2.5 %collective-permute-start.3 = (bf16[1,200,200]{2,1,0:T(8,128)(2,1)}, bf16[1,200,200]{2,1,0:T(8,128)(2,1)}, u32[]{:S(2)}, u32[]{:S(2)}) collective-permute-start(bf16[1,200,200]{2,1,0:T(8,128)(2,1)} %constant_dynamic-slice_fusion.1), channel_id=1, source_target_pairs={{0,8},{1,5},{2,10},{3,7},{4,0},{5,13},{6,2},{7,15},{8,16},{9,1},{1... | collective-permute-start | bytes 240008 | tf_op jit(solution)/shard_map/ppermute | solution.py:395
  31.3 1.2 %gather_fusion = s32[8]{0:T(128)} fusion(s32[8]{0:T(128)S(1)} %copy-done.40, s32[1024]{0:T(1024)S(1)} %pad_clamp_fusion), kind=kCustom, calls=%fused_computation | custom fusion | bytes 96 | tf_op jit(solution)/shard_map/gather | solution.py:411
  35.2 4.2 %slots.1 = (bf16[4,16,32,200]{3,2,1,0:T(8,128)(2,1)S(1)}, bf16[8,200,256]{2,1,0:T(8,128)(2,1)S(1)}, f32[4,256,8]{2,1,0:T(8,128)S(1)}, f32[4,8,256]{2,1,0:T(8,128)S(1)}, f32[4,1,1024]{2,1,0:T(1,128)S(1)}) custom-call(s32[27]{0:T(128)S(1)} %concatenate.6.scalars, s32[8,256]{1,0:T(8,128)S(1)} %reshape.74.own, s32[8,256]{1,0:T(8,128)S(1)} %copy-done.25, ...), custom_call_target="tpu_custom_call" | custom-call | flops 1000000000 | bytes 10000000 | tf_op jit(solution)/shard_map/slots/pallas_call | solution.py:167
  39.5 8.6 %scores.1 = (bf16[8,200,128]{2,1,0:T(8,128)(2,1)}, bf16[4,256,200]{2,1,0:T(8,128)(2,1)S(1)}, bf16[4,256,1024]{2,1,0:T(8,128)(2,1)S(1)}, bf16[4,256,200]{2,1,0:T(...) custom-call(s32[27]{0:T(128)S(1)} %concatenate.6.scalars, ...), custom_call_target="tpu_custom_call" | custom-call | flops 3000000000 | bytes 20000000 | tf_op jit(solution)/shard_map/scores/pallas_call | solution.py:167
  48.1 1.3 %copy-done.26 = bf16[4,256,1024]{2,1,0:T(8,128)(2,1)} copy-done((bf16[4,256,1024]{2,1,0:T(8,128)(2,1)}, bf16[4,256,1024]{2,1,0:T(8,128)(2,1)S(1)}, u32[]{:S(2)}) %copy-start.26) | copy-done | bytes 2097176
  51.9 5.8 %all-to-all-start = ((bf16[8,200,128]{2,1,0:T(8,128)(2,1)}), bf16[8,200,128]{2,1,0:T(8,128)(2,1)S(1)}, u32[]{:S(2)}, u32[]{:S(2)}) async-start(bf16[8,200,128]{2,1,0:T(8,128)(2,1)} %get-tuple-element.35), calls=%async_computation | async-start | bytes 819200 | tf_op jit(solution)/shard_map/all_to_all | solution.py:476
  63.2 1.6 %copy-done.27 = bf16[4,256,1024]{2,1,0:T(8,128)(2,1)S(1)} copy-done((bf16[4,256,1024]{2,1,0:T(8,128)(2,1)S(1)}, bf16[4,256,1024]{2,1,0:T(8,128)(2,1)}, u32[]{:S(2)}) %copy-start.27) | copy-done | bytes 2097176
  64.8 1.0 %copy-done.29 = f32[4,256,8]{2,1,0:T(8,128)S(1)} copy-done((f32[4,256,8]{2,1,0:T(8,128)S(1)}, f32[4,256,8]{2,1,0:T(8,128)}, u32[]{:S(2)}) %copy-start.29) | copy-done | bytes 32792
  65.8 1.0 %copy-done.31 = bf16[4,256,200]{2,1,0:T(8,128)(2,1)S(1)} copy-done((bf16[4,256,200]{2,1,0:T(8,128)(2,1)S(1)}, bf16[4,256,200]{2,1,0:T(8,128)(2,1)}, u32[]{:S(2)}) %copy-start.31) | copy-done | bytes 409624
  66.9 1.0 %copy-done.33 = bf16[4,256,200]{2,1,0:T(8,128)(2,1)S(1)} copy-done((bf16[4,256,200]{2,1,0:T(8,128)(2,1)S(1)}, bf16[4,256,200]{2,1,0:T(8,128)(2,1)}, u32[]{:S(2)}) %copy-start.33) | copy-done | bytes 409624
  69.0 1.0 %copy-done.37 = bf16[4,256,200]{2,1,0:T(8,128)(2,1)S(1)} copy-done((bf16[4,256,200]{2,1,0:T(8,128)(2,1)S(1)}, bf16[4,256,200]{2,1,0:T(8,128)(2,1)}, u32[]{:S(2)}) %copy-start.37) | copy-done | bytes 409624
  70.8 7.0 %returns.1 = (bf16[512,200]{1,0:T(8,128)(2,1)S(1)}, f32[1024,200]{1,0:T(8,128)S(1)}) custom-call(s32[27]{0:T(128)S(1)} %concatenate.6.scalars, bf16[2,200,200]{2,1,0:T(8,128)(2,1)S(1)} %convert_element_type.8.o0, bf16[2,200,200]{2,1,0:T(8,128)(2,1)S(1)} %copy-done.11, bf16[2,200,200]{2,1,0:T(8,128)(2,1)S(1)} %copy-done.13, ...), custom_call_target="tpu_custom_call" | custom-call | flops 3000000000 | bytes 20000000 | tf_op jit(solution)/shard_map/returns/pallas_call | solution.py:167
  77.8 2.1 %collective-permute-start.13 = (bf16[512,200]{1,0:T(8,128)(2,1)S(1)}, bf16[512,200]{1,0:T(8,128)(2,1)S(1)}, u32[]{:S(2)}, u32[]{:S(2)}) collective-permute-start(bf16[512,200]{1,0:T(8,128)(2,1)S(1)} %get-tuple-element.32), channel_id=1, source_target_pairs={{0,4},{4,8},{8,12},{12,16},{16,20},{20,24},{24,28},{28,0},{1,5},{5... | collective-permute-start | bytes 614408 | tf_op jit(solution)/shard_map/ppermute | solution.py:22
  79.9 9.1 %collective-permute-done.13.mine = bf16[512,200]{1,0:T(8,128)(2,1)S(1)} collective-permute-done((bf16[512,200]{1,0:T(8,128)(2,1)S(1)}, bf16[512,200]{1,0:T(8,128)(2,1)S(1)}, u32[]{:S(2)}, u32[]{:S(2)}) %collective-permute-start.13) | collective-permute-done | bytes 204832 | tf_op jit(solution)/shard_map/ppermute | solution.py:22
  89.7 1.4 %collective-permute-start.17 = (bf16[200,128]{1,0:T(8,128)(2,1)}, bf16[200,128]{1,0:T(8,128)(2,1)}, u32[]{:S(2)}, u32[]{:S(2)}) collective-permute-start(bf16[200,128]{1,0:T(8,128)(2,1)} %reduce_sum.12.own), channel_id=1, source_target_pairs={{0,3},{1,2},{2,1},{3,0},{4,7},{5,6},{6,5},{7,4},{8,11},{9,10},{10,... | collective-permute-start | bytes 153608 | tf_op jit(solution)/shard_map/ppermute | solution.py:385
  95.8 2.4 %entity_update.1 = (f32[1024,200]{1,0:T(8,128)S(1)}, f32[8,128]{1,0:T(8,128)}) custom-call(s32[27]{0:T(128)S(1)} %copy-done.7, f32[1024,200]{1,0:T(8,128)S(1)} %get-tuple-element.31.source_total, bf16[512,200]{1,0:T(8,128)(2,1)S(1)} %copy-done.3, bf16[512,200]{1,0:T(8,128)(2,1)S(1)} %copy-done.5, f32[1024,200]{1,0:T(8,128)S(1)} %copy.17.table, ...), custom_call_target="tpu_custom_call" | custom-call | flops 10000000 | bytes 4000000 | tf_op jit(solution)/shard_map/entity_update/pallas_call | solution.py:167
  98.3 1.2 %copy.19 = f32[1024,200]{0,1:T(8,128)} copy(f32[1024,200]{1,0:T(8,128)S(1)} %get-tuple-element.42) | data formatting | bytes 1638400
  100.2 2.3 %operator_update.1 = (f32[2,200,200]{2,1,0:T(8,128)}, f32[2,200,200]{2,1,0:T(8,128)}) custom-call(s32[27]{0:T(128)S(1)} %copy-done.8, bf16[200,128]{1,0:T(8,128)(2,1)} %reduce_sum.12.own, bf16[200,128]{1,0:T(8,128)(2,1)} %collective-permute-done.15.near, bf16[200,128]{1,0:T(8,128)(2,1)} %collective-permute-done.16.far, ...), custom_call_target="tpu_custom_call" | custom-call | flops 10000000 | bytes 2000000 | tf_op jit(solution)/shard_map/operator_update/pallas_call | solution.py:167
  (122 shorter events, 27.5 us)
Async XLA Ops:
  1.7 10.8 %copy-start.41 = (s32[8]{0:T(128)S(1)}, s32[8]{0:T(128)}, u32[]{:S(2)}) copy-start(s32[8]{0:T(128)} %constant.71.clone) | copy-start | bytes 100
  1.7 11.4 %collective-permute-start = (bf16[2,200,200]{2,1,0:T(8,128)(2,1)S(1)}, bf16[2,200,200]{2,1,0:T(8,128)(2,1)S(1)}, u32[]{:S(2)}, u32[]{:S(2)}) collective-permute-start(bf16[2,200,200]{2,1,0:T(8,128)(2,1)S(1)} %convert_element_type.8.o0), channel_id=1, source_target_pairs={{0,8},{1,5},{2,10},{3,7},{4,0},{5,13},{6,2},{7,15},{8,16},{9,1},{1... | collective-permute-start | bytes 480008 | tf_op jit(solution)/shard_map/ppermute | solution.py:395
  5.6 21.5 %collective-permute-start.10 = (s32[8,256]{1,0:T(8,128)S(1)}, s32[8,256]{1,0:T(8,128)S(1)}, u32[]{:S(2)}, u32[]{:S(2)}) collective-permute-start(s32[8,256]{1,0:T(8,128)S(1)} %reshape.74.own), channel_id=1, source_target_pairs={{0,3},{1,2},{2,1},{3,0},{4,7},{5,6},{6,5},{7,4},{8,11},{9,10},{10,... | collective-permute-start | bytes 24584 | tf_op jit(solution)/shard_map/ppermute | solution.py:385
  6.2 21.5 %collective-permute-start.9 = (s32[8,256]{1,0:T(8,128)S(1)}, s32[8,256]{1,0:T(8,128)S(1)}, u32[]{:S(2)}, u32[]{:S(2)}) collective-permute-start(s32[8,256]{1,0:T(8,128)S(1)} %reshape.74.own), channel_id=1, source_target_pairs={{0,2},{1,3},{2,0},{3,1},{4,6},{5,7},{6,4},{7,5},{8,10},{9,11},{10,... | collective-permute-start | bytes 24584 | tf_op jit(solution)/shard_map/ppermute | solution.py:385
  7.2 23.5 %collective-permute-start.8 = (s32[8,256]{1,0:T(8,128)S(1)}, s32[8,256]{1,0:T(8,128)S(1)}, u32[]{:S(2)}, u32[]{:S(2)}) collective-permute-start(s32[8,256]{1,0:T(8,128)S(1)} %reshape.74.own), channel_id=1, source_target_pairs={{0,1},{1,0},{2,3},{3,2},{4,5},{5,4},{6,7},{7,6},{8,9},{9,8},{10,11... | collective-permute-start | bytes 24584 | tf_op jit(solution)/shard_map/ppermute | solution.py:385
  7.4 23.9 %copy-start.40 = (s32[8]{0:T(128)S(1)}, s32[8]{0:T(128)}, u32[]{:S(2)}) copy-start(s32[8]{0:T(128)} %constant.72.clone) | copy-start | bytes 100
  9.0 15.4 %collective-permute-start.11 = (bf16[512,200]{1,0:T(8,128)(2,1)S(1)}, bf16[512,200]{1,0:T(8,128)(2,1)S(1)}, u32[]{:S(2)}, u32[]{:S(2)}) collective-permute-start(bf16[512,200]{1,0:T(8,128)(2,1)S(1)} %constant_dynamic-slice_fusion), channel_id=1, source_target_pairs={{0,28},{4,0},{8,4},{12,8},{16,12},{20,16},{24,20},{28,24},{1,29},{... | collective-permute-start | bytes 614408 | tf_op jit(solution)/shard_map/ppermute | solution.py:22
  13.1 26.4 %copy-start.10 = (bf16[2,200,200]{2,1,0:T(8,128)(2,1)}, bf16[2,200,200]{2,1,0:T(8,128)(2,1)S(1)}, u32[]{:S(2)}) copy-start(bf16[2,200,200]{2,1,0:T(8,128)(2,1)S(1)} %collective-permute-done.a1) | copy-start | bytes 480004
  13.1 7.6 %collective-permute-start.1 = (bf16[2,200,200]{2,1,0:T(8,128)(2,1)S(1)}, bf16[2,200,200]{2,1,0:T(8,128)(2,1)S(1)}, u32[]{:S(2)}, u32[]{:S(2)}) collective-permute-start(bf16[2,200,200]{2,1,0:T(8,128)(2,1)S(1)} %collective-permute-done.a1), channel_id=1, source_target_pairs={{0,8},{1,5},{2,10},{3,7},{4,0},{5,13},{6,2},{7,15},{8,16},{9,1},{1... | collective-permute-start | bytes 480008 | tf_op jit(solution)/shard_map/ppermute | solution.py:395
  20.7 18.8 %copy-start.12 = (bf16[2,200,200]{2,1,0:T(8,128)(2,1)}, bf16[2,200,200]{2,1,0:T(8,128)(2,1)S(1)}, u32[]{:S(2)}) copy-start(bf16[2,200,200]{2,1,0:T(8,128)(2,1)S(1)} %collective-permute-done.1.a2) | copy-start | bytes 480004
  20.7 5.8 %collective-permute-start.2 = (bf16[2,200,200]{2,1,0:T(8,128)(2,1)S(1)}, bf16[2,200,200]{2,1,0:T(8,128)(2,1)S(1)}, u32[]{:S(2)}, u32[]{:S(2)}) collective-permute-start(bf16[2,200,200]{2,1,0:T(8,128)(2,1)S(1)} %collective-permute-done.1.a2), channel_id=1, source_target_pairs={{0,8},{1,5},{2,10},{3,7},{4,0},{5,13},{6,2},{7,15},{8,16},{9,1},{1... | collective-permute-start | bytes 480008 | tf_op jit(solution)/shard_map/ppermute | solution.py:395
  24.4 15.0 %collective-permute-start.7 = (bf16[2,200,200]{2,1,0:T(8,128)(2,1)S(1)}, bf16[2,200,200]{2,1,0:T(8,128)(2,1)S(1)}, u32[]{:S(2)}, u32[]{:S(2)}) collective-permute-start(bf16[2,200,200]{2,1,0:T(8,128)(2,1)S(1)} %collective-permute-done.a1), channel_id=1, source_target_pairs={{0,1},{1,0},{2,3},{3,2},{4,5},{5,4},{6,7},{7,6},{8,9},{9,8},{10,11... | collective-permute-start | bytes 480008 | tf_op jit(solution)/shard_map/ppermute | solution.py:385
  26.5 13.0 %collective-permute-start.12 = (bf16[512,200]{1,0:T(8,128)(2,1)S(1)}, bf16[512,200]{1,0:T(8,128)(2,1)S(1)}, u32[]{:S(2)}, u32[]{:S(2)}) collective-permute-start(bf16[512,200]{1,0:T(8,128)(2,1)S(1)} %collective-permute-done.11.mine), channel_id=1, source_target_pairs={{0,1},{1,0},{2,3},{3,2},{4,5},{5,4},{6,7},{7,6},{8,9},{9,8},{10,11... | collective-permute-start | bytes 614408 | tf_op jit(solution)/shard_map/ppermute | solution.py:385
  27.1 12.3 %collective-permute-start.6 = (bf16[2,200,200]{2,1,0:T(8,128)(2,1)S(1)}, bf16[2,200,200]{2,1,0:T(8,128)(2,1)S(1)}, u32[]{:S(2)}, u32[]{:S(2)}) collective-permute-start(bf16[2,200,200]{2,1,0:T(8,128)(2,1)S(1)} %collective-permute-done.1.a2), channel_id=1, source_target_pairs={{0,1},{1,0},{2,3},{3,2},{4,5},{5,4},{6,7},{7,6},{8,9},{9,8},{10,11... | collective-permute-start | bytes 480008 | tf_op jit(solution)/shard_map/ppermute | solution.py:385
  28.2 5.0 %collective-permute-start.3 = (bf16[1,200,200]{2,1,0:T(8,128)(2,1)}, bf16[1,200,200]{2,1,0:T(8,128)(2,1)}, u32[]{:S(2)}, u32[]{:S(2)}) collective-permute-start(bf16[1,200,200]{2,1,0:T(8,128)(2,1)} %constant_dynamic-slice_fusion.1), channel_id=1, source_target_pairs={{0,8},{1,5},{2,10},{3,7},{4,0},{5,13},{6,2},{7,15},{8,16},{9,1},{1... | collective-permute-start | bytes 240008 | tf_op jit(solution)/shard_map/ppermute | solution.py:395
  31.3 8.2 %collective-permute-start.5 = (bf16[2,200,200]{2,1,0:T(8,128)(2,1)S(1)}, bf16[2,200,200]{2,1,0:T(8,128)(2,1)S(1)}, u32[]{:S(2)}, u32[]{:S(2)}) collective-permute-start(bf16[2,200,200]{2,1,0:T(8,128)(2,1)S(1)} %collective-permute-done.2.a3), channel_id=1, source_target_pairs={{0,1},{1,0},{2,3},{3,2},{4,5},{5,4},{6,7},{7,6},{8,9},{9,8},{10,11... | collective-permute-start | bytes 480008 | tf_op jit(solution)/shard_map/ppermute | solution.py:385
  33.2 24.4 %copy-start.6 = (s32[27]{0:T(128)}, s32[27]{0:T(128)S(1)}, u32[]{:S(2)}) copy-start(s32[27]{0:T(128)S(1)} %concatenate.6.scalars) | copy-start | bytes 328
  33.3 6.2 %collective-permute-start.4 = (bf16[1,200,200]{2,1,0:T(8,128)(2,1)}, bf16[1,200,200]{2,1,0:T(8,128)(2,1)S(1)}, u32[]{:S(2)}, u32[]{:S(2)}) collective-permute-start(bf16[1,200,200]{2,1,0:T(8,128)(2,1)} %collective-permute-done.3.a4), channel_id=1, source_target_pairs={{0,1},{1,0},{2,3},{3,2},{4,5},{5,4},{6,7},{7,6},{8,9},{9,8},{10,11... | collective-permute-start | bytes 240008 | tf_op jit(solution)/shard_map/ppermute | solution.py:385
  51.9 37.2 %all-to-all-start = ((bf16[8,200,128]{2,1,0:T(8,128)(2,1)}), bf16[8,200,128]{2,1,0:T(8,128)(2,1)S(1)}, u32[]{:S(2)}, u32[]{:S(2)}) async-start(bf16[8,200,128]{2,1,0:T(8,128)(2,1)} %get-tuple-element.35), calls=%async_computation | async-start | bytes 819200 | tf_op jit(solution)/shard_map/all_to_all | solution.py:476
  77.8 11.2 %collective-permute-start.13 = (bf16[512,200]{1,0:T(8,128)(2,1)S(1)}, bf16[512,200]{1,0:T(8,128)(2,1)S(1)}, u32[]{:S(2)}, u32[]{:S(2)}) collective-permute-start(bf16[512,200]{1,0:T(8,128)(2,1)S(1)} %get-tuple-element.32), channel_id=1, source_target_pairs={{0,4},{4,8},{8,12},{12,16},{16,20},{20,24},{24,28},{28,0},{1,5},{5... | collective-permute-start | bytes 614408 | tf_op jit(solution)/shard_map/ppermute | solution.py:22
  89.0 2.8 %collective-permute-start.14 = (bf16[512,200]{1,0:T(8,128)(2,1)S(1)}, bf16[512,200]{1,0:T(8,128)(2,1)S(1)}, u32[]{:S(2)}, u32[]{:S(2)}) collective-permute-start(bf16[512,200]{1,0:T(8,128)(2,1)S(1)} %collective-permute-done.13.mine), channel_id=1, source_target_pairs={{0,1},{1,0},{2,3},{3,2},{4,5},{5,4},{6,7},{7,6},{8,9},{9,8},{10,11... | collective-permute-start | bytes 614408 | tf_op jit(solution)/shard_map/ppermute | solution.py:385
  89.7 9.8 %collective-permute-start.17 = (bf16[200,128]{1,0:T(8,128)(2,1)}, bf16[200,128]{1,0:T(8,128)(2,1)}, u32[]{:S(2)}, u32[]{:S(2)}) collective-permute-start(bf16[200,128]{1,0:T(8,128)(2,1)} %reduce_sum.12.own), channel_id=1, source_target_pairs={{0,3},{1,2},{2,1},{3,0},{4,7},{5,6},{6,5},{7,4},{8,11},{9,10},{10,... | collective-permute-start | bytes 153608 | tf_op jit(solution)/shard_map/ppermute | solution.py:385
  91.1 8.4 %collective-permute-start.16 = (bf16[200,128]{1,0:T(8,128)(2,1)}, bf16[200,128]{1,0:T(8,128)(2,1)}, u32[]{:S(2)}, u32[]{:S(2)}) collective-permute-start(bf16[200,128]{1,0:T(8,128)(2,1)} %reduce_sum.12.own), channel_id=1, source_target_pairs={{0,2},{1,3},{2,0},{3,1},{4,6},{5,7},{6,4},{7,5},{8,10},{9,11},{10,... | collective-permute-start | bytes 153608 | tf_op jit(solution)/shard_map/ppermute | solution.py:385
  91.9 7.6 %collective-permute-start.15 = (bf16[200,128]{1,0:T(8,128)(2,1)}, bf16[200,128]{1,0:T(8,128)(2,1)}, u32[]{:S(2)}, u32[]{:S(2)}) collective-permute-start(bf16[200,128]{1,0:T(8,128)(2,1)} %reduce_sum.12.own), channel_id=1, source_target_pairs={{0,1},{1,0},{2,3},{3,2},{4,5},{5,4},{6,7},{7,6},{8,9},{9,8},{10,11... | collective-permute-start | bytes 153608 | tf_op jit(solution)/shard_map/ppermute | solution.py:385
  (37 other events, 90.3 us)

commit v2 on v0

--- a/solution.py
+++ b/solution.py
@@ -1,6 +1,10 @@
+import functools
+
 import jax
 import jax.numpy as jnp
 from jax import lax
+from jax.experimental import pallas as pl
+from jax.experimental.pallas import tpu as pltpu
 from jax.sharding import PartitionSpec as P
 
 SPAN = 256
@@ -72,7 +76,7 @@
     return (updated, fresh_moments)
 
 
-def shards(
+def exchanged_shards(
     entity_table,
     entity_state,
     operators,
@@ -127,6 +131,355 @@
     return (new_table, new_entity_state, new_operators, new_operator_state)
 
 
+bf16 = jnp.bfloat16
+f32 = jnp.float32
+CORES = 2
+LANES = 128
+RING = (0, 2, 4, 6, 7, 5, 3, 1)
+PLACE = tuple(RING.index(e) for e in range(8))
+SLOTS = 32
+QUARTER = 64
+VMEM = pltpu.VMEM
+NT = (((1,), (1,)), ((), ()))
+TN = (((0,), (0,)), ((), ()))
+
+
+def dot(a, b, dims=(((1,), (0,)), ((), ()))):
+    return lax.dot_general(a, b, dims, preferred_element_type=f32)
+
+
+def lanes_of(shape):
+    return lax.broadcasted_iota(jnp.int32, shape, 1)
+
+
+def rows_of(shape):
+    return lax.broadcasted_iota(jnp.int32, shape, 0)
+
+
+def one_hot(mask):
+    return jnp.where(mask, 1.0, 0.0).astype(bf16)
+
+
+def call(body, outs, name, flops, size, operands, limit=16, scratch=()):
+    whole = pl.BlockSpec(memory_space=VMEM)
+    return pl.pallas_call(
+        body,
+        out_shape=outs,
+        in_specs=[whole] * len(operands),
+        out_specs=[whole] * len(outs),
+        scratch_shapes=list(scratch),
+        name=name,
+        cost_estimate=pl.CostEstimate(flops=flops, bytes_accessed=size, transcendentals=0),
+        compiler_params=pltpu.CompilerParams(vmem_limit_bytes=limit * 2**20),
+    )(*operands)
+
+
+def chosen_from(listed, at):
+    found = jnp.zeros_like(at)
+    for i, value in enumerate(listed):
+        found = jnp.where(at == i, value, found)
+    return found
+
+
+def position():
+    rep = lax.axis_index("rep")
+    core = lax.rem(rep, CORES)
+    return core, rep, chosen_from(PLACE, lax.axis_index("ent")), 2 * core - 1
+
+
+def slot_kernel(own, near, far, across, table, slotted, turned, rows, counts):
+    reps, _, edges = rows.shape
+    buffers = (own, near, far, across)
+    places = slotted.shape[1]
+    core, me, here, sign = position()
+    ring = len(RING)
+    before = one_hot(rows_of((edges, edges)) > lanes_of((edges, edges)))
+    for m in range(reps):
+        block = lax.bitwise_xor(me, m)
+        ids = buffers[m][...]
+        relation = ids[2:3]
+        offset = lax.bitwise_and(
+            sign * (chosen_from(PLACE, lax.shift_right_logical(relation, 1)) - here), ring - 1
+        )
+        parity = lax.bitwise_and(relation, 1)
+        local = 2 * offset + jnp.where(
+            offset == ring // 2, lax.bitwise_xor(parity, core), parity
+        )
+        stacked = jnp.concatenate([ids[0:2], local, ids[3:8]], axis=0).astype(f32)
+        standing = stacked.T
+        local_column = standing[:, 2:3].astype(jnp.int32)
+        named = lanes_of((edges, LANES)) == local_column
+        ahead = dot(before, one_hot(named))
+        slot = local_column.astype(f32) * SLOTS + jnp.sum(
+            jnp.where(named, ahead, 0.0), axis=1, keepdims=True
+        )
+        standing = jnp.where(lanes_of(standing.shape) == 2, slot, standing)
+        lying = standing.T
+        rows[block] = lying
+        picked = one_hot(
+            lanes_of((edges, table.shape[1])) == standing[:, 0:1].astype(jnp.int32)
+        )
+        source_rows = dot(picked, table[...], NT).astype(bf16)
+        into = one_hot(rows_of((places * SLOTS, edges)) == lying[2:3].astype(jnp.int32))
+        slotted[block] = dot(into, source_rows).astype(bf16).reshape(places, SLOTS, -1)
+        tally = jnp.zeros((8, LANES), f32)
+        for k in range(3, 7):
+            drawn = ids[k : k + 1]
+            high = one_hot(rows_of((8, edges)) == lax.shift_right_arithmetic(drawn, 7))
+            low = one_hot(rows_of((LANES, edges)) == lax.bitwise_and(drawn, LANES - 1))
+            tally = tally + dot(high, low, NT)
+        counts[block] = jnp.concatenate([tally[k : k + 1] for k in range(8)], axis=1)
+    for m in range(places // 2):
+        pair = slotted[:, 2 * m : 2 * m + 2].reshape(reps * 2 * SLOTS, -1)
+        turned[m] = pair.astype(f32).T.astype(bf16)
+
+
+def score_kernel(
+    negative_count, o0, a1, a2, a3, a4, b4, b3, b2, b1, slotted, turned, rows, counts, mine, other,
+    s0, s1, s2, s3, s4, s5, s6, s7, weights, sides, query, table, moved,
+):
+    core, me, *_ = position()
+    reps, places = slotted.shape[:2]
+    width, entities = table.shape
+    half = mine.shape[1]
+    edges = rows.shape[2]
+    table[:, pl.ds(pl.multiple_of(core * half, half), half)] = mine[...]
+    table[:, pl.ds(pl.multiple_of((1 - core) * half, half), half)] = other[...]
+    for place, op in enumerate(operator_list(o0, a1, a2, a3, a4, b4, b3, b2, b1)):
+        given = slotted[:, place].reshape(reps * SLOTS, width)
+        moved[:, place] = dot(given, op()).astype(bf16).reshape(reps, SLOTS, width)
+    chosen_lane = lanes_of((width, LANES)) % QUARTER
+    quarter = width // reps
+    chosen = one_hot(
+        (rows_of((width, LANES)) == chosen_lane + me * quarter) & (chosen_lane < quarter)
+    )
+    for b in range(reps):
+        lying = rows[b]
+        standing = lying.T.astype(jnp.int32)
+        out_of = one_hot(lanes_of((edges, places * SLOTS)) == standing[:, 2:3])
+        made = dot(out_of, moved[b].reshape(places * SLOTS, width))
+        made_half = made.astype(bf16)
+        scores = dot(made_half, table[...])
+        aimed = lanes_of((edges, entities)) == standing[:, 1:2]
+        positive = jnp.sum(jnp.where(aimed, scores, 0.0), axis=1, keepdims=True)
+        positive_grad = -(0.5 * jnp.tanh(-0.5 * positive) + 0.5)
+        share = (0.5 * jnp.tanh(0.5 * scores) + 0.5) * (1.0 / negative_count)
+        weighted = (share.astype(bf16).astype(f32) * counts[b]).astype(bf16)
+        target_rows = dot(one_hot(aimed), table[...], NT)
+        asked = (positive_grad * target_rows + dot(weighted, table[...], NT)).astype(bf16)
+        push = positive_grad * made
+        push_half = push.astype(bf16)
+        weights[b] = weighted
+        sides[b, :edges] = made_half
+        sides[b, edges : 2 * edges] = push_half
+        sides[b, 2 * edges :] = (push - push_half.astype(f32)).astype(bf16)
+        query[b] = asked
+        part = dot(asked, chosen).astype(bf16)
+        into = one_hot(rows_of((places * SLOTS, edges)) == lying[2:3].astype(jnp.int32))
+        moved[b, :, :, 0:LANES] = dot(into, part).astype(bf16).reshape(places, SLOTS, LANES)
+    size = reps * 2 * SLOTS
+    parity = lax.bitwise_and(lax.shift_right_logical(rows_of((size, LANES)), 5), 1)
+    side = lax.shift_right_logical(lanes_of((size, LANES)), 6)
+    for m, outgoing in enumerate((s0, s1, s2, s3, s4, s5, s6, s7)):
+        pair = moved[:, 2 * m : 2 * m + 2, :, 0:LANES].reshape(size, LANES)
+        kept = side == (lax.bitwise_xor(parity, core) if m == places // 4 else parity)
+        pair = jnp.where(kept, pair.astype(f32), 0.0).astype(bf16)
+        outgoing[...] = dot(turned[m], pair).astype(bf16)
+
+
+def operator_list(o0, a1, a2, a3, a4, b4, b3, b2, b1):
+    listed = [(o0, 0), (o0, 1)]
+    for ref in (a1, a2, a3):
+        listed += [(ref, 0), (ref, 1)]
+    listed += [(a4, 0), (b4, 0)]
+    for ref in (b3, b2, b1):
+        listed += [(ref, 0), (ref, 1)]
+    return [lambda ref=ref, i=i: ref[i] for ref, i in listed]
+
+
+def target_kernel(rows, weights, sides, target_half, total):
+    core, *_ = position()
+    half = target_half.shape[1]
+    reps, edges, entities = weights.shape
+    for b in range(reps):
+        standing = rows[b].T.astype(jnp.int32)
+        aimed = one_hot(lanes_of((edges, entities)) == standing[:, 1:2])
+        faces = jnp.concatenate([weights[b], aimed, aimed], axis=0)
+        grown = dot(sides[b], faces, TN)
+        if b == 0:
+            total[...] = grown
+        else:
+            total[...] += grown
+    target_half[...] = total[:, pl.ds(pl.multiple_of(core * half, half), half)].astype(bf16)
+
+
+def source_kernel(
+    o0, a1, a2, a3, a4, b4, b3, b2, b1, rows, query, source_total, held
+):
+    reps, places, _, width = held.shape
+    entities = source_total.shape[1]
+    edges = rows.shape[2]
+    for b in range(reps):
+        into = one_hot(rows_of((places * SLOTS, edges)) == rows[b][2:3].astype(jnp.int32))
+        held[b] = dot(into, query[b]).astype(bf16).reshape(places, SLOTS, width)
+    for place, op in enumerate(operator_list(o0, a1, a2, a3, a4, b4, b3, b2, b1)):
+        given = held[:, place].reshape(-1, width)
+        held[:, place] = dot(given, op(), NT).astype(bf16).reshape(-1, SLOTS, width)
+    for b in range(reps):
+        standing = rows[b].T.astype(jnp.int32)
+        out_of = one_hot(lanes_of((edges, places * SLOTS)) == standing[:, 2:3])
+        back = dot(out_of, held[b].reshape(places * SLOTS, width)).astype(bf16)
+        spread = one_hot(lanes_of((edges, entities)) == standing[:, 0:1])
+        grown = dot(back, spread, TN)
+        if b == 0:
+            source_total[...] = grown
+        else:
+            source_total[...] += grown
+
+
+def entity_kernel(source_total, mine, other, table, state, new_table, new_state):
+    core, *_ = position()
+    half = mine.shape[1]
+    width = table.shape[0]
+    for ref, side in ((mine, core), (other, 1 - core)):
+        at = pl.ds(pl.multiple_of(side * half, half), half)
+        g = source_total[:, at] + ref[...].astype(f32)
+        moments = state[:, at] + jnp.sum(g * g, axis=0, keepdims=True) * (1.0 / width)
+        new_state[:, at] = moments
+        new_table[:, at] = table[:, at] - g * (entity_rate / (jnp.sqrt(moments) + epsilon))
+
+
+def operator_kernel(own, near, far, across, operators, state, new_operators, new_state):
+    _, me, *_ = position()
+    width = operators.shape[1]
+    quarter = width // 4
+    buffers = (own, near, far, across)
+    lane = rows_of((LANES, width))
+    inside = lane % QUARTER
+    for i in range(operators.shape[0]):
+        g = jnp.zeros((width, width), f32)
+        for m in range(4):
+            starting = lax.bitwise_xor(me, m) * quarter
+            put = one_hot(
+                (lane // QUARTER == i)
+                & (inside < quarter)
+                & (inside + starting == lanes_of((LANES, width)))
+            )
+            g = g + dot(buffers[m][...], put)
+        moments = state[i] + g * g
+        new_state[i] = moments
+        new_operators[i] = operators[i] - operator_rate * g / (jnp.sqrt(moments) + epsilon)
+
+
+def rep_swapped(array, by):
+    peers = lax.axis_size("rep")
+    return lax.ppermute(array, "rep", [(i, i ^ by) for i in range(peers)])
+
+
+def ring_step(array, steps=1):
+    groups, reps = lax.axis_size("ent"), lax.axis_size("rep")
+    pairs = []
+    for e in range(groups):
+        for r in range(reps):
+            to = RING[(PLACE[e] + (steps if r % CORES == 0 else -steps)) % groups]
+            pairs.append((e * reps + r, to * reps + r))
+    return lax.ppermute(array, ("ent", "rep"), pairs)
+
+
+def gathered_shards(
+    entity_table, entity_state, operators, operator_state, sources, destinations, relations, negatives
+):
+    groups, reps = lax.axis_size("ent"), lax.axis_size("rep")
+    entities, width = entity_table.shape
+    edges = sources.shape[0]
+    relation_count = groups * operators.shape[0]
+    half = entities // CORES
+    core = lax.axis_index("rep") % CORES
+
+    operators_half = operators.astype(bf16)
+    table = entity_table.T
+    table_half = table.astype(bf16)
+    ids = jnp.concatenate(
+        [
+            sources,
+            destinations,
+            relations[:, 0],
+            negatives[0],
+            jnp.full((5 * edges - negatives.shape[1],), -1, jnp.int32),
+        ]
+    ).reshape(8, edges)
+    places = relation_count
+    slot_out = [
+        jax.ShapeDtypeStruct((reps, places, SLOTS, width), bf16),
+        jax.ShapeDtypeStruct((places // 2, width, reps * 2 * SLOTS), bf16),
+        jax.ShapeDtypeStruct((reps, 8, edges), f32),
+        jax.ShapeDtypeStruct((reps, 1, entities), f32),
+    ]
+    a1 = ring_step(operators_half)
+    others = [rep_swapped(ids, by) for by in (1, 2, 3)]
+    own_half = lax.dynamic_slice_in_dim(table_half, core * half, half, 1)
+    mine = passed_along(own_half, "ent", -1)
+    a1, *others = lax.optimization_barrier((a1, *others))
+    a2 = ring_step(a1)
+    b1 = rep_swapped(a1, 1)
+    slots = call(slot_kernel, slot_out, "slots", 10**9, 10**7, (ids, *others, table_half))
+    a2, b1, mine, *slots = lax.optimization_barrier((a2, b1, mine, *slots))
+    slotted, turned, rows, counts = slots
+    a3 = ring_step(a2)
+    other = rep_swapped(mine, 1)
+    b2 = rep_swapped(a2, 1)
+    a3, b2, other = lax.optimization_barrier((a3, b2, other))
+    a4 = ring_step(lax.dynamic_slice_in_dim(a3, core, 1, 0))
+    b3 = rep_swapped(a3, 1)
+    a4, b3 = lax.optimization_barrier((a4, b3))
+    b4 = rep_swapped(a4, 1)
+    gathered = (operators_half, a1, a2, a3, a4, b4, b3, b2, b1)
+
+    score_out = [jax.ShapeDtypeStruct((width, LANES), bf16)] * groups + [
+        jax.ShapeDtypeStruct((reps, edges, entities), bf16),
+        jax.ShapeDtypeStruct((reps, 3 * edges, width), bf16),
+        jax.ShapeDtypeStruct((reps, edges, width), bf16),
+    ]
+    *outgoing, weights, sides, query = call(
+        functools.partial(score_kernel, negatives.shape[1]), score_out, "scores", 3 * 10**9, 2 * 10**7,
+        (*gathered, slotted, turned, rows, counts, mine, other),
+        scratch=[VMEM((width, entities), bf16), VMEM((reps, places, SLOTS, width), bf16)],
+    )
+    arrived = [outgoing[0]] + [ring_step(part, -m) for m, part in enumerate(outgoing) if m > 0]
+    (target_half,) = call(
+        target_kernel,
+        [jax.ShapeDtypeStruct((width, half), bf16)],
+        "targets", 2 * 10**9, 10**7, (rows, weights, sides),
+        scratch=[VMEM((width, entities), f32)],
+    )
+    (source_total,) = call(
+        source_kernel,
+        [jax.ShapeDtypeStruct((width, entities), f32)],
+        "sources", 2 * 10**9, 10**7, (*gathered, rows, query),
+        scratch=[VMEM((reps, places, SLOTS, width), bf16)],
+    )
+    home_mine = passed_along(target_half, "ent", 1)
+    home_other = rep_swapped(home_mine, 1)
+    quarter = sum(part.astype(f32) for part in arrived).astype(bf16)
+    quarters = [rep_swapped(quarter, by) for by in (1, 2, 3)]
+    new_table, new_state = call(
+        entity_kernel,
+        [
+            jax.ShapeDtypeStruct((width, entities), f32),
+            jax.ShapeDtypeStruct((1, entities), f32),
+        ],
+        "entity_update", 10**7, 4 * 10**6,
+        (source_total, home_mine, home_other, table, entity_state.reshape(1, -1)),
+    )
+    new_operators, new_operator_state = call(
+        operator_kernel,
+        [jax.ShapeDtypeStruct(operators.shape, f32)] * 2,
+        "operator_update", 10**7, 2 * 10**6,
+        (quarter, *quarters, operators, operator_state),
+    )
+    return (new_table.T, new_state.reshape(-1), new_operators, new_operator_state)
+
+
 def solution(mesh):
     placed = (
         P("ent", None),
@@ -138,8 +491,9 @@
         P(("ent", "rep"), None),
         P(("ent", "rep"), None),
     )
+    small = mesh.shape["ent"] == len(RING) and mesh.shape["rep"] == 2 * CORES
     return jax.shard_map(
-        shards,
+        gathered_shards if small else exchanged_shards,
         mesh=mesh,
         in_specs=placed,
         out_specs=(P("ent", None), P("ent"), P("ent", None, None), P("ent", None, None)),

time: 175 us -> 66.4 us (0.38)
  waiting for transfers between devices: 68.1 us -> 16.4 us
  local copies, waits for them, and re-layouts: 42.1 us -> 2.15 us
  other arithmetic: 22.1 us -> 2.31 us
  Pallas kernels: 0 us -> 16.7 us
  between operations: 14.4 us -> 0.82 us
  starting transfers between devices: 23.4 us -> 27.8 us
  matrix products: 3.77 us -> 0 us
    psum x1 -> x0, waiting for transfers between devices: 41.7 us -> none  [shards(): total_grad, total_operator = lax.psum((entity_grad, operator_grad), 'rep')]
    gather x15 -> x0, local copies, waits for them, and re-layouts: 26.9 us -> none  [the longest x9 17.5 us: place_slots(): leading = jnp.searchsorted(ranked, ranked, side='left')]
    ppermute x0 -> x23, starting transfers between devices: none -> 23.6 us  [the longest x11 16.6 us: ring_step(): return lax.ppermute(array, ('ent', 'rep'), pairs)]
    pallas_call x0 -> x6, Pallas kernels: none -> 16.7 us  [call(): pl.pallas_call(body, out_shape=outs, in_specs=[whole] * len(operands), ou...]
    ppermute x0 -> x23, waiting for transfers between devices: none -> 16.4 us  [the longest x11 11.9 us: ring_step(): return lax.ppermute(array, ('ent', 'rep'), pairs)]
    ppermute x2, waiting for transfers between devices: 15.7 us -> 0.01 us  [passed_along(): lax.ppermute(array, axis, [(i, (i + by) % peers) for i in range(peers)])]
    all_to_all x4 -> x0, starting transfers between devices: 15.3 us -> none  [the longest x1 4.55 us: shards(): lax.all_to_all(source_grads, 'ent', split_axis=0, concat_axis=0, tiled=True)]
    scatter-add x3 -> x0, other arithmetic: 12 us -> none  [the longest x1 6.45 us: span_step(): return (running.at[negative_block].add(row_update), query_part)]
  transfers between devices with their start and end apart: 7 -> 25, of which waited for: 5 -> 8; matrix products, arithmetic and copies ran while one was open for 28% -> 3% of each run, Pallas kernels for 0% -> 12%
where the time goes in v2:
time: 66.4 us; the launch traced here: 66.2 us
  starting transfers between devices  27.8 us (42%)
  Pallas kernels  16.7 us (25%)
  waiting for transfers between devices  16.4 us (25%)
  other arithmetic  2.31 us (3%)
  local copies, waits for them, and re-layouts  2.15 us (3%)
  between operations  0.82 us (1%)
    pallas_call x6, Pallas kernels, call(): pl.pallas_call(body, out_shape=outs, in_specs=[whole] * len(operands), ou...  16.7 us
    ppermute x11, starting transfers between devices, ring_step(): return lax.ppermute(array, ('ent', 'rep'), pairs)  16.6 us
    ppermute x11, waiting for transfers between devices, ring_step(): return lax.ppermute(array, ('ent', 'rep'), pairs)  11.9 us
    ppermute x12, starting transfers between devices, rep_swapped(): return lax.ppermute(array, 'rep', [(i, i ^ by) for i in range(peers)])  6.96 us
    ppermute x12, waiting for transfers between devices, rep_swapped(): return lax.ppermute(array, 'rep', [(i, i ^ by) for i in range(peers)])  4.41 us
    ppermute x2, starting transfers between devices, passed_along(): lax.ppermute(array, axis, [(i, (i + by) % peers) for i in range(peers)])  4.2 us
    unnamed x20, local copies, waits for them, and re-layouts  1.35 us
  transfers between devices with their start and end apart: 25, of which 8 were waited for; matrix products, arithmetic and copies ran while one was open for 3% of the time, Pallas kernels for 12%

profile of v2, /device:TPU:0, one launch (start us, length us, event | category | flops | bytes accessed | tf_op | source)
XLA Modules:
  0.0 66.2 jit_solution(1463309471373076820)
XLA Ops:
  1.7 3.1 %collective-permute-start = (bf16[2,200,200]{2,1,0:T(8,128)(2,1)S(1)}, bf16[2,200,200]{2,1,0:T(8,128)(2,1)S(1)}, u32[]{:S(2)}, u32[]{:S(2)}) collective-permute-start(bf16[2,200,200]{2,1,0:T(8,128)(2,1)S(1)} %convert_element_type.33.o0), channel_id=1, source_target_pairs={{0,8},{1,5},{2,10},{3,7},{4,0},{5,13},{6,2},{7,15},{8,16},{9,1},{1... | collective-permute-start | bytes 480008 | tf_op jit(solution)/shard_map/ppermute | solution.py:386
  4.8 1.2 %bitcast_convert_fusion.table = bf16[200,1024]{1,0:T(8,128)(2,1)S(1)} fusion(f32[1024,200]{0,1:T(8,128)} %param.8), kind=kLoop, calls=%fused_computation.3 | loop fusion | flops 204800 | bytes 1228800 | tf_op jit(solution)/shard_map/convert_element_type | solution.py:401
  6.7 3.4 %collective-permute-start.6 = (bf16[200,512]{1,0:T(8,128)(2,1)}, bf16[200,512]{1,0:T(8,128)(2,1)S(1)}, u32[]{:S(2)}, u32[]{:S(2)}) collective-permute-start(bf16[200,512]{1,0:T(8,128)(2,1)} %constant_dynamic-slice_fusion.1), channel_id=1, source_target_pairs={{0,28},{4,0},{8,4},{12,8},{16,12},{20,16},{24,20},{28,24},{1,29},{... | collective-permute-start | bytes 614408 | tf_op jit(solution)/shard_map/ppermute | solution.py:22
  10.7 1.1 %collective-permute-start.2 = (s32[8,256]{1,0:T(8,128)S(1)}, s32[8,256]{1,0:T(8,128)S(1)}, u32[]{:S(2)}, u32[]{:S(2)}) collective-permute-start(s32[8,256]{1,0:T(8,128)S(1)} %reshape.17.own), channel_id=1, source_target_pairs={{0,2},{1,3},{2,0},{3,1},{4,6},{5,7},{6,4},{7,5},{8,10},{9,11},{10,... | collective-permute-start | bytes 24584 | tf_op jit(solution)/shard_map/ppermute | solution.py:376
  12.1 1.2 %collective-permute-done.3.across = s32[8,256]{1,0:T(8,128)S(1)} collective-permute-done((s32[8,256]{1,0:T(8,128)S(1)}, s32[8,256]{1,0:T(8,128)S(1)}, u32[]{:S(2)}, u32[]{:S(2)}) %collective-permute-start.3) | collective-permute-done | bytes 8224 | tf_op jit(solution)/shard_map/ppermute | solution.py:376
  14.5 3.8 %slots.1 = (bf16[4,16,32,200]{3,2,1,0:T(8,128)(2,1)S(1)}, bf16[8,200,256]{2,1,0:T(8,128)(2,1)S(1)}, f32[4,8,256]{2,1,0:T(8,128)S(1)}, f32[4,1,1024]{2,1,0:T(1,128)S(1)}) custom-call(s32[8,256]{1,0:T(8,128)S(1)} %reshape.17.own, s32[8,256]{1,0:T(8,128)S(1)} %collective-permute-done.1.near, s32[8,256]{1,0:T(8,128)S(1)} %collective-permute-done.2.far, ...), custom_call_target="tpu_custom_call" | custom-call | flops 1000000000 | bytes 10000000 | tf_op jit(solution)/shard_map/slots/pallas_call | solution.py:165
  18.9 1.3 %collective-permute-done.4.a2 = bf16[2,200,200]{2,1,0:T(8,128)(2,1)S(1)} collective-permute-done((bf16[2,200,200]{2,1,0:T(8,128)(2,1)S(1)}, bf16[2,200,200]{2,1,0:T(8,128)(2,1)S(1)}, u32[]{:S(2)}, u32[]{:S(2)}) %collective-permute-start.4) | collective-permute-done | bytes 160032 | tf_op jit(solution)/shard_map/ppermute | solution.py:386
  22.0 4.5 %collective-permute-done.7.a3 = bf16[2,200,200]{2,1,0:T(8,128)(2,1)S(1)} collective-permute-done((bf16[2,200,200]{2,1,0:T(8,128)(2,1)S(1)}, bf16[2,200,200]{2,1,0:T(8,128)(2,1)S(1)}, u32[]{:S(2)}, u32[]{:S(2)}) %collective-permute-start.7) | collective-permute-done | bytes 160032 | tf_op jit(solution)/shard_map/ppermute | solution.py:386
  27.0 4.2 %collective-permute-done.10.a4 = bf16[1,200,200]{2,1,0:T(8,128)(2,1)S(1)} collective-permute-done((bf16[1,200,200]{2,1,0:T(8,128)(2,1)S(1)}, bf16[1,200,200]{2,1,0:T(8,128)(2,1)S(1)}, u32[]{:S(2)}, u32[]{:S(2)}) %collective-permute-start.10) | collective-permute-done | bytes 80032 | tf_op jit(solution)/shard_map/ppermute | solution.py:386
  31.3 1.3 %collective-permute-done.12.b4 = bf16[1,200,200]{2,1,0:T(8,128)(2,1)S(1)} collective-permute-done((bf16[1,200,200]{2,1,0:T(8,128)(2,1)S(1)}, bf16[1,200,200]{2,1,0:T(8,128)(2,1)S(1)}, u32[]{:S(2)}, u32[]{:S(2)}) %collective-permute-start.12) | collective-permute-done | bytes 80032 | tf_op jit(solution)/shard_map/ppermute | solution.py:376
  33.3 5.4 %scores.1 = (bf16[200,128]{1,0:T(8,128)(2,1)S(1)}, bf16[200,128]{1,0:T(8,128)(2,1)S(1)}, bf16[200,128]{1,0:T(8,128)(2,1)S(1)}, bf16[200,128]{1,0:T(8,128)(2,1)S(...) custom-call(bf16[2,200,200]{2,1,0:T(8,128)(2,1)S(1)} %convert_elemen, ...), custom_call_target="tpu_custom_call" | custom-call | flops 3000000000 | bytes 20000000 | tf_op jit(solution)/shard_map/scores/pallas_call | solution.py:165
  38.6 1.9 %targets.1 = bf16[200,512]{1,0:T(8,128)(2,1)S(1)} custom-call(f32[4,8,256]{2,1,0:T(8,128)S(1)} %get-tuple-element.54.rows, bf16[4,256,1024]{2,1,0:T(8,128)(2,1)S(1)} %get-tuple-element.60.weights, bf16[4,768,200]{2,1,0:T(8,128)(2,1)S(1)} %get-tuple-element.61.sides), custom_call_target="tpu_custom_call" | custom-call | flops 2000000000 | bytes 10000000 | tf_op jit(solution)/shard_map/targets/pallas_call | solution.py:165
  41.4 1.1 %collective-permute-start.15 = (bf16[200,128]{1,0:T(8,128)(2,1)S(1)}, bf16[200,128]{1,0:T(8,128)(2,1)S(1)}, u32[]{:S(2)}, u32[]{:S(2)}) collective-permute-start(bf16[200,128]{1,0:T(8,128)(2,1)S(1)} %get-tuple-element.65), channel_id=1, source_target_pairs={{0,4},{1,9},{2,6},{3,11},{4,12},{5,1},{6,14},{7,3},{8,0},{9,17},{1... | collective-permute-start | bytes 153608 | tf_op jit(solution)/shard_map/ppermute | solution.py:386
  42.5 1.6 %collective-permute-start.16 = (bf16[200,128]{1,0:T(8,128)(2,1)S(1)}, bf16[200,128]{1,0:T(8,128)(2,1)S(1)}, u32[]{:S(2)}, u32[]{:S(2)}) collective-permute-start(bf16[200,128]{1,0:T(8,128)(2,1)S(1)} %get-tuple-element.66), channel_id=1, source_target_pairs={{0,12},{1,17},{2,14},{3,19},{4,20},{5,9},{6,22},{7,11},{8,4},{9,25... | collective-permute-start | bytes 153608 | tf_op jit(solution)/shard_map/ppermute | solution.py:386
  44.1 1.8 %collective-permute-start.17 = (bf16[200,128]{1,0:T(8,128)(2,1)S(1)}, bf16[200,128]{1,0:T(8,128)(2,1)S(1)}, u32[]{:S(2)}, u32[]{:S(2)}) collective-permute-start(bf16[200,128]{1,0:T(8,128)(2,1)S(1)} %get-tuple-element.67), channel_id=1, source_target_pairs={{0,20},{1,25},{2,22},{3,27},{4,28},{5,17},{6,30},{7,19},{8,12},{9,... | collective-permute-start | bytes 153608 | tf_op jit(solution)/shard_map/ppermute | solution.py:386
  45.9 2.2 %collective-permute-start.18 = (bf16[200,128]{1,0:T(8,128)(2,1)S(1)}, bf16[200,128]{1,0:T(8,128)(2,1)S(1)}, u32[]{:S(2)}, u32[]{:S(2)}) collective-permute-start(bf16[200,128]{1,0:T(8,128)(2,1)S(1)} %get-tuple-element.68), channel_id=1, source_target_pairs={{0,28},{1,29},{2,30},{3,31},{4,24},{5,25},{6,26},{7,27},{8,20},{9,... | collective-permute-start | bytes 153608 | tf_op jit(solution)/shard_map/ppermute | solution.py:386
  48.1 2.5 %collective-permute-start.19 = (bf16[200,128]{1,0:T(8,128)(2,1)S(1)}, bf16[200,128]{1,0:T(8,128)(2,1)S(1)}, u32[]{:S(2)}, u32[]{:S(2)}) collective-permute-start(bf16[200,128]{1,0:T(8,128)(2,1)S(1)} %get-tuple-element.69), channel_id=1, source_target_pairs={{0,24},{1,21},{2,26},{3,23},{4,16},{5,29},{6,18},{7,31},{8,28},{9,... | collective-permute-start | bytes 153608 | tf_op jit(solution)/shard_map/ppermute | solution.py:386
  50.7 2.3 %collective-permute-start.20 = (bf16[200,128]{1,0:T(8,128)(2,1)S(1)}, bf16[200,128]{1,0:T(8,128)(2,1)S(1)}, u32[]{:S(2)}, u32[]{:S(2)}) collective-permute-start(bf16[200,128]{1,0:T(8,128)(2,1)S(1)} %get-tuple-element.70), channel_id=1, source_target_pairs={{0,16},{1,13},{2,18},{3,15},{4,8},{5,21},{6,10},{7,23},{8,24},{9,5... | collective-permute-start | bytes 153608 | tf_op jit(solution)/shard_map/ppermute | solution.py:386
  54.1 1.6 %collective-permute-start.14 = (bf16[200,512]{1,0:T(8,128)(2,1)S(1)}, bf16[200,512]{1,0:T(8,128)(2,1)S(1)}, u32[]{:S(2)}, u32[]{:S(2)}) collective-permute-start(bf16[200,512]{1,0:T(8,128)(2,1)S(1)} %collective-permute-done.13.mine), channel_id=1, source_target_pairs={{0,1},{1,0},{2,3},{3,2},{4,5},{5,4},{6,7},{7,6},{8,9},{9,8},{10,11... | collective-permute-start | bytes 614408 | tf_op jit(solution)/shard_map/ppermute | solution.py:376
  55.7 1.8 %collective-permute-done.19 = bf16[200,128]{1,0:T(8,128)(2,1)S(1)} collective-permute-done((bf16[200,128]{1,0:T(8,128)(2,1)S(1)}, bf16[200,128]{1,0:T(8,128)(2,1)S(1)}, u32[]{:S(2)}, u32[]{:S(2)}) %collective-permute-start.19) | collective-permute-done | bytes 51232 | tf_op jit(solution)/shard_map/ppermute | solution.py:386
  57.6 1.8 %collective-permute-start.24 = (bf16[200,128]{1,0:T(8,128)(2,1)S(1)}, bf16[200,128]{1,0:T(8,128)(2,1)S(1)}, u32[]{:S(2)}, u32[]{:S(2)}) collective-permute-start(bf16[200,128]{1,0:T(8,128)(2,1)S(1)} %add_convert_fusion.own), channel_id=1, source_target_pairs={{0,3},{1,2},{2,1},{3,0},{4,7},{5,6},{6,5},{7,4},{8,11},{9,10},{10,... | collective-permute-start | bytes 153608 | tf_op jit(solution)/shard_map/ppermute | solution.py:376
  60.5 3.1 %sources.1.source_total = f32[200,1024]{1,0:T(8,128)S(1)} custom-call(bf16[2,200,200]{2,1,0:T(8,128)(2,1)S(1)} %convert_element_type.33.o0, bf16[2,200,200]{2,1,0:T(8,128)(2,1)S(1)} %collective-permute-done.a1, bf16[2,200,200]{2,1,0:T(8,128)(2,1)S(1)} %collective-permute-done.4.a2, bf16[2,200,200]{2,1,0:T(8,128)(2,1)S(1)} %collective-permute-done.7.a3, ...), custom_call_target="tpu_custom_call" | custom-call | flops 2000000000 | bytes 10000000 | tf_op jit(solution)/shard_map/sources/pallas_call | solution.py:165
  63.6 1.4 %operator_update.1 = (f32[2,200,200]{2,1,0:T(8,128)}, f32[2,200,200]{2,1,0:T(8,128)}) custom-call(bf16[200,128]{1,0:T(8,128)(2,1)S(1)} %add_convert_fusion.own, bf16[200,128]{1,0:T(8,128)(2,1)S(1)} %collective-permute-done.22.near, bf16[200,128]{1,0:T(8,128)(2,1)S(1)} %collective-permute-done.23.far, bf16[200,128]{1,0:T(8,128)(2,1)S(1)} %collective-permute-done.24.across, ...), custom_call_target="tpu_custom_call" | custom-call | flops 10000000 | bytes 2000000 | tf_op jit(solution)/shard_map/operator_update/pallas_call | solution.py:165
  65.0 1.2 %entity_update.1 = (f32[200,1024]{1,0:T(8,128)}, f32[1,1024]{1,0:T(1,128)}) custom-call(f32[200,1024]{1,0:T(8,128)S(1)} %sources.1.source_total, bf16[200,512]{1,0:T(8,128)(2,1)S(1)} %collective-permute-done.13.mine, bf16[200,512]{1,0:T(8,128)(2,1)S(1)} %collective-permute-done.14.other, f32[200,1024]{1,0:T(8,128)S(1)} %bitcast.7, f32[1,1024]{1,0:T(1,128)S(1)} %bitcast.8), custom_call_target="tpu_custom_call" | custom-call | flops 10000000 | bytes 4000000 | tf_op jit(solution)/shard_map/entity_update/pallas_call | solution.py:165
  (60 shorter events, 10.4 us)
Async XLA Ops:
  1.7 12.7 %collective-permute-start = (bf16[2,200,200]{2,1,0:T(8,128)(2,1)S(1)}, bf16[2,200,200]{2,1,0:T(8,128)(2,1)S(1)}, u32[]{:S(2)}, u32[]{:S(2)}) collective-permute-start(bf16[2,200,200]{2,1,0:T(8,128)(2,1)S(1)} %convert_element_type.33.o0), channel_id=1, source_target_pairs={{0,8},{1,5},{2,10},{3,7},{4,0},{5,13},{6,2},{7,15},{8,16},{9,1},{1... | collective-permute-start | bytes 480008 | tf_op jit(solution)/shard_map/ppermute | solution.py:386
  6.7 12.2 %collective-permute-start.6 = (bf16[200,512]{1,0:T(8,128)(2,1)}, bf16[200,512]{1,0:T(8,128)(2,1)S(1)}, u32[]{:S(2)}, u32[]{:S(2)}) collective-permute-start(bf16[200,512]{1,0:T(8,128)(2,1)} %constant_dynamic-slice_fusion.1), channel_id=1, source_target_pairs={{0,28},{4,0},{8,4},{12,8},{16,12},{20,16},{24,20},{28,24},{1,29},{... | collective-permute-start | bytes 614408 | tf_op jit(solution)/shard_map/ppermute | solution.py:22
  10.2 3.1 %collective-permute-start.3 = (s32[8,256]{1,0:T(8,128)S(1)}, s32[8,256]{1,0:T(8,128)S(1)}, u32[]{:S(2)}, u32[]{:S(2)}) collective-permute-start(s32[8,256]{1,0:T(8,128)S(1)} %reshape.17.own), channel_id=1, source_target_pairs={{0,3},{1,2},{2,1},{3,0},{4,7},{5,6},{6,5},{7,4},{8,11},{9,10},{10,... | collective-permute-start | bytes 24584 | tf_op jit(solution)/shard_map/ppermute | solution.py:376
  10.7 3.7 %collective-permute-start.2 = (s32[8,256]{1,0:T(8,128)S(1)}, s32[8,256]{1,0:T(8,128)S(1)}, u32[]{:S(2)}, u32[]{:S(2)}) collective-permute-start(s32[8,256]{1,0:T(8,128)S(1)} %reshape.17.own), channel_id=1, source_target_pairs={{0,2},{1,3},{2,0},{3,1},{4,6},{5,7},{6,4},{7,5},{8,10},{9,11},{10,... | collective-permute-start | bytes 24584 | tf_op jit(solution)/shard_map/ppermute | solution.py:376
  11.8 2.5 %collective-permute-start.1 = (s32[8,256]{1,0:T(8,128)S(1)}, s32[8,256]{1,0:T(8,128)S(1)}, u32[]{:S(2)}, u32[]{:S(2)}) collective-permute-start(s32[8,256]{1,0:T(8,128)S(1)} %reshape.17.own), channel_id=1, source_target_pairs={{0,1},{1,0},{2,3},{3,2},{4,5},{5,4},{6,7},{7,6},{8,9},{9,8},{10,11... | collective-permute-start | bytes 24584 | tf_op jit(solution)/shard_map/ppermute | solution.py:376
  14.4 4.5 %collective-permute-start.5 = (bf16[2,200,200]{2,1,0:T(8,128)(2,1)S(1)}, bf16[2,200,200]{2,1,0:T(8,128)(2,1)S(1)}, u32[]{:S(2)}, u32[]{:S(2)}) collective-permute-start(bf16[2,200,200]{2,1,0:T(8,128)(2,1)S(1)} %collective-permute-done.a1), channel_id=1, source_target_pairs={{0,1},{1,0},{2,3},{3,2},{4,5},{5,4},{6,7},{7,6},{8,9},{9,8},{10,11... | collective-permute-start | bytes 480008 | tf_op jit(solution)/shard_map/ppermute | solution.py:376
  14.5 5.8 %collective-permute-start.4 = (bf16[2,200,200]{2,1,0:T(8,128)(2,1)S(1)}, bf16[2,200,200]{2,1,0:T(8,128)(2,1)S(1)}, u32[]{:S(2)}, u32[]{:S(2)}) collective-permute-start(bf16[2,200,200]{2,1,0:T(8,128)(2,1)S(1)} %collective-permute-done.a1), channel_id=1, source_target_pairs={{0,8},{1,5},{2,10},{3,7},{4,0},{5,13},{6,2},{7,15},{8,16},{9,1},{1... | collective-permute-start | bytes 480008 | tf_op jit(solution)/shard_map/ppermute | solution.py:386
  20.2 6.3 %collective-permute-start.9 = (bf16[200,512]{1,0:T(8,128)(2,1)S(1)}, bf16[200,512]{1,0:T(8,128)(2,1)S(1)}, u32[]{:S(2)}, u32[]{:S(2)}) collective-permute-start(bf16[200,512]{1,0:T(8,128)(2,1)S(1)} %collective-permute-done.6.mine), channel_id=1, source_target_pairs={{0,1},{1,0},{2,3},{3,2},{4,5},{5,4},{6,7},{7,6},{8,9},{9,8},{10,11... | collective-permute-start | bytes 614408 | tf_op jit(solution)/shard_map/ppermute | solution.py:376
  20.3 1.7 %collective-permute-start.8 = (bf16[2,200,200]{2,1,0:T(8,128)(2,1)S(1)}, bf16[2,200,200]{2,1,0:T(8,128)(2,1)S(1)}, u32[]{:S(2)}, u32[]{:S(2)}) collective-permute-start(bf16[2,200,200]{2,1,0:T(8,128)(2,1)S(1)} %collective-permute-done.4.a2), channel_id=1, source_target_pairs={{0,1},{1,0},{2,3},{3,2},{4,5},{5,4},{6,7},{7,6},{8,9},{9,8},{10,11... | collective-permute-start | bytes 480008 | tf_op jit(solution)/shard_map/ppermute | solution.py:376
  20.8 5.8 %collective-permute-start.7 = (bf16[2,200,200]{2,1,0:T(8,128)(2,1)S(1)}, bf16[2,200,200]{2,1,0:T(8,128)(2,1)S(1)}, u32[]{:S(2)}, u32[]{:S(2)}) collective-permute-start(bf16[2,200,200]{2,1,0:T(8,128)(2,1)S(1)} %collective-permute-done.4.a2), channel_id=1, source_target_pairs={{0,8},{1,5},{2,10},{3,7},{4,0},{5,13},{6,2},{7,15},{8,16},{9,1},{1... | collective-permute-start | bytes 480008 | tf_op jit(solution)/shard_map/ppermute | solution.py:386
  26.5 4.7 %collective-permute-start.11 = (bf16[2,200,200]{2,1,0:T(8,128)(2,1)S(1)}, bf16[2,200,200]{2,1,0:T(8,128)(2,1)S(1)}, u32[]{:S(2)}, u32[]{:S(2)}) collective-permute-start(bf16[2,200,200]{2,1,0:T(8,128)(2,1)S(1)} %collective-permute-done.7.a3), channel_id=1, source_target_pairs={{0,1},{1,0},{2,3},{3,2},{4,5},{5,4},{6,7},{7,6},{8,9},{9,8},{10,11... | collective-permute-start | bytes 480008 | tf_op jit(solution)/shard_map/ppermute | solution.py:376
  26.5 4.7 %collective-permute-start.10 = (bf16[1,200,200]{2,1,0:T(8,128)(2,1)S(1)}, bf16[1,200,200]{2,1,0:T(8,128)(2,1)S(1)}, u32[]{:S(2)}, u32[]{:S(2)}) collective-permute-start(bf16[1,200,200]{2,1,0:T(8,128)(2,1)S(1)} %constant_dynamic-slice_fusion), channel_id=1, source_target_pairs={{0,8},{1,5},{2,10},{3,7},{4,0},{5,13},{6,2},{7,15},{8,16},{9,1},{1... | collective-permute-start | bytes 240008 | tf_op jit(solution)/shard_map/ppermute | solution.py:386
  40.6 13.5 %collective-permute-start.13 = (bf16[200,512]{1,0:T(8,128)(2,1)S(1)}, bf16[200,512]{1,0:T(8,128)(2,1)S(1)}, u32[]{:S(2)}, u32[]{:S(2)}) collective-permute-start(bf16[200,512]{1,0:T(8,128)(2,1)S(1)} %targets.1), channel_id=1, source_target_pairs={{0,4},{4,8},{8,12},{12,16},{16,20},{20,24},{24,28},{28,0},{1,5},{5... | collective-permute-start | bytes 614408 | tf_op jit(solution)/shard_map/ppermute | solution.py:22
  41.4 6.8 %collective-permute-start.15 = (bf16[200,128]{1,0:T(8,128)(2,1)S(1)}, bf16[200,128]{1,0:T(8,128)(2,1)S(1)}, u32[]{:S(2)}, u32[]{:S(2)}) collective-permute-start(bf16[200,128]{1,0:T(8,128)(2,1)S(1)} %get-tuple-element.65), channel_id=1, source_target_pairs={{0,4},{1,9},{2,6},{3,11},{4,12},{5,1},{6,14},{7,3},{8,0},{9,17},{1... | collective-permute-start | bytes 153608 | tf_op jit(solution)/shard_map/ppermute | solution.py:386
  42.5 8.2 %collective-permute-start.16 = (bf16[200,128]{1,0:T(8,128)(2,1)S(1)}, bf16[200,128]{1,0:T(8,128)(2,1)S(1)}, u32[]{:S(2)}, u32[]{:S(2)}) collective-permute-start(bf16[200,128]{1,0:T(8,128)(2,1)S(1)} %get-tuple-element.66), channel_id=1, source_target_pairs={{0,12},{1,17},{2,14},{3,19},{4,20},{5,9},{6,22},{7,11},{8,4},{9,25... | collective-permute-start | bytes 153608 | tf_op jit(solution)/shard_map/ppermute | solution.py:386
  44.1 8.8 %collective-permute-start.17 = (bf16[200,128]{1,0:T(8,128)(2,1)S(1)}, bf16[200,128]{1,0:T(8,128)(2,1)S(1)}, u32[]{:S(2)}, u32[]{:S(2)}) collective-permute-start(bf16[200,128]{1,0:T(8,128)(2,1)S(1)} %get-tuple-element.67), channel_id=1, source_target_pairs={{0,20},{1,25},{2,22},{3,27},{4,28},{5,17},{6,30},{7,19},{8,12},{9,... | collective-permute-start | bytes 153608 | tf_op jit(solution)/shard_map/ppermute | solution.py:386
  45.9 9.8 %collective-permute-start.18 = (bf16[200,128]{1,0:T(8,128)(2,1)S(1)}, bf16[200,128]{1,0:T(8,128)(2,1)S(1)}, u32[]{:S(2)}, u32[]{:S(2)}) collective-permute-start(bf16[200,128]{1,0:T(8,128)(2,1)S(1)} %get-tuple-element.68), channel_id=1, source_target_pairs={{0,28},{1,29},{2,30},{3,31},{4,24},{5,25},{6,26},{7,27},{8,20},{9,... | collective-permute-start | bytes 153608 | tf_op jit(solution)/shard_map/ppermute | solution.py:386
  48.1 9.4 %collective-permute-start.19 = (bf16[200,128]{1,0:T(8,128)(2,1)S(1)}, bf16[200,128]{1,0:T(8,128)(2,1)S(1)}, u32[]{:S(2)}, u32[]{:S(2)}) collective-permute-start(bf16[200,128]{1,0:T(8,128)(2,1)S(1)} %get-tuple-element.69), channel_id=1, source_target_pairs={{0,24},{1,21},{2,26},{3,23},{4,16},{5,29},{6,18},{7,31},{8,28},{9,... | collective-permute-start | bytes 153608 | tf_op jit(solution)/shard_map/ppermute | solution.py:386
  50.7 6.9 %collective-permute-start.20 = (bf16[200,128]{1,0:T(8,128)(2,1)S(1)}, bf16[200,128]{1,0:T(8,128)(2,1)S(1)}, u32[]{:S(2)}, u32[]{:S(2)}) collective-permute-start(bf16[200,128]{1,0:T(8,128)(2,1)S(1)} %get-tuple-element.70), channel_id=1, source_target_pairs={{0,16},{1,13},{2,18},{3,15},{4,8},{5,21},{6,10},{7,23},{8,24},{9,5... | collective-permute-start | bytes 153608 | tf_op jit(solution)/shard_map/ppermute | solution.py:386
  53.0 4.6 %collective-permute-start.21 = (bf16[200,128]{1,0:T(8,128)(2,1)S(1)}, bf16[200,128]{1,0:T(8,128)(2,1)S(1)}, u32[]{:S(2)}, u32[]{:S(2)}) collective-permute-start(bf16[200,128]{1,0:T(8,128)(2,1)S(1)} %get-tuple-element.71), channel_id=1, source_target_pairs={{0,8},{1,5},{2,10},{3,7},{4,0},{5,13},{6,2},{7,15},{8,16},{9,1},{1... | collective-permute-start | bytes 153608 | tf_op jit(solution)/shard_map/ppermute | solution.py:386
  54.1 10.9 %collective-permute-start.14 = (bf16[200,512]{1,0:T(8,128)(2,1)S(1)}, bf16[200,512]{1,0:T(8,128)(2,1)S(1)}, u32[]{:S(2)}, u32[]{:S(2)}) collective-permute-start(bf16[200,512]{1,0:T(8,128)(2,1)S(1)} %collective-permute-done.13.mine), channel_id=1, source_target_pairs={{0,1},{1,0},{2,3},{3,2},{4,5},{5,4},{6,7},{7,6},{8,9},{9,8},{10,11... | collective-permute-start | bytes 614408 | tf_op jit(solution)/shard_map/ppermute | solution.py:376
  57.6 5.9 %collective-permute-start.24 = (bf16[200,128]{1,0:T(8,128)(2,1)S(1)}, bf16[200,128]{1,0:T(8,128)(2,1)S(1)}, u32[]{:S(2)}, u32[]{:S(2)}) collective-permute-start(bf16[200,128]{1,0:T(8,128)(2,1)S(1)} %add_convert_fusion.own), channel_id=1, source_target_pairs={{0,3},{1,2},{2,1},{3,0},{4,7},{5,6},{6,5},{7,4},{8,11},{9,10},{10,... | collective-permute-start | bytes 153608 | tf_op jit(solution)/shard_map/ppermute | solution.py:376
  59.4 4.2 %collective-permute-start.23 = (bf16[200,128]{1,0:T(8,128)(2,1)S(1)}, bf16[200,128]{1,0:T(8,128)(2,1)S(1)}, u32[]{:S(2)}, u32[]{:S(2)}) collective-permute-start(bf16[200,128]{1,0:T(8,128)(2,1)S(1)} %add_convert_fusion.own), channel_id=1, source_target_pairs={{0,2},{1,3},{2,0},{3,1},{4,6},{5,7},{6,4},{7,5},{8,10},{9,11},{10,... | collective-permute-start | bytes 153608 | tf_op jit(solution)/shard_map/ppermute | solution.py:376
  60.4 3.1 %collective-permute-start.22 = (bf16[200,128]{1,0:T(8,128)(2,1)S(1)}, bf16[200,128]{1,0:T(8,128)(2,1)S(1)}, u32[]{:S(2)}, u32[]{:S(2)}) collective-permute-start(bf16[200,128]{1,0:T(8,128)(2,1)S(1)} %add_convert_fusion.own), channel_id=1, source_target_pairs={{0,1},{1,0},{2,3},{3,2},{4,5},{5,4},{6,7},{7,6},{8,9},{9,8},{10,11... | collective-permute-start | bytes 153608 | tf_op jit(solution)/shard_map/ppermute | solution.py:376
  (11 other events, 56.0 us)

commit v3 on v2

--- a/solution.py
+++ b/solution.py
@@ -138,7 +138,7 @@
 RING = (0, 2, 4, 6, 7, 5, 3, 1)
 PLACE = tuple(RING.index(e) for e in range(8))
 SLOTS = 32
-QUARTER = 64
+OFFSETS = ((0, 4), (3, 1), (5, 7), (2, 6))
 VMEM = pltpu.VMEM
 NT = (((1,), (1,)), ((), ()))
 TN = (((0,), (0,)), ((), ()))
@@ -160,12 +160,13 @@
     return jnp.where(mask, 1.0, 0.0).astype(bf16)
 
 
-def call(body, outs, name, flops, size, operands, limit=16, scratch=()):
+def call(body, outs, name, flops, size, operands, limit=16, scratch=(), far=()):
     whole = pl.BlockSpec(memory_space=VMEM)
+    kept = pl.BlockSpec(memory_space=pl.ANY)
     return pl.pallas_call(
         body,
         out_shape=outs,
-        in_specs=[whole] * len(operands),
+        in_specs=[kept if i in far else whole for i in range(len(operands))],
         out_specs=[whole] * len(outs),
         scratch_shapes=list(scratch),
         name=name,
@@ -187,56 +188,63 @@
     return core, rep, chosen_from(PLACE, lax.axis_index("ent")), 2 * core - 1
 
 
-def slot_kernel(own, near, far, across, table, slotted, turned, rows, counts):
-    reps, _, edges = rows.shape
-    buffers = (own, near, far, across)
-    places = slotted.shape[1]
+def slot_kernel(own, near, far, across, table_far, slotted, rows, counts, table, got):
+    fetch = pltpu.make_async_copy(table_far, table, got)
+    fetch.start()
     core, me, here, sign = position()
     ring = len(RING)
+    reps, _, edges = rows.shape
+    places = slotted.shape[1]
+    ids = [ref[...] for ref in (own, near, far, across)]
     before = one_hot(rows_of((edges, edges)) > lanes_of((edges, edges)))
+    relation = jnp.concatenate([block[2:3] for block in ids], axis=0)
+    offset = lax.bitwise_and(
+        sign * (chosen_from(PLACE, lax.shift_right_logical(relation, 1)) - here), ring - 1
+    )
+    parity = lax.bitwise_and(relation, 1)
+    local = 2 * offset + jnp.where(offset == ring // 2, lax.bitwise_xor(parity, core), parity)
+    ends = [block[i : i + 1] for i in (0, 1) for block in ids]
+    standing = jnp.concatenate([local, *ends], axis=0).astype(f32).T
+    column = lambda i: standing[:, i : i + 1].astype(jnp.int32)
+    named = [lanes_of((edges, LANES)) == column(m) for m in range(reps)]
+    ahead = dot(before, one_hot(jnp.concatenate(named, axis=1)))
+    slots = jnp.concatenate(
+        [
+            standing[:, m : m + 1] * SLOTS
+            + jnp.sum(
+                jnp.where(named[m], ahead[:, m * LANES : (m + 1) * LANES], 0.0), axis=1, keepdims=True
+            )
+            for m in range(reps)
+        ],
+        axis=1,
+    ).T
     for m in range(reps):
         block = lax.bitwise_xor(me, m)
-        ids = buffers[m][...]
-        relation = ids[2:3]
-        offset = lax.bitwise_and(
-            sign * (chosen_from(PLACE, lax.shift_right_logical(relation, 1)) - here), ring - 1
+        lying = jnp.concatenate(
+            [ids[m][0:2].astype(f32), slots[m : m + 1], ids[m][3:8].astype(f32)], axis=0
         )
-        parity = lax.bitwise_and(relation, 1)
-        local = 2 * offset + jnp.where(
-            offset == ring // 2, lax.bitwise_xor(parity, core), parity
-        )
-        stacked = jnp.concatenate([ids[0:2], local, ids[3:8]], axis=0).astype(f32)
-        standing = stacked.T
-        local_column = standing[:, 2:3].astype(jnp.int32)
-        named = lanes_of((edges, LANES)) == local_column
-        ahead = dot(before, one_hot(named))
-        slot = local_column.astype(f32) * SLOTS + jnp.sum(
-            jnp.where(named, ahead, 0.0), axis=1, keepdims=True
-        )
-        standing = jnp.where(lanes_of(standing.shape) == 2, slot, standing)
-        lying = standing.T
         rows[block] = lying
-        picked = one_hot(
-            lanes_of((edges, table.shape[1])) == standing[:, 0:1].astype(jnp.int32)
-        )
-        source_rows = dot(picked, table[...], NT).astype(bf16)
-        into = one_hot(rows_of((places * SLOTS, edges)) == lying[2:3].astype(jnp.int32))
-        slotted[block] = dot(into, source_rows).astype(bf16).reshape(places, SLOTS, -1)
         tally = jnp.zeros((8, LANES), f32)
         for k in range(3, 7):
-            drawn = ids[k : k + 1]
+            drawn = ids[m][k : k + 1]
             high = one_hot(rows_of((8, edges)) == lax.shift_right_arithmetic(drawn, 7))
             low = one_hot(rows_of((LANES, edges)) == lax.bitwise_and(drawn, LANES - 1))
             tally = tally + dot(high, low, NT)
         counts[block] = jnp.concatenate([tally[k : k + 1] for k in range(8)], axis=1)
-    for m in range(places // 2):
-        pair = slotted[:, 2 * m : 2 * m + 2].reshape(reps * 2 * SLOTS, -1)
-        turned[m] = pair.astype(f32).T.astype(bf16)
+    picked = [
+        one_hot(lanes_of((edges, table.shape[1])) == column(reps + m)) for m in range(reps)
+    ]
+    fetch.wait()
+    source_rows = dot(jnp.concatenate(picked, axis=0), table[...].astype(bf16), NT).astype(bf16)
+    for m in range(reps):
+        into = one_hot(rows_of((places * SLOTS, edges)) == slots[m : m + 1].astype(jnp.int32))
+        given = dot(into, source_rows[m * edges : (m + 1) * edges]).astype(bf16)
+        slotted[lax.bitwise_xor(me, m)] = given.reshape(places, SLOTS, -1)
 
 
 def score_kernel(
-    negative_count, o0, a1, a2, a3, a4, b4, b3, b2, b1, slotted, turned, rows, counts, mine, other,
-    s0, s1, s2, s3, s4, s5, s6, s7, weights, sides, query, table, moved,
+    negative_count, o0, a1, a2, a3, a4, b4, b3, b2, b1, slotted, rows, counts, mine, other,
+    s0, s1, s2, s3, weights, sides, query, table, moved, asking,
 ):
     core, me, *_ = position()
     reps, places = slotted.shape[:2]
@@ -248,11 +256,11 @@
     for place, op in enumerate(operator_list(o0, a1, a2, a3, a4, b4, b3, b2, b1)):
         given = slotted[:, place].reshape(reps * SLOTS, width)
         moved[:, place] = dot(given, op()).astype(bf16).reshape(reps, SLOTS, width)
-    chosen_lane = lanes_of((width, LANES)) % QUARTER
-    quarter = width // reps
-    chosen = one_hot(
-        (rows_of((width, LANES)) == chosen_lane + me * quarter) & (chosen_lane < quarter)
-    )
+    sent = (s0, s1, s2, s3)
+    handed = []
+    for near, far in OFFSETS:
+        offset = jnp.where(me < CORES, near, far)
+        handed.append(2 * offset + jnp.where(offset == len(RING) // 2, 0, core))
     for b in range(reps):
         lying = rows[b]
         standing = lying.T.astype(jnp.int32)
@@ -274,17 +282,14 @@
         sides[b, edges : 2 * edges] = push_half
         sides[b, 2 * edges :] = (push - push_half.astype(f32)).astype(bf16)
         query[b] = asked
-        part = dot(asked, chosen).astype(bf16)
-        into = one_hot(rows_of((places * SLOTS, edges)) == lying[2:3].astype(jnp.int32))
-        moved[b, :, :, 0:LANES] = dot(into, part).astype(bf16).reshape(places, SLOTS, LANES)
-    size = reps * 2 * SLOTS
-    parity = lax.bitwise_and(lax.shift_right_logical(rows_of((size, LANES)), 5), 1)
-    side = lax.shift_right_logical(lanes_of((size, LANES)), 6)
-    for m, outgoing in enumerate((s0, s1, s2, s3, s4, s5, s6, s7)):
-        pair = moved[:, 2 * m : 2 * m + 2, :, 0:LANES].reshape(size, LANES)
-        kept = side == (lax.bitwise_xor(parity, core) if m == places // 4 else parity)
-        pair = jnp.where(kept, pair.astype(f32), 0.0).astype(bf16)
-        outgoing[...] = dot(turned[m], pair).astype(bf16)
+        slot = lying[2:3].astype(jnp.int32)
+        into = jnp.concatenate(
+            [one_hot(rows_of((SLOTS, edges)) + place * SLOTS == slot) for place in handed], axis=0
+        )
+        asking[b] = dot(into, asked).astype(bf16).reshape(len(sent), SLOTS, width)
+    for k, place in enumerate(handed):
+        given = slotted[:, pl.ds(place, 1)].reshape(reps * SLOTS, width)
+        sent[k][...] = dot(given, asking[:, k].reshape(reps * SLOTS, width), TN).astype(bf16)
 
 
 def operator_list(o0, a1, a2, a3, a4, b4, b3, b2, b1):
@@ -297,28 +302,22 @@
     return [lambda ref=ref, i=i: ref[i] for ref, i in listed]
 
 
-def target_kernel(rows, weights, sides, target_half, total):
+def return_kernel(
+    o0, a1, a2, a3, a4, b4, b3, b2, b1, rows, weights, sides, query, target_half, source_total, total, held
+):
     core, *_ = position()
+    reps, edges, entities = weights.shape
+    places, width = held.shape[1], held.shape[3]
     half = target_half.shape[1]
-    reps, edges, entities = weights.shape
+    standing = [rows[b].T.astype(jnp.int32) for b in range(reps)]
     for b in range(reps):
-        standing = rows[b].T.astype(jnp.int32)
-        aimed = one_hot(lanes_of((edges, entities)) == standing[:, 1:2])
-        faces = jnp.concatenate([weights[b], aimed, aimed], axis=0)
-        grown = dot(sides[b], faces, TN)
+        aimed = one_hot(lanes_of((edges, entities)) == standing[b][:, 1:2])
+        grown = dot(sides[b], jnp.concatenate([weights[b], aimed, aimed], axis=0), TN)
         if b == 0:
             total[...] = grown
         else:
             total[...] += grown
     target_half[...] = total[:, pl.ds(pl.multiple_of(core * half, half), half)].astype(bf16)
-
-
-def source_kernel(
-    o0, a1, a2, a3, a4, b4, b3, b2, b1, rows, query, source_total, held
-):
-    reps, places, _, width = held.shape
-    entities = source_total.shape[1]
-    edges = rows.shape[2]
     for b in range(reps):
         into = one_hot(rows_of((places * SLOTS, edges)) == rows[b][2:3].astype(jnp.int32))
         held[b] = dot(into, query[b]).astype(bf16).reshape(places, SLOTS, width)
@@ -326,10 +325,9 @@
         given = held[:, place].reshape(-1, width)
         held[:, place] = dot(given, op(), NT).astype(bf16).reshape(-1, SLOTS, width)
     for b in range(reps):
-        standing = rows[b].T.astype(jnp.int32)
-        out_of = one_hot(lanes_of((edges, places * SLOTS)) == standing[:, 2:3])
+        out_of = one_hot(lanes_of((edges, places * SLOTS)) == standing[b][:, 2:3])
         back = dot(out_of, held[b].reshape(places * SLOTS, width)).astype(bf16)
-        spread = one_hot(lanes_of((edges, entities)) == standing[:, 0:1])
+        spread = one_hot(lanes_of((edges, entities)) == standing[b][:, 0:1])
         grown = dot(back, spread, TN)
         if b == 0:
             source_total[...] = grown
@@ -341,31 +339,18 @@
     core, *_ = position()
     half = mine.shape[1]
     width = table.shape[0]
-    for ref, side in ((mine, core), (other, 1 - core)):
+    for part, side in ((mine, core), (other, 1 - core)):
         at = pl.ds(pl.multiple_of(side * half, half), half)
-        g = source_total[:, at] + ref[...].astype(f32)
+        g = source_total[:, at] + part[...].astype(f32)
         moments = state[:, at] + jnp.sum(g * g, axis=0, keepdims=True) * (1.0 / width)
         new_state[:, at] = moments
         new_table[:, at] = table[:, at] - g * (entity_rate / (jnp.sqrt(moments) + epsilon))
 
 
-def operator_kernel(own, near, far, across, operators, state, new_operators, new_state):
-    _, me, *_ = position()
-    width = operators.shape[1]
-    quarter = width // 4
-    buffers = (own, near, far, across)
-    lane = rows_of((LANES, width))
-    inside = lane % QUARTER
+def operator_kernel(own, other, operators, state, new_operators, new_state):
+    core, *_ = position()
     for i in range(operators.shape[0]):
-        g = jnp.zeros((width, width), f32)
-        for m in range(4):
-            starting = lax.bitwise_xor(me, m) * quarter
-            put = one_hot(
-                (lane // QUARTER == i)
-                & (inside < quarter)
-                & (inside + starting == lanes_of((LANES, width)))
-            )
-            g = g + dot(buffers[m][...], put)
+        g = jnp.where(core == i, own[...], other[...])
         moments = state[i] + g * g
         new_state[i] = moments
         new_operators[i] = operators[i] - operator_rate * g / (jnp.sqrt(moments) + epsilon)
@@ -376,14 +361,23 @@
     return lax.ppermute(array, "rep", [(i, i ^ by) for i in range(peers)])
 
 
-def ring_step(array, steps=1):
+def along_ring(array, offset_of):
     groups, reps = lax.axis_size("ent"), lax.axis_size("rep")
     pairs = []
     for e in range(groups):
         for r in range(reps):
-            to = RING[(PLACE[e] + (steps if r % CORES == 0 else -steps)) % groups]
+            way = offset_of(r) if r % CORES == 1 else -offset_of(r)
+            to = RING[(PLACE[e] + way) % groups]
             pairs.append((e * reps + r, to * reps + r))
     return lax.ppermute(array, ("ent", "rep"), pairs)
+
+
+def ring_step(array):
+    return along_ring(array, lambda r: -1)
+
+
+def handed_on(array, k):
+    return along_ring(array, lambda r: OFFSETS[k][0 if r < CORES else 1])
 
 
 def gathered_shards(
@@ -398,7 +392,6 @@
 
     operators_half = operators.astype(bf16)
     table = entity_table.T
-    table_half = table.astype(bf16)
     ids = jnp.concatenate(
         [
             sources,
@@ -411,71 +404,75 @@
     places = relation_count
     slot_out = [
         jax.ShapeDtypeStruct((reps, places, SLOTS, width), bf16),
-        jax.ShapeDtypeStruct((places // 2, width, reps * 2 * SLOTS), bf16),
         jax.ShapeDtypeStruct((reps, 8, edges), f32),
         jax.ShapeDtypeStruct((reps, 1, entities), f32),
     ]
     a1 = ring_step(operators_half)
     others = [rep_swapped(ids, by) for by in (1, 2, 3)]
-    own_half = lax.dynamic_slice_in_dim(table_half, core * half, half, 1)
-    mine = passed_along(own_half, "ent", -1)
-    a1, *others = lax.optimization_barrier((a1, *others))
+    own_half = lax.dynamic_slice_in_dim(table, core * half, half, 1).astype(bf16)
+    a1, own_half, *others = lax.optimization_barrier((a1, own_half, *others))
     a2 = ring_step(a1)
     b1 = rep_swapped(a1, 1)
-    slots = call(slot_kernel, slot_out, "slots", 10**9, 10**7, (ids, *others, table_half))
-    a2, b1, mine, *slots = lax.optimization_barrier((a2, b1, mine, *slots))
-    slotted, turned, rows, counts = slots
+    b1, own_half = lax.optimization_barrier((b1, own_half))
+    mine = passed_along(own_half, "ent", -1)
+    a2, b1, *others = lax.optimization_barrier((a2, b1, *others))
     a3 = ring_step(a2)
-    other = rep_swapped(mine, 1)
     b2 = rep_swapped(a2, 1)
-    a3, b2, other = lax.optimization_barrier((a3, b2, other))
+    slots = call(
+        slot_kernel, slot_out, "slots", 10**8, 10**6, (ids, *others, table),
+        scratch=[VMEM((width, entities), f32), pltpu.SemaphoreType.DMA],
+        far=(4,),
+    )
+    a3, b2, mine, *slots = lax.optimization_barrier((a3, b2, mine, *slots))
+    slotted, rows, counts = slots
     a4 = ring_step(lax.dynamic_slice_in_dim(a3, core, 1, 0))
     b3 = rep_swapped(a3, 1)
-    a4, b3 = lax.optimization_barrier((a4, b3))
+    other = rep_swapped(mine, 1)
+    a4, b3, other = lax.optimization_barrier((a4, b3, other))
     b4 = rep_swapped(a4, 1)
     gathered = (operators_half, a1, a2, a3, a4, b4, b3, b2, b1)
 
-    score_out = [jax.ShapeDtypeStruct((width, LANES), bf16)] * groups + [
+    score_out = [jax.ShapeDtypeStruct((width, width), bf16)] * len(OFFSETS) + [
         jax.ShapeDtypeStruct((reps, edges, entities), bf16),
         jax.ShapeDtypeStruct((reps, 3 * edges, width), bf16),
         jax.ShapeDtypeStruct((reps, edges, width), bf16),
     ]
-    *outgoing, weights, sides, query = call(
-        functools.partial(score_kernel, negatives.shape[1]), score_out, "scores", 3 * 10**9, 2 * 10**7,
-        (*gathered, slotted, turned, rows, counts, mine, other),
-        scratch=[VMEM((width, entities), bf16), VMEM((reps, places, SLOTS, width), bf16)],
-    )
-    arrived = [outgoing[0]] + [ring_step(part, -m) for m, part in enumerate(outgoing) if m > 0]
-    (target_half,) = call(
-        target_kernel,
-        [jax.ShapeDtypeStruct((width, half), bf16)],
-        "targets", 2 * 10**9, 10**7, (rows, weights, sides),
-        scratch=[VMEM((width, entities), f32)],
-    )
-    (source_total,) = call(
-        source_kernel,
-        [jax.ShapeDtypeStruct((width, entities), f32)],
-        "sources", 2 * 10**9, 10**7, (*gathered, rows, query),
-        scratch=[VMEM((reps, places, SLOTS, width), bf16)],
+    *handed, weights, sides, query = call(
+        functools.partial(score_kernel, negatives.shape[1]), score_out, "scores", 10**9, 10**6,
+        (*gathered, slotted, rows, counts, mine, other),
+        scratch=[
+            VMEM((width, entities), bf16),
+            VMEM((reps, places, SLOTS, width), bf16),
+            VMEM((reps, len(OFFSETS), SLOTS, width), bf16),
+        ],
+    )
+    arrived = [handed_on(matrix, k) for k, matrix in enumerate(handed)]
+    target_half, source_total = call(
+        return_kernel,
+        [jax.ShapeDtypeStruct((width, half), bf16), jax.ShapeDtypeStruct((width, entities), f32)],
+        "returns", 10**8, 10**6, (*gathered, rows, weights, sides, query),
+        scratch=[VMEM((width, entities), f32), VMEM((reps, places, SLOTS, width), bf16)],
     )
     home_mine = passed_along(target_half, "ent", 1)
     home_other = rep_swapped(home_mine, 1)
-    quarter = sum(part.astype(f32) for part in arrived).astype(bf16)
-    quarters = [rep_swapped(quarter, by) for by in (1, 2, 3)]
+    source_total, *arrived = lax.optimization_barrier((source_total, *arrived))
+    one_chip = sum(matrix.astype(f32) for matrix in arrived).astype(bf16)
+    one_relation = one_chip.astype(f32) + rep_swapped(one_chip, CORES).astype(f32)
+    other_relation = rep_swapped(one_relation, 1)
     new_table, new_state = call(
         entity_kernel,
         [
             jax.ShapeDtypeStruct((width, entities), f32),
             jax.ShapeDtypeStruct((1, entities), f32),
         ],
-        "entity_update", 10**7, 4 * 10**6,
+        "entity_update", 10**6, 10**6,
         (source_total, home_mine, home_other, table, entity_state.reshape(1, -1)),
     )
     new_operators, new_operator_state = call(
         operator_kernel,
         [jax.ShapeDtypeStruct(operators.shape, f32)] * 2,
-        "operator_update", 10**7, 2 * 10**6,
-        (quarter, *quarters, operators, operator_state),
+        "operator_update", 10**6, 10**6,
+        (one_relation, other_relation, operators, operator_state),
     )
     return (new_table.T, new_state.reshape(-1), new_operators, new_operator_state)
 

time: 66.4 us -> 59.2 us (0.89)
  starting transfers between devices: 27.8 us -> 21.8 us
  Pallas kernels: 16.7 us -> 14.2 us
  waiting for transfers between devices: 16.4 us -> 17.8 us
  other arithmetic: 2.31 us -> 1.12 us
  local copies, waits for them, and re-layouts: 2.15 us -> 3.01 us
    ppermute x11 -> x8, starting transfers between devices: 16.6 us -> 10.9 us  [along_ring(): return lax.ppermute(array, ('ent', 'rep'), pairs)]
    ppermute x2, waiting for transfers between devices: 0.01 us -> 4.61 us  [passed_along(): lax.ppermute(array, axis, [(i, (i + by) % peers) for i in range(peers)])]
    ppermute x11 -> x8, waiting for transfers between devices: 11.9 us -> 9.33 us  [along_ring(): return lax.ppermute(array, ('ent', 'rep'), pairs)]
    pallas_call x6 -> x5, Pallas kernels: 16.7 us -> 14.2 us  [call(): pl.pallas_call(body, out_shape=outs, in_specs=[kept if i in far else whol...]
    ppermute x12 -> x11, starting transfers between devices: 6.96 us -> 4.76 us  [rep_swapped(): return lax.ppermute(array, 'rep', [(i, i ^ by) for i in range(peers)])]
    ppermute x2, starting transfers between devices: 4.2 us -> 6.06 us  [passed_along(): lax.ppermute(array, axis, [(i, (i + by) % peers) for i in range(peers)])]
    convert_element_type x2 -> x1, other arithmetic: 1.26 us -> 0.06 us  [gathered_shards(): one_chip = sum((matrix.astype(f32) for matrix in arrived)).astype(bf16)]
    convert_element_type x0 -> x1, local copies, waits for them, and re-layouts: none -> 1.03 us  [gathered_shards(): lax.dynamic_slice_in_dim(table, core * half, half, 1).astype(bf16)]
  transfers between devices with their start and end apart: 25 -> 21, of which waited for: 8 -> 9; matrix products, arithmetic and copies ran while one was open for 3% -> 3% of each run, Pallas kernels for 12% -> 14%
where the time goes in v3:
time: 59.2 us; the launch traced here: 58.6 us
  starting transfers between devices  21.8 us (37%)
  waiting for transfers between devices  17.8 us (30%)
  Pallas kernels  14.2 us (24%)
  local copies, waits for them, and re-layouts  3.01 us (5%)
  other arithmetic  1.12 us (2%)
  between operations  0.74 us (1%)
    pallas_call x5, Pallas kernels, call(): pl.pallas_call(body, out_shape=outs, in_specs=[kept if i in far else whol...  14.2 us
    ppermute x8, starting transfers between devices, along_ring(): return lax.ppermute(array, ('ent', 'rep'), pairs)  10.9 us
    ppermute x8, waiting for transfers between devices, along_ring(): return lax.ppermute(array, ('ent', 'rep'), pairs)  9.33 us
    ppermute x2, starting transfers between devices, passed_along(): lax.ppermute(array, axis, [(i, (i + by) % peers) for i in range(peers)])  6.06 us
    ppermute x11, starting transfers between devices, rep_swapped(): return lax.ppermute(array, 'rep', [(i, i ^ by) for i in range(peers)])  4.76 us
    ppermute x2, waiting for transfers between devices, passed_along(): lax.ppermute(array, axis, [(i, (i + by) % peers) for i in range(peers)])  4.61 us
    ppermute x11, waiting for transfers between devices, rep_swapped(): return lax.ppermute(array, 'rep', [(i, i ^ by) for i in range(peers)])  3.82 us
  transfers between devices with their start and end apart: 21, of which 9 were waited for; matrix products, arithmetic and copies ran while one was open for 3% of the time, Pallas kernels for 14%

profile of v3, /device:TPU:0, one launch (start us, length us, event | category | flops | bytes accessed | tf_op | source)
XLA Modules:
  0.0 58.6 jit_solution(17323209864869181619)
XLA Ops:
  0.6 1.0 %convert_element_type.30.o0 = bf16[2,200,200]{2,1,0:T(8,128)(2,1)S(1)} convert(f32[2,200,200]{2,1,0:T(8,128)} %operators.1) | non-fusion elementwise | flops 80000 | bytes 480000 | tf_op jit(solution)/shard_map/convert_element_type | solution.py:393
  1.7 3.1 %collective-permute-start = (bf16[2,200,200]{2,1,0:T(8,128)(2,1)S(1)}, bf16[2,200,200]{2,1,0:T(8,128)(2,1)S(1)}, u32[]{:S(2)}, u32[]{:S(2)}) collective-permute-start(bf16[2,200,200]{2,1,0:T(8,128)(2,1)S(1)} %convert_element_type.30.o0), channel_id=1, source_target_pairs={{0,8},{1,5},{2,10},{3,7},{4,0},{5,13},{6,2},{7,15},{8,16},{9,1},{1... | collective-permute-start | bytes 480008 | tf_op jit(solution)/shard_map/ppermute | solution.py:372
  7.4 1.0 %fusion = bf16[200,512]{1,0:T(8,128)(2,1)S(1)} fusion(f32[1024,200]{0,1:T(8,128)} %param.8, s32[]{:T(128)S(6)} %select_n.14), kind=kLoop, calls=%fused_computation.1 | loop fusion | bytes 409604 | tf_op jit(solution)/shard_map/convert_element_type | solution.py:412
  8.6 1.2 %collective-permute-done.2.far = s32[8,256]{1,0:T(8,128)S(1)} collective-permute-done((s32[8,256]{1,0:T(8,128)S(1)}, s32[8,256]{1,0:T(8,128)S(1)}, u32[]{:S(2)}, u32[]{:S(2)}) %collective-permute-start.2) | collective-permute-done | bytes 8224 | tf_op jit(solution)/shard_map/ppermute | solution.py:361
  9.9 1.3 %collective-permute-start.4 = (bf16[2,200,200]{2,1,0:T(8,128)(2,1)S(1)}, bf16[2,200,200]{2,1,0:T(8,128)(2,1)S(1)}, u32[]{:S(2)}, u32[]{:S(2)}) collective-permute-start(bf16[2,200,200]{2,1,0:T(8,128)(2,1)S(1)} %collective-permute-done.a1), channel_id=1, source_target_pairs={{0,8},{1,5},{2,10},{3,7},{4,0},{5,13},{6,2},{7,15},{8,16},{9,1},{1... | collective-permute-start | bytes 480008 | tf_op jit(solution)/shard_map/ppermute | solution.py:372
  11.3 3.7 %collective-permute-start.8 = (bf16[200,512]{1,0:T(8,128)(2,1)S(1)}, bf16[200,512]{1,0:T(8,128)(2,1)S(1)}, u32[]{:S(2)}, u32[]{:S(2)}) collective-permute-start(bf16[200,512]{1,0:T(8,128)(2,1)S(1)} %fusion), channel_id=1, source_target_pairs={{0,28},{4,0},{8,4},{12,8},{16,12},{20,16},{24,20},{28,24},{1,29},{... | collective-permute-start | bytes 614408 | tf_op jit(solution)/shard_map/ppermute | solution.py:22
  14.9 2.3 %collective-permute-done.4.a2 = bf16[2,200,200]{2,1,0:T(8,128)(2,1)S(1)} collective-permute-done((bf16[2,200,200]{2,1,0:T(8,128)(2,1)S(1)}, bf16[2,200,200]{2,1,0:T(8,128)(2,1)S(1)}, u32[]{:S(2)}, u32[]{:S(2)}) %collective-permute-start.4) | collective-permute-done | bytes 160032 | tf_op jit(solution)/shard_map/ppermute | solution.py:372
  17.2 1.1 %copy-done = f32[1024,200]{0,1:T(8,128)S(1)} copy-done((f32[1024,200]{0,1:T(8,128)S(1)}, f32[1024,200]{0,1:T(8,128)}, u32[]{:S(2)}) %copy-start) | copy-done | bytes 819224
  18.4 2.7 %slots.1 = (bf16[4,16,32,200]{3,2,1,0:T(8,128)(2,1)S(1)}, f32[4,8,256]{2,1,0:T(8,128)S(1)}, f32[4,1,1024]{2,1,0:T(1,128)S(1)}) custom-call(s32[8,256]{1,0:T(8,128)S(1)} %reshape.17.own, s32[8,256]{1,0:T(8,128)S(1)} %collective-permute-done.1.near, s32[8,256]{1,0:T(8,128)S(1)} %collective-permute-done.2.far, s32[8,256]{1,0:T(8,128)S(1)} %collective-permute-done.3.across, ...), custom_call_target="tpu_custom_call" | custom-call | flops 100000000 | bytes 1000000 | tf_op jit(solution)/shard_map/slots/pallas_call | solution.py:166
  21.1 1.9 %collective-permute-done.6.a3 = bf16[2,200,200]{2,1,0:T(8,128)(2,1)S(1)} collective-permute-done((bf16[2,200,200]{2,1,0:T(8,128)(2,1)S(1)}, bf16[2,200,200]{2,1,0:T(8,128)(2,1)S(1)}, u32[]{:S(2)}, u32[]{:S(2)}) %collective-permute-start.6) | collective-permute-done | bytes 160032 | tf_op jit(solution)/shard_map/ppermute | solution.py:372
  23.5 1.3 %collective-permute-start.9 = (bf16[1,200,200]{2,1,0:T(8,128)(2,1)S(1)}, bf16[1,200,200]{2,1,0:T(8,128)(2,1)S(1)}, u32[]{:S(2)}, u32[]{:S(2)}) collective-permute-start(bf16[1,200,200]{2,1,0:T(8,128)(2,1)S(1)} %constant_dynamic-slice_fusion), channel_id=1, source_target_pairs={{0,8},{1,5},{2,10},{3,7},{4,0},{5,13},{6,2},{7,15},{8,16},{9,1},{1... | collective-permute-start | bytes 240008 | tf_op jit(solution)/shard_map/ppermute | solution.py:372
  24.8 3.4 %collective-permute-done.9.a4 = bf16[1,200,200]{2,1,0:T(8,128)(2,1)S(1)} collective-permute-done((bf16[1,200,200]{2,1,0:T(8,128)(2,1)S(1)}, bf16[1,200,200]{2,1,0:T(8,128)(2,1)S(1)}, u32[]{:S(2)}, u32[]{:S(2)}) %collective-permute-start.9) | collective-permute-done | bytes 80032 | tf_op jit(solution)/shard_map/ppermute | solution.py:372
  28.2 1.3 %collective-permute-done.12.b4 = bf16[1,200,200]{2,1,0:T(8,128)(2,1)S(1)} collective-permute-done((bf16[1,200,200]{2,1,0:T(8,128)(2,1)S(1)}, bf16[1,200,200]{2,1,0:T(8,128)(2,1)S(1)}, u32[]{:S(2)}, u32[]{:S(2)}) %collective-permute-start.12) | collective-permute-done | bytes 80032 | tf_op jit(solution)/shard_map/ppermute | solution.py:361
  29.5 4.6 %scores.1 = (bf16[200,200]{1,0:T(8,128)(2,1)S(1)}, bf16[200,200]{1,0:T(8,128)(2,1)S(1)}, bf16[200,200]{1,0:T(8,128)(2,1)S(1)}, bf16[200,200]{1,0:T(8,128)(2,1)S(...) custom-call(bf16[2,200,200]{2,1,0:T(8,128)(2,1)S(1)} %convert_element_type, ...), custom_call_target="tpu_custom_call" | custom-call | flops 1000000000 | bytes 1000000 | tf_op jit(solution)/shard_map/scores/pallas_call | solution.py:166
  34.9 2.5 %collective-permute-start.14 = (bf16[200,200]{1,0:T(8,128)(2,1)S(1)}, bf16[200,200]{1,0:T(8,128)(2,1)S(1)}, u32[]{:S(2)}, u32[]{:S(2)}) collective-permute-start(bf16[200,200]{1,0:T(8,128)(2,1)S(1)} %get-tuple-element.75), channel_id=1, source_target_pairs={{0,20},{1,25},{2,6},{3,11},{4,28},{5,17},{6,14},{7,3},{8,12},{9,29... | collective-permute-start | bytes 240008 | tf_op jit(solution)/shard_map/ppermute | solution.py:372
  37.4 1.3 %collective-permute-start.15 = (bf16[200,200]{1,0:T(8,128)(2,1)S(1)}, bf16[200,200]{1,0:T(8,128)(2,1)S(1)}, u32[]{:S(2)}, u32[]{:S(2)}) collective-permute-start(bf16[200,200]{1,0:T(8,128)(2,1)S(1)} %get-tuple-element.76), channel_id=1, source_target_pairs={{0,24},{1,21},{2,10},{3,7},{4,16},{5,29},{6,2},{7,15},{8,28},{9,13... | collective-permute-start | bytes 240008 | tf_op jit(solution)/shard_map/ppermute | solution.py:372
  39.4 4.7 %returns.1 = (bf16[200,512]{1,0:T(8,128)(2,1)S(1)}, f32[200,1024]{1,0:T(8,128)S(1)}) custom-call(bf16[2,200,200]{2,1,0:T(8,128)(2,1)S(1)} %convert_element_type.30.o0, bf16[2,200,200]{2,1,0:T(8,128)(2,1)S(1)} %collective-permute-done.a1, bf16[2,200,200]{2,1,0:T(8,128)(2,1)S(1)} %collective-permute-done.4.a2, ...), custom_call_target="tpu_custom_call" | custom-call | flops 100000000 | bytes 1000000 | tf_op jit(solution)/shard_map/returns/pallas_call | solution.py:166
  44.1 2.4 %collective-permute-start.17 = (bf16[200,512]{1,0:T(8,128)(2,1)S(1)}, bf16[200,512]{1,0:T(8,128)(2,1)S(1)}, u32[]{:S(2)}, u32[]{:S(2)}) collective-permute-start(bf16[200,512]{1,0:T(8,128)(2,1)S(1)} %get-tuple-element.79), channel_id=1, source_target_pairs={{0,4},{4,8},{8,12},{12,16},{16,20},{20,24},{24,28},{28,0},{1,5},{5... | collective-permute-start | bytes 614408 | tf_op jit(solution)/shard_map/ppermute | solution.py:22
  46.5 1.7 %collective-permute-done.15 = bf16[200,200]{1,0:T(8,128)(2,1)S(1)} collective-permute-done((bf16[200,200]{1,0:T(8,128)(2,1)S(1)}, bf16[200,200]{1,0:T(8,128)(2,1)S(1)}, u32[]{:S(2)}, u32[]{:S(2)}) %collective-permute-start.15) | collective-permute-done | bytes 80032 | tf_op jit(solution)/shard_map/ppermute | solution.py:372
  48.3 1.7 %collective-permute-start.19 = (bf16[200,200]{1,0:T(8,128)(2,1)S(1)}, bf16[200,200]{1,0:T(8,128)(2,1)S(1)}, u32[]{:S(2)}, u32[]{:S(2)}) collective-permute-start(bf16[200,200]{1,0:T(8,128)(2,1)S(1)} %add_convert_fusion), channel_id=1, source_target_pairs={{0,2},{1,3},{2,0},{3,1},{4,6},{5,7},{6,4},{7,5},{8,10},{9,11},{10,... | collective-permute-start | bytes 240008 | tf_op jit(solution)/shard_map/ppermute | solution.py:361
  50.0 4.6 %collective-permute-done.17.mine = bf16[200,512]{1,0:T(8,128)(2,1)S(1)} collective-permute-done((bf16[200,512]{1,0:T(8,128)(2,1)S(1)}, bf16[200,512]{1,0:T(8,128)(2,1)S(1)}, u32[]{:S(2)}, u32[]{:S(2)}) %collective-permute-start.17) | collective-permute-done | bytes 204832 | tf_op jit(solution)/shard_map/ppermute | solution.py:22
  55.2 1.1 %collective-permute-done.20.other = f32[200,200]{1,0:T(8,128)S(1)} collective-permute-done((f32[200,200]{1,0:T(8,128)S(1)}, f32[200,200]{1,0:T(8,128)S(1)}, u32[]{:S(2)}, u32[]{:S(2)}) %collective-permute-start.20) | collective-permute-done | bytes 160032 | tf_op jit(solution)/shard_map/ppermute | solution.py:361
  56.4 1.1 %operator_update.1 = (f32[2,200,200]{2,1,0:T(8,128)}, f32[2,200,200]{2,1,0:T(8,128)}) custom-call(f32[200,200]{1,0:T(8,128)S(1)} %convert_add_fusion.own, f32[200,200]{1,0:T(8,128)S(1)} %collective-permute-done.20.other, f32[2,200,200]{2,1,0:T(8,128)S(1)} %copy-done.2, f32[2,200,200]{2,1,0:T(8,128)S(1)} %copy-done.3), custom_call_target="tpu_custom_call" | custom-call | flops 1000000 | bytes 1000000 | tf_op jit(solution)/shard_map/operator_update/pallas_call | solution.py:166
  57.4 1.2 %entity_update.1 = (f32[200,1024]{1,0:T(8,128)}, f32[1,1024]{1,0:T(1,128)}) custom-call(f32[200,1024]{1,0:T(8,128)S(1)} %get-tuple-element.78.source_total, bf16[200,512]{1,0:T(8,128)(2,1)S(1)} %collective-permute-done.17.mine, bf16[200,512]{1,0:T(8,128)(2,1)S(1)} %collective-permute-done.18.other, f32[200,1024]{1,0:T(8,128)S(1)} %bitcast.9, ...), custom_call_target="tpu_custom_call" | custom-call | flops 1000000 | bytes 1000000 | tf_op jit(solution)/shard_map/entity_update/pallas_call | solution.py:166
  (41 shorter events, 5.6 us)
Async XLA Ops:
  1.7 8.2 %collective-permute-start = (bf16[2,200,200]{2,1,0:T(8,128)(2,1)S(1)}, bf16[2,200,200]{2,1,0:T(8,128)(2,1)S(1)}, u32[]{:S(2)}, u32[]{:S(2)}) collective-permute-start(bf16[2,200,200]{2,1,0:T(8,128)(2,1)S(1)} %convert_element_type.30.o0), channel_id=1, source_target_pairs={{0,8},{1,5},{2,10},{3,7},{4,0},{5,13},{6,2},{7,15},{8,16},{9,1},{1... | collective-permute-start | bytes 480008 | tf_op jit(solution)/shard_map/ppermute | solution.py:372
  5.6 3.1 %collective-permute-start.3 = (s32[8,256]{1,0:T(8,128)S(1)}, s32[8,256]{1,0:T(8,128)S(1)}, u32[]{:S(2)}, u32[]{:S(2)}) collective-permute-start(s32[8,256]{1,0:T(8,128)S(1)} %reshape.17.own), channel_id=1, source_target_pairs={{0,3},{1,2},{2,1},{3,0},{4,7},{5,6},{6,5},{7,4},{8,11},{9,10},{10,... | collective-permute-start | bytes 24584 | tf_op jit(solution)/shard_map/ppermute | solution.py:361
  6.1 3.7 %collective-permute-start.2 = (s32[8,256]{1,0:T(8,128)S(1)}, s32[8,256]{1,0:T(8,128)S(1)}, u32[]{:S(2)}, u32[]{:S(2)}) collective-permute-start(s32[8,256]{1,0:T(8,128)S(1)} %reshape.17.own), channel_id=1, source_target_pairs={{0,2},{1,3},{2,0},{3,1},{4,6},{5,7},{6,4},{7,5},{8,10},{9,11},{10,... | collective-permute-start | bytes 24584 | tf_op jit(solution)/shard_map/ppermute | solution.py:361
  7.1 2.7 %collective-permute-start.1 = (s32[8,256]{1,0:T(8,128)S(1)}, s32[8,256]{1,0:T(8,128)S(1)}, u32[]{:S(2)}, u32[]{:S(2)}) collective-permute-start(s32[8,256]{1,0:T(8,128)S(1)} %reshape.17.own), channel_id=1, source_target_pairs={{0,1},{1,0},{2,3},{3,2},{4,5},{5,4},{6,7},{7,6},{8,9},{9,8},{10,11... | collective-permute-start | bytes 24584 | tf_op jit(solution)/shard_map/ppermute | solution.py:361
  9.8 1.5 %collective-permute-start.5 = (bf16[2,200,200]{2,1,0:T(8,128)(2,1)S(1)}, bf16[2,200,200]{2,1,0:T(8,128)(2,1)S(1)}, u32[]{:S(2)}, u32[]{:S(2)}) collective-permute-start(bf16[2,200,200]{2,1,0:T(8,128)(2,1)S(1)} %collective-permute-done.a1), channel_id=1, source_target_pairs={{0,1},{1,0},{2,3},{3,2},{4,5},{5,4},{6,7},{7,6},{8,9},{9,8},{10,11... | collective-permute-start | bytes 480008 | tf_op jit(solution)/shard_map/ppermute | solution.py:361
  9.9 7.3 %collective-permute-start.4 = (bf16[2,200,200]{2,1,0:T(8,128)(2,1)S(1)}, bf16[2,200,200]{2,1,0:T(8,128)(2,1)S(1)}, u32[]{:S(2)}, u32[]{:S(2)}) collective-permute-start(bf16[2,200,200]{2,1,0:T(8,128)(2,1)S(1)} %collective-permute-done.a1), channel_id=1, source_target_pairs={{0,8},{1,5},{2,10},{3,7},{4,0},{5,13},{6,2},{7,15},{8,16},{9,1},{1... | collective-permute-start | bytes 480008 | tf_op jit(solution)/shard_map/ppermute | solution.py:372
  11.3 11.7 %collective-permute-start.8 = (bf16[200,512]{1,0:T(8,128)(2,1)S(1)}, bf16[200,512]{1,0:T(8,128)(2,1)S(1)}, u32[]{:S(2)}, u32[]{:S(2)}) collective-permute-start(bf16[200,512]{1,0:T(8,128)(2,1)S(1)} %fusion), channel_id=1, source_target_pairs={{0,28},{4,0},{8,4},{12,8},{16,12},{20,16},{24,20},{28,24},{1,29},{... | collective-permute-start | bytes 614408 | tf_op jit(solution)/shard_map/ppermute | solution.py:22
  17.2 3.9 %collective-permute-start.7 = (bf16[2,200,200]{2,1,0:T(8,128)(2,1)S(1)}, bf16[2,200,200]{2,1,0:T(8,128)(2,1)S(1)}, u32[]{:S(2)}, u32[]{:S(2)}) collective-permute-start(bf16[2,200,200]{2,1,0:T(8,128)(2,1)S(1)} %collective-permute-done.4.a2), channel_id=1, source_target_pairs={{0,1},{1,0},{2,3},{3,2},{4,5},{5,4},{6,7},{7,6},{8,9},{9,8},{10,11... | collective-permute-start | bytes 480008 | tf_op jit(solution)/shard_map/ppermute | solution.py:361
  17.2 5.8 %collective-permute-start.6 = (bf16[2,200,200]{2,1,0:T(8,128)(2,1)S(1)}, bf16[2,200,200]{2,1,0:T(8,128)(2,1)S(1)}, u32[]{:S(2)}, u32[]{:S(2)}) collective-permute-start(bf16[2,200,200]{2,1,0:T(8,128)(2,1)S(1)} %collective-permute-done.4.a2), channel_id=1, source_target_pairs={{0,8},{1,5},{2,10},{3,7},{4,0},{5,13},{6,2},{7,15},{8,16},{9,1},{1... | collective-permute-start | bytes 480008 | tf_op jit(solution)/shard_map/ppermute | solution.py:372
  23.0 5.2 %collective-permute-start.11 = (bf16[200,512]{1,0:T(8,128)(2,1)S(1)}, bf16[200,512]{1,0:T(8,128)(2,1)S(1)}, u32[]{:S(2)}, u32[]{:S(2)}) collective-permute-start(bf16[200,512]{1,0:T(8,128)(2,1)S(1)} %collective-permute-done.8.mine), channel_id=1, source_target_pairs={{0,1},{1,0},{2,3},{3,2},{4,5},{5,4},{6,7},{7,6},{8,9},{9,8},{10,11... | collective-permute-start | bytes 614408 | tf_op jit(solution)/shard_map/ppermute | solution.py:361
  23.0 5.2 %collective-permute-start.10 = (bf16[2,200,200]{2,1,0:T(8,128)(2,1)S(1)}, bf16[2,200,200]{2,1,0:T(8,128)(2,1)S(1)}, u32[]{:S(2)}, u32[]{:S(2)}) collective-permute-start(bf16[2,200,200]{2,1,0:T(8,128)(2,1)S(1)} %collective-permute-done.6.a3), channel_id=1, source_target_pairs={{0,1},{1,0},{2,3},{3,2},{4,5},{5,4},{6,7},{7,6},{8,9},{9,8},{10,11... | collective-permute-start | bytes 480008 | tf_op jit(solution)/shard_map/ppermute | solution.py:361
  23.5 4.7 %collective-permute-start.9 = (bf16[1,200,200]{2,1,0:T(8,128)(2,1)S(1)}, bf16[1,200,200]{2,1,0:T(8,128)(2,1)S(1)}, u32[]{:S(2)}, u32[]{:S(2)}) collective-permute-start(bf16[1,200,200]{2,1,0:T(8,128)(2,1)S(1)} %constant_dynamic-slice_fusion), channel_id=1, source_target_pairs={{0,8},{1,5},{2,10},{3,7},{4,0},{5,13},{6,2},{7,15},{8,16},{9,1},{1... | collective-permute-start | bytes 240008 | tf_op jit(solution)/shard_map/ppermute | solution.py:372
  28.2 1.3 %collective-permute-start.12 = (bf16[1,200,200]{2,1,0:T(8,128)(2,1)S(1)}, bf16[1,200,200]{2,1,0:T(8,128)(2,1)S(1)}, u32[]{:S(2)}, u32[]{:S(2)}) collective-permute-start(bf16[1,200,200]{2,1,0:T(8,128)(2,1)S(1)} %collective-permute-done.9.a4), channel_id=1, source_target_pairs={{0,1},{1,0},{2,3},{3,2},{4,5},{5,4},{6,7},{7,6},{8,9},{9,8},{10,11... | collective-permute-start | bytes 240008 | tf_op jit(solution)/shard_map/ppermute | solution.py:361
  34.2 12.4 %collective-permute-start.13 = (bf16[200,200]{1,0:T(8,128)(2,1)S(1)}, bf16[200,200]{1,0:T(8,128)(2,1)S(1)}, u32[]{:S(2)}, u32[]{:S(2)}) collective-permute-start(bf16[200,200]{1,0:T(8,128)(2,1)S(1)} %get-tuple-element.74), channel_id=1, source_target_pairs={{0,0},{1,1},{2,30},{3,31},{4,4},{5,5},{6,26},{7,27},{8,8},{9,9},{1... | collective-permute-start | bytes 240008 | tf_op jit(solution)/shard_map/ppermute | solution.py:372
  34.9 11.7 %collective-permute-start.14 = (bf16[200,200]{1,0:T(8,128)(2,1)S(1)}, bf16[200,200]{1,0:T(8,128)(2,1)S(1)}, u32[]{:S(2)}, u32[]{:S(2)}) collective-permute-start(bf16[200,200]{1,0:T(8,128)(2,1)S(1)} %get-tuple-element.75), channel_id=1, source_target_pairs={{0,20},{1,25},{2,6},{3,11},{4,28},{5,17},{6,14},{7,3},{8,12},{9,29... | collective-permute-start | bytes 240008 | tf_op jit(solution)/shard_map/ppermute | solution.py:372
  37.4 10.9 %collective-permute-start.15 = (bf16[200,200]{1,0:T(8,128)(2,1)S(1)}, bf16[200,200]{1,0:T(8,128)(2,1)S(1)}, u32[]{:S(2)}, u32[]{:S(2)}) collective-permute-start(bf16[200,200]{1,0:T(8,128)(2,1)S(1)} %get-tuple-element.76), channel_id=1, source_target_pairs={{0,24},{1,21},{2,10},{3,7},{4,16},{5,29},{6,2},{7,15},{8,28},{9,13... | collective-permute-start | bytes 240008 | tf_op jit(solution)/shard_map/ppermute | solution.py:372
  38.7 9.5 %collective-permute-start.16 = (bf16[200,200]{1,0:T(8,128)(2,1)S(1)}, bf16[200,200]{1,0:T(8,128)(2,1)S(1)}, u32[]{:S(2)}, u32[]{:S(2)}) collective-permute-start(bf16[200,200]{1,0:T(8,128)(2,1)S(1)} %get-tuple-element.77), channel_id=1, source_target_pairs={{0,12},{1,17},{2,18},{3,15},{4,20},{5,9},{6,10},{7,23},{8,4},{9,25... | collective-permute-start | bytes 240008 | tf_op jit(solution)/shard_map/ppermute | solution.py:372
  39.4 16.9 %copy-start.2 = (f32[2,200,200]{2,1,0:T(8,128)S(1)}, f32[2,200,200]{2,1,0:T(8,128)}, u32[]{:S(2)}) copy-start(f32[2,200,200]{2,1,0:T(8,128)} %operators.1) | copy-start | bytes 960004
  39.4 16.9 %copy-start.3 = (f32[2,200,200]{2,1,0:T(8,128)S(1)}, f32[2,200,200]{2,1,0:T(8,128)}, u32[]{:S(2)}) copy-start(f32[2,200,200]{2,1,0:T(8,128)} %state.1) | copy-start | bytes 960004
  44.1 13.3 %copy-start.1 = (f32[1024,200]{0,1:T(8,128)S(1)}, f32[1024,200]{0,1:T(8,128)}, u32[]{:S(2)}) copy-start(f32[1024,200]{0,1:T(8,128)} %param.8) | copy-start | bytes 2457604
  44.1 10.5 %collective-permute-start.17 = (bf16[200,512]{1,0:T(8,128)(2,1)S(1)}, bf16[200,512]{1,0:T(8,128)(2,1)S(1)}, u32[]{:S(2)}, u32[]{:S(2)}) collective-permute-start(bf16[200,512]{1,0:T(8,128)(2,1)S(1)} %get-tuple-element.79), channel_id=1, source_target_pairs={{0,4},{4,8},{8,12},{12,16},{16,20},{20,24},{24,28},{28,0},{1,5},{5... | collective-permute-start | bytes 614408 | tf_op jit(solution)/shard_map/ppermute | solution.py:22
  48.3 6.3 %collective-permute-start.19 = (bf16[200,200]{1,0:T(8,128)(2,1)S(1)}, bf16[200,200]{1,0:T(8,128)(2,1)S(1)}, u32[]{:S(2)}, u32[]{:S(2)}) collective-permute-start(bf16[200,200]{1,0:T(8,128)(2,1)S(1)} %add_convert_fusion), channel_id=1, source_target_pairs={{0,2},{1,3},{2,0},{3,1},{4,6},{5,7},{6,4},{7,5},{8,10},{9,11},{10,... | collective-permute-start | bytes 240008 | tf_op jit(solution)/shard_map/ppermute | solution.py:361
  54.6 2.8 %collective-permute-start.18 = (bf16[200,512]{1,0:T(8,128)(2,1)S(1)}, bf16[200,512]{1,0:T(8,128)(2,1)S(1)}, u32[]{:S(2)}, u32[]{:S(2)}) collective-permute-start(bf16[200,512]{1,0:T(8,128)(2,1)S(1)} %collective-permute-done.17.mine), channel_id=1, source_target_pairs={{0,1},{1,0},{2,3},{3,2},{4,5},{5,4},{6,7},{7,6},{8,9},{9,8},{10,11... | collective-permute-start | bytes 614408 | tf_op jit(solution)/shard_map/ppermute | solution.py:361
  54.7 1.7 %collective-permute-start.20 = (f32[200,200]{1,0:T(8,128)S(1)}, f32[200,200]{1,0:T(8,128)S(1)}, u32[]{:S(2)}, u32[]{:S(2)}) collective-permute-start(f32[200,200]{1,0:T(8,128)S(1)} %convert_add_fusion.own), channel_id=1, source_target_pairs={{0,1},{1,0},{2,3},{3,2},{4,5},{5,4},{6,7},{7,6},{8,9},{9,8},{10,11... | collective-permute-start | bytes 480008 | tf_op jit(solution)/shard_map/ppermute | solution.py:361
  (2 other events, 14.5 us)

commit v4 on v3

--- a/solution.py
+++ b/solution.py
@@ -138,6 +138,7 @@
 RING = (0, 2, 4, 6, 7, 5, 3, 1)
 PLACE = tuple(RING.index(e) for e in range(8))
 SLOTS = 32
+SIDE = 104
 OFFSETS = ((0, 4), (3, 1), (5, 7), (2, 6))
 VMEM = pltpu.VMEM
 NT = (((1,), (1,)), ((), ()))
@@ -160,13 +161,12 @@
     return jnp.where(mask, 1.0, 0.0).astype(bf16)
 
 
-def call(body, outs, name, flops, size, operands, limit=16, scratch=(), far=()):
+def call(body, outs, name, flops, size, operands, limit=16, scratch=()):
     whole = pl.BlockSpec(memory_space=VMEM)
-    kept = pl.BlockSpec(memory_space=pl.ANY)
     return pl.pallas_call(
         body,
         out_shape=outs,
-        in_specs=[kept if i in far else whole for i in range(len(operands))],
+        in_specs=[whole] * len(operands),
         out_specs=[whole] * len(outs),
         scratch_shapes=list(scratch),
         name=name,
@@ -188,9 +188,7 @@
     return core, rep, chosen_from(PLACE, lax.axis_index("ent")), 2 * core - 1
 
 
-def slot_kernel(own, near, far, across, table_far, slotted, rows, counts, table, got):
-    fetch = pltpu.make_async_copy(table_far, table, got)
-    fetch.start()
+def slot_kernel(own, near, far, across, table, slotted, rows, counts):
     core, me, here, sign = position()
     ring = len(RING)
     reps, _, edges = rows.shape
@@ -234,8 +232,7 @@
     picked = [
         one_hot(lanes_of((edges, table.shape[1])) == column(reps + m)) for m in range(reps)
     ]
-    fetch.wait()
-    source_rows = dot(jnp.concatenate(picked, axis=0), table[...].astype(bf16), NT).astype(bf16)
+    source_rows = dot(jnp.concatenate(picked, axis=0), table[...], NT).astype(bf16)
     for m in range(reps):
         into = one_hot(rows_of((places * SLOTS, edges)) == slots[m : m + 1].astype(jnp.int32))
         given = dot(into, source_rows[m * edges : (m + 1) * edges]).astype(bf16)
@@ -261,35 +258,63 @@
     for near, far in OFFSETS:
         offset = jnp.where(me < CORES, near, far)
         handed.append(2 * offset + jnp.where(offset == len(RING) // 2, 0, core))
+    lying = [rows[b] for b in range(reps)]
+    standing = [block.T.astype(jnp.int32) for block in lying]
+    made = []
     for b in range(reps):
-        lying = rows[b]
-        standing = lying.T.astype(jnp.int32)
-        out_of = one_hot(lanes_of((edges, places * SLOTS)) == standing[:, 2:3])
-        made = dot(out_of, moved[b].reshape(places * SLOTS, width))
-        made_half = made.astype(bf16)
-        scores = dot(made_half, table[...])
-        aimed = lanes_of((edges, entities)) == standing[:, 1:2]
-        positive = jnp.sum(jnp.where(aimed, scores, 0.0), axis=1, keepdims=True)
-        positive_grad = -(0.5 * jnp.tanh(-0.5 * positive) + 0.5)
-        share = (0.5 * jnp.tanh(0.5 * scores) + 0.5) * (1.0 / negative_count)
-        weighted = (share.astype(bf16).astype(f32) * counts[b]).astype(bf16)
-        target_rows = dot(one_hot(aimed), table[...], NT)
-        asked = (positive_grad * target_rows + dot(weighted, table[...], NT)).astype(bf16)
-        push = positive_grad * made
-        push_half = push.astype(bf16)
-        weights[b] = weighted
-        sides[b, :edges] = made_half
-        sides[b, edges : 2 * edges] = push_half
-        sides[b, 2 * edges :] = (push - push_half.astype(f32)).astype(bf16)
-        query[b] = asked
-        slot = lying[2:3].astype(jnp.int32)
+        out_of = one_hot(lanes_of((edges, places * SLOTS)) == standing[b][:, 2:3])
+        made.append(dot(out_of, moved[b].reshape(places * SLOTS, width)))
+    made = jnp.concatenate(made, axis=0)
+    made_half = made.astype(bf16)
+    scores = dot(made_half, table[...])
+    aimed = lanes_of((reps * edges, entities)) == jnp.concatenate(
+        [block[:, 1:2] for block in standing], axis=0
+    )
+    positive = jnp.sum(jnp.where(aimed, scores, 0.0), axis=1, keepdims=True)
+    positive_grad = -(0.5 * jnp.tanh(-0.5 * positive) + 0.5)
+    share = (0.5 * jnp.tanh(0.5 * scores) + 0.5) * (1.0 / negative_count)
+    share = share.astype(bf16).astype(f32)
+    weighted = jnp.concatenate(
+        [share[b * edges : (b + 1) * edges] * counts[b] for b in range(reps)], axis=0
+    ).astype(bf16)
+    target_rows = dot(one_hot(aimed), table[...], NT)
+    asked = (positive_grad * target_rows + dot(weighted, table[...], NT)).astype(bf16)
+    push = positive_grad * made
+    push_half = push.astype(bf16)
+    push_rest = (push - push_half.astype(f32)).astype(bf16)
+    for b in range(reps):
+        at = slice(b * edges, (b + 1) * edges)
+        weights[b] = weighted[at]
+        sides[b, :edges] = made_half[at]
+        sides[b, edges : 2 * edges] = push_half[at]
+        sides[b, 2 * edges :] = push_rest[at]
+        query[b] = asked[at]
+        slot = lying[b][2:3].astype(jnp.int32)
         into = jnp.concatenate(
             [one_hot(rows_of((SLOTS, edges)) + place * SLOTS == slot) for place in handed], axis=0
         )
-        asking[b] = dot(into, asked).astype(bf16).reshape(len(sent), SLOTS, width)
+        asking[b] = dot(into, asked[at]).astype(bf16).reshape(len(sent), SLOTS, width)
     for k, place in enumerate(handed):
         given = slotted[:, pl.ds(place, 1)].reshape(reps * SLOTS, width)
-        sent[k][...] = dot(given, asking[:, k].reshape(reps * SLOTS, width), TN).astype(bf16)
+        sent[k][...] = packed(dot(given, asking[:, k].reshape(reps * SLOTS, width), TN)).astype(bf16)
+
+
+def packed(matrix):
+    low, side, spare = matrix[:, :LANES], matrix[:, LANES : LANES + 64], matrix[:, LANES + 64 :]
+    side = jnp.concatenate([side[:SIDE], side[side.shape[0] - SIDE :]], axis=1)
+    spare = spare.T
+    rest = jnp.zeros((spare.shape[0], 2 * LANES - spare.shape[1]), spare.dtype)
+    return jnp.concatenate(
+        [low, side, spare[:, :LANES], jnp.concatenate([spare[:, LANES:], rest], axis=1)], axis=0
+    )
+
+
+def unpacked(rows, size):
+    low, side, spare = rows[:size], rows[size : size + SIDE], rows[size + SIDE :]
+    side = jnp.concatenate([side[:, :64], side[2 * SIDE - size :, 64:]], axis=0)
+    count = size - LANES - 64
+    spare = jnp.concatenate([spare[:count], spare[count:, : size - LANES]], axis=1)
+    return jnp.concatenate([low, side, spare.T], axis=1)
 
 
 def operator_list(o0, a1, a2, a3, a4, b4, b3, b2, b1):
@@ -302,22 +327,23 @@
     return [lambda ref=ref, i=i: ref[i] for ref, i in listed]
 
 
-def return_kernel(
-    o0, a1, a2, a3, a4, b4, b3, b2, b1, rows, weights, sides, query, target_half, source_total, total, held
-):
+def target_kernel(rows, weights, sides, target_half, total):
     core, *_ = position()
     reps, edges, entities = weights.shape
-    places, width = held.shape[1], held.shape[3]
     half = target_half.shape[1]
-    standing = [rows[b].T.astype(jnp.int32) for b in range(reps)]
     for b in range(reps):
-        aimed = one_hot(lanes_of((edges, entities)) == standing[b][:, 1:2])
+        aimed = one_hot(lanes_of((edges, entities)) == rows[b].T[:, 1:2].astype(jnp.int32))
         grown = dot(sides[b], jnp.concatenate([weights[b], aimed, aimed], axis=0), TN)
         if b == 0:
             total[...] = grown
         else:
             total[...] += grown
     target_half[...] = total[:, pl.ds(pl.multiple_of(core * half, half), half)].astype(bf16)
+
+
+def source_kernel(o0, a1, a2, a3, a4, b4, b3, b2, b1, rows, query, source_total, held):
+    reps, places, _, width = held.shape
+    edges, entities = rows.shape[2], source_total.shape[1]
     for b in range(reps):
         into = one_hot(rows_of((places * SLOTS, edges)) == rows[b][2:3].astype(jnp.int32))
         held[b] = dot(into, query[b]).astype(bf16).reshape(places, SLOTS, width)
@@ -325,9 +351,10 @@
         given = held[:, place].reshape(-1, width)
         held[:, place] = dot(given, op(), NT).astype(bf16).reshape(-1, SLOTS, width)
     for b in range(reps):
-        out_of = one_hot(lanes_of((edges, places * SLOTS)) == standing[b][:, 2:3])
+        standing = rows[b].T.astype(jnp.int32)
+        out_of = one_hot(lanes_of((edges, places * SLOTS)) == standing[:, 2:3])
         back = dot(out_of, held[b].reshape(places * SLOTS, width)).astype(bf16)
-        spread = one_hot(lanes_of((edges, entities)) == standing[b][:, 0:1])
+        spread = one_hot(lanes_of((edges, entities)) == standing[:, 0:1])
         grown = dot(back, spread, TN)
         if b == 0:
             source_total[...] = grown
@@ -350,7 +377,7 @@
 def operator_kernel(own, other, operators, state, new_operators, new_state):
     core, *_ = position()
     for i in range(operators.shape[0]):
-        g = jnp.where(core == i, own[...], other[...])
+        g = unpacked(jnp.where(core == i, own[...], other[...]), operators.shape[1])
         moments = state[i] + g * g
         new_state[i] = moments
         new_operators[i] = operators[i] - operator_rate * g / (jnp.sqrt(moments) + epsilon)
@@ -415,24 +442,21 @@
     b1 = rep_swapped(a1, 1)
     b1, own_half = lax.optimization_barrier((b1, own_half))
     mine = passed_along(own_half, "ent", -1)
-    a2, b1, *others = lax.optimization_barrier((a2, b1, *others))
+    a2, b1, late_table = lax.optimization_barrier((a2, b1, table))
     a3 = ring_step(a2)
     b2 = rep_swapped(a2, 1)
-    slots = call(
-        slot_kernel, slot_out, "slots", 10**8, 10**6, (ids, *others, table),
-        scratch=[VMEM((width, entities), f32), pltpu.SemaphoreType.DMA],
-        far=(4,),
-    )
+    table_half = late_table.astype(bf16)
+    slots = call(slot_kernel, slot_out, "slots", 10**8, 10**6, (ids, *others, table_half))
     a3, b2, mine, *slots = lax.optimization_barrier((a3, b2, mine, *slots))
     slotted, rows, counts = slots
     a4 = ring_step(lax.dynamic_slice_in_dim(a3, core, 1, 0))
+    other = rep_swapped(mine, 1)
+    a4, a3 = lax.optimization_barrier((a4, a3))
     b3 = rep_swapped(a3, 1)
-    other = rep_swapped(mine, 1)
-    a4, b3, other = lax.optimization_barrier((a4, b3, other))
     b4 = rep_swapped(a4, 1)
     gathered = (operators_half, a1, a2, a3, a4, b4, b3, b2, b1)
 
-    score_out = [jax.ShapeDtypeStruct((width, width), bf16)] * len(OFFSETS) + [
+    score_out = [jax.ShapeDtypeStruct((width + SIDE + 16, LANES), bf16)] * len(OFFSETS) + [
         jax.ShapeDtypeStruct((reps, edges, entities), bf16),
         jax.ShapeDtypeStruct((reps, 3 * edges, width), bf16),
         jax.ShapeDtypeStruct((reps, edges, width), bf16),
@@ -447,11 +471,18 @@
         ],
     )
     arrived = [handed_on(matrix, k) for k, matrix in enumerate(handed)]
-    target_half, source_total = call(
-        return_kernel,
-        [jax.ShapeDtypeStruct((width, half), bf16), jax.ShapeDtypeStruct((width, entities), f32)],
-        "returns", 10**8, 10**6, (*gathered, rows, weights, sides, query),
-        scratch=[VMEM((width, entities), f32), VMEM((reps, places, SLOTS, width), bf16)],
+    (target_half,) = call(
+        target_kernel,
+        [jax.ShapeDtypeStruct((width, half), bf16)],
+        "targets", 10**8, 10**6, (rows, weights, sides),
+        scratch=[VMEM((width, entities), f32)],
+    )
+    query, target_half = lax.optimization_barrier((query, target_half))
+    (source_total,) = call(
+        source_kernel,
+        [jax.ShapeDtypeStruct((width, entities), f32)],
+        "sources", 10**8, 10**6, (*gathered, rows, query),
+        scratch=[VMEM((reps, places, SLOTS, width), bf16)],
     )
     home_mine = passed_along(target_half, "ent", 1)
     home_other = rep_swapped(home_mine, 1)

time: 59.2 us -> 56.5 us (0.954)
  waiting for transfers between devices: 17.8 us -> 14.5 us
  starting transfers between devices: 21.8 us -> 23.1 us
  other arithmetic: 1.12 us -> 2.29 us
  local copies, waits for them, and re-layouts: 3.01 us -> 1.88 us
  Pallas kernels: 14.2 us -> 13.6 us
    ppermute x2, waiting for transfers between devices: 4.61 us -> 1.58 us  [passed_along(): lax.ppermute(array, axis, [(i, (i + by) % peers) for i in range(peers)])]
    convert_element_type x0 -> x1, other arithmetic: none -> 1.2 us  [gathered_shards(): table_half = late_table.astype(bf16)]
    ppermute x11, starting transfers between devices: 4.76 us -> 5.94 us  [rep_swapped(): return lax.ppermute(array, 'rep', [(i, i ^ by) for i in range(peers)])]
    unnamed x10 -> x8, local copies, waits for them, and re-layouts: 1.16 us -> 0.03 us
    ppermute x8, waiting for transfers between devices: 9.33 us -> 8.22 us  [along_ring(): return lax.ppermute(array, ('ent', 'rep'), pairs)]
    ppermute x11, waiting for transfers between devices: 3.82 us -> 4.7 us  [rep_swapped(): return lax.ppermute(array, 'rep', [(i, i ^ by) for i in range(peers)])]
    pallas_call x5 -> x6, Pallas kernels: 14.2 us -> 13.6 us  [call(): pl.pallas_call(body, out_shape=outs, in_specs=[whole] * len(operands), ou...]
  transfers between devices with their start and end apart: 21 -> 21, of which waited for: 9 -> 9; matrix products, arithmetic and copies ran while one was open for 3% -> 6% of each run, Pallas kernels for 14% -> 15%
where the time goes in v4:
time: 56.5 us; the launch traced here: 56.2 us
  starting transfers between devices  23.1 us (41%)
  waiting for transfers between devices  14.5 us (26%)
  Pallas kernels  13.6 us (24%)
  other arithmetic  2.29 us (4%)
  local copies, waits for them, and re-layouts  1.88 us (3%)
  between operations  0.79 us (1%)
    pallas_call x6, Pallas kernels, call(): pl.pallas_call(body, out_shape=outs, in_specs=[whole] * len(operands), ou...  13.6 us
    ppermute x8, starting transfers between devices, along_ring(): return lax.ppermute(array, ('ent', 'rep'), pairs)  10.9 us
    ppermute x8, waiting for transfers between devices, along_ring(): return lax.ppermute(array, ('ent', 'rep'), pairs)  8.22 us
    ppermute x2, starting transfers between devices, passed_along(): lax.ppermute(array, axis, [(i, (i + by) % peers) for i in range(peers)])  6.26 us
    ppermute x11, starting transfers between devices, rep_swapped(): return lax.ppermute(array, 'rep', [(i, i ^ by) for i in range(peers)])  5.94 us
    ppermute x11, waiting for transfers between devices, rep_swapped(): return lax.ppermute(array, 'rep', [(i, i ^ by) for i in range(peers)])  4.7 us
    ppermute x2, waiting for transfers between devices, passed_along(): lax.ppermute(array, axis, [(i, (i + by) % peers) for i in range(peers)])  1.58 us
    convert_element_type x1, other arithmetic, gathered_shards(): table_half = late_table.astype(bf16)  1.2 us
  transfers between devices with their start and end apart: 21, of which 9 were waited for; matrix products, arithmetic and copies ran while one was open for 6% of the time, Pallas kernels for 15%

profile of v4, /device:TPU:0, one launch (start us, length us, event | category | flops | bytes accessed | tf_op | source)
XLA Modules:
  0.0 56.2 jit_solution(18336000712750854099)
XLA Ops:
  0.6 1.0 %convert_element_type.33.o0 = bf16[2,200,200]{2,1,0:T(8,128)(2,1)S(1)} convert(f32[2,200,200]{2,1,0:T(8,128)} %operators.1) | non-fusion elementwise | flops 80000 | bytes 480000 | tf_op jit(solution)/shard_map/convert_element_type | solution.py:420
  1.7 3.1 %collective-permute-start = (bf16[2,200,200]{2,1,0:T(8,128)(2,1)S(1)}, bf16[2,200,200]{2,1,0:T(8,128)(2,1)S(1)}, u32[]{:S(2)}, u32[]{:S(2)}) collective-permute-start(bf16[2,200,200]{2,1,0:T(8,128)(2,1)S(1)} %convert_element_type.33.o0), channel_id=1, source_target_pairs={{0,8},{1,5},{2,10},{3,7},{4,0},{5,13},{6,2},{7,15},{8,16},{9,1},{1... | collective-permute-start | bytes 480008 | tf_op jit(solution)/shard_map/ppermute | solution.py:399
  7.4 1.0 %fusion = bf16[200,512]{1,0:T(8,128)(2,1)S(1)} fusion(f32[1024,200]{0,1:T(8,128)} %param.8, s32[]{:T(128)S(6)} %select_n.14), kind=kLoop, calls=%fused_computation.1 | loop fusion | bytes 409604 | tf_op jit(solution)/shard_map/convert_element_type | solution.py:439
  8.6 1.2 %collective-permute-done.2.far = s32[8,256]{1,0:T(8,128)S(1)} collective-permute-done((s32[8,256]{1,0:T(8,128)S(1)}, s32[8,256]{1,0:T(8,128)S(1)}, u32[]{:S(2)}, u32[]{:S(2)}) %collective-permute-start.2) | collective-permute-done | bytes 8224 | tf_op jit(solution)/shard_map/ppermute | solution.py:388
  9.9 1.3 %collective-permute-start.4 = (bf16[2,200,200]{2,1,0:T(8,128)(2,1)S(1)}, bf16[2,200,200]{2,1,0:T(8,128)(2,1)S(1)}, u32[]{:S(2)}, u32[]{:S(2)}) collective-permute-start(bf16[2,200,200]{2,1,0:T(8,128)(2,1)S(1)} %collective-permute-done.a1), channel_id=1, source_target_pairs={{0,8},{1,5},{2,10},{3,7},{4,0},{5,13},{6,2},{7,15},{8,16},{9,1},{1... | collective-permute-start | bytes 480008 | tf_op jit(solution)/shard_map/ppermute | solution.py:399
  11.3 3.7 %collective-permute-start.8 = (bf16[200,512]{1,0:T(8,128)(2,1)S(1)}, bf16[200,512]{1,0:T(8,128)(2,1)S(1)}, u32[]{:S(2)}, u32[]{:S(2)}) collective-permute-start(bf16[200,512]{1,0:T(8,128)(2,1)S(1)} %fusion), channel_id=1, source_target_pairs={{0,28},{4,0},{8,4},{12,8},{16,12},{20,16},{24,20},{28,24},{1,29},{... | collective-permute-start | bytes 614408 | tf_op jit(solution)/shard_map/ppermute | solution.py:22
  14.9 2.3 %collective-permute-done.4.a2 = bf16[2,200,200]{2,1,0:T(8,128)(2,1)S(1)} collective-permute-done((bf16[2,200,200]{2,1,0:T(8,128)(2,1)S(1)}, bf16[2,200,200]{2,1,0:T(8,128)(2,1)S(1)}, u32[]{:S(2)}, u32[]{:S(2)}) %collective-permute-start.4) | collective-permute-done | bytes 160032 | tf_op jit(solution)/shard_map/ppermute | solution.py:399
  17.2 1.2 %convert_element_type.36.table = bf16[200,1024]{1,0:T(8,128)(2,1)S(1)} convert(f32[200,1024]{1,0:T(8,128)} %bitcast.8) | non-fusion elementwise | flops 204800 | bytes 1228800 | tf_op jit(solution)/shard_map/convert_element_type | solution.py:448
  18.4 2.0 %slots.1 = (bf16[4,16,32,200]{3,2,1,0:T(8,128)(2,1)S(1)}, f32[4,8,256]{2,1,0:T(8,128)S(1)}, f32[4,1,1024]{2,1,0:T(1,128)S(1)}) custom-call(s32[8,256]{1,0:T(8,128)S(1)} %reshape.17.own, s32[8,256]{1,0:T(8,128)S(1)} %collective-permute-done.1.near, s32[8,256]{1,0:T(8,128)S(1)} %collective-permute-done.2.far, s32[8,256]{1,0:T(8,128)S(1)} %collective-permute-done.3.across, ...), custom_call_target="tpu_custom_call" | custom-call | flops 100000000 | bytes 1000000 | tf_op jit(solution)/shard_map/slots/pallas_call | solution.py:166
  20.5 2.5 %collective-permute-done.6.a3 = bf16[2,200,200]{2,1,0:T(8,128)(2,1)S(1)} collective-permute-done((bf16[2,200,200]{2,1,0:T(8,128)(2,1)S(1)}, bf16[2,200,200]{2,1,0:T(8,128)(2,1)S(1)}, u32[]{:S(2)}, u32[]{:S(2)}) %collective-permute-start.6) | collective-permute-done | bytes 160032 | tf_op jit(solution)/shard_map/ppermute | solution.py:399
  23.0 1.3 %collective-permute-start.9 = (bf16[1,200,200]{2,1,0:T(8,128)(2,1)S(1)}, bf16[1,200,200]{2,1,0:T(8,128)(2,1)S(1)}, u32[]{:S(2)}, u32[]{:S(2)}) collective-permute-start(bf16[1,200,200]{2,1,0:T(8,128)(2,1)S(1)} %constant_dynamic-slice_fusion), channel_id=1, source_target_pairs={{0,8},{1,5},{2,10},{3,7},{4,0},{5,13},{6,2},{7,15},{8,16},{9,1},{1... | collective-permute-start | bytes 240008 | tf_op jit(solution)/shard_map/ppermute | solution.py:399
  24.3 3.4 %collective-permute-done.9.a4 = bf16[1,200,200]{2,1,0:T(8,128)(2,1)S(1)} collective-permute-done((bf16[1,200,200]{2,1,0:T(8,128)(2,1)S(1)}, bf16[1,200,200]{2,1,0:T(8,128)(2,1)S(1)}, u32[]{:S(2)}, u32[]{:S(2)}) %collective-permute-start.9) | collective-permute-done | bytes 80032 | tf_op jit(solution)/shard_map/ppermute | solution.py:399
  28.2 1.1 %collective-permute-done.10.b4 = bf16[1,200,200]{2,1,0:T(8,128)(2,1)S(1)} collective-permute-done((bf16[1,200,200]{2,1,0:T(8,128)(2,1)S(1)}, bf16[1,200,200]{2,1,0:T(8,128)(2,1)S(1)}, u32[]{:S(2)}, u32[]{:S(2)}) %collective-permute-start.10) | collective-permute-done | bytes 80032 | tf_op jit(solution)/shard_map/ppermute | solution.py:388
  29.3 4.2 %scores.1 = (bf16[320,128]{1,0:T(8,128)(2,1)S(1)}, bf16[320,128]{1,0:T(8,128)(2,1)S(1)}, bf16[320,128]{1,0:T(8,128)(2,1)S(1)}, bf16[320,128]{1,0:T(8,128)(2,1)S(...) custom-call(bf16[2,200,200]{2,1,0:T(8,128)(2,1)S(1)} %convert_element_type, ...), custom_call_target="tpu_custom_call" | custom-call | flops 1000000000 | bytes 1000000 | tf_op jit(solution)/shard_map/scores/pallas_call | solution.py:166
  34.2 2.5 %collective-permute-start.14 = (bf16[320,128]{1,0:T(8,128)(2,1)S(1)}, bf16[320,128]{1,0:T(8,128)(2,1)S(1)}, u32[]{:S(2)}, u32[]{:S(2)}) collective-permute-start(bf16[320,128]{1,0:T(8,128)(2,1)S(1)} %get-tuple-element.69), channel_id=1, source_target_pairs={{0,20},{1,25},{2,6},{3,11},{4,28},{5,17},{6,14},{7,3},{8,12},{9,29... | collective-permute-start | bytes 245768 | tf_op jit(solution)/shard_map/ppermute | solution.py:399
  36.7 1.4 %collective-permute-start.15 = (bf16[320,128]{1,0:T(8,128)(2,1)S(1)}, bf16[320,128]{1,0:T(8,128)(2,1)S(1)}, u32[]{:S(2)}, u32[]{:S(2)}) collective-permute-start(bf16[320,128]{1,0:T(8,128)(2,1)S(1)} %get-tuple-element.70), channel_id=1, source_target_pairs={{0,24},{1,21},{2,10},{3,7},{4,16},{5,29},{6,2},{7,15},{8,28},{9,13... | collective-permute-start | bytes 245768 | tf_op jit(solution)/shard_map/ppermute | solution.py:399
  38.7 2.0 %targets.1 = bf16[200,512]{1,0:T(8,128)(2,1)S(1)} custom-call(f32[4,8,256]{2,1,0:T(8,128)S(1)} %get-tuple-element.60.rows, bf16[4,256,1024]{2,1,0:T(8,128)(2,1)S(1)} %get-tuple-element.65.weights, bf16[4,768,200]{2,1,0:T(8,128)(2,1)S(1)} %get-tuple-element.66.sides), custom_call_target="tpu_custom_call" | custom-call | flops 100000000 | bytes 1000000 | tf_op jit(solution)/shard_map/targets/pallas_call | solution.py:166
  40.7 2.6 %collective-permute-start.17 = (bf16[200,512]{1,0:T(8,128)(2,1)S(1)}, bf16[200,512]{1,0:T(8,128)(2,1)S(1)}, u32[]{:S(2)}, u32[]{:S(2)}) collective-permute-start(bf16[200,512]{1,0:T(8,128)(2,1)S(1)} %targets.1), channel_id=1, source_target_pairs={{0,4},{4,8},{8,12},{12,16},{16,20},{20,24},{24,28},{28,0},{1,5},{5... | collective-permute-start | bytes 614408 | tf_op jit(solution)/shard_map/ppermute | solution.py:22
  43.4 3.1 %sources.1.source_total = f32[200,1024]{1,0:T(8,128)S(1)} custom-call(bf16[2,200,200]{2,1,0:T(8,128)(2,1)S(1)} %convert_element_type.33.o0, bf16[2,200,200]{2,1,0:T(8,128)(2,1)S(1)} %collective-permute-done.a1, bf16[2,200,200]{2,1,0:T(8,128)(2,1)S(1)} %collective-permute-done.4.a2, bf16[2,200,200]{2,1,0:T(8,128)(2,1)S(1)} %collective-permute-done.6.a3, ...), custom_call_target="tpu_custom_call" | custom-call | flops 100000000 | bytes 1000000 | tf_op jit(solution)/shard_map/sources/pallas_call | solution.py:166
  46.5 3.4 %collective-permute-start.19 = (bf16[320,128]{1,0:T(8,128)(2,1)S(1)}, bf16[320,128]{1,0:T(8,128)(2,1)S(1)}, u32[]{:S(2)}, u32[]{:S(2)}) collective-permute-start(bf16[320,128]{1,0:T(8,128)(2,1)S(1)} %add_convert_fusion), channel_id=1, source_target_pairs={{0,2},{1,3},{2,0},{3,1},{4,6},{5,7},{6,4},{7,5},{8,10},{9,11},{10,... | collective-permute-start | bytes 245768 | tf_op jit(solution)/shard_map/ppermute | solution.py:388
  49.9 1.6 %collective-permute-done.17.mine = bf16[200,512]{1,0:T(8,128)(2,1)S(1)} collective-permute-done((bf16[200,512]{1,0:T(8,128)(2,1)S(1)}, bf16[200,512]{1,0:T(8,128)(2,1)S(1)}, u32[]{:S(2)}, u32[]{:S(2)}) %collective-permute-start.17) | collective-permute-done | bytes 204832 | tf_op jit(solution)/shard_map/ppermute | solution.py:22
  52.4 1.4 %collective-permute-done.20.other = f32[320,128]{1,0:T(8,128)S(1)} collective-permute-done((f32[320,128]{1,0:T(8,128)S(1)}, f32[320,128]{1,0:T(8,128)S(1)}, u32[]{:S(2)}, u32[]{:S(2)}) %collective-permute-start.20) | collective-permute-done | bytes 163872 | tf_op jit(solution)/shard_map/ppermute | solution.py:388
  53.8 1.2 %operator_update.1 = (f32[2,200,200]{2,1,0:T(8,128)}, f32[2,200,200]{2,1,0:T(8,128)}) custom-call(f32[320,128]{1,0:T(8,128)S(1)} %convert_add_fusion.own, f32[320,128]{1,0:T(8,128)S(1)} %collective-permute-done.20.other, f32[2,200,200]{2,1,0:T(8,128)S(1)} %copy-done.1, f32[2,200,200]{2,1,0:T(8,128)S(1)} %copy-done.2), custom_call_target="tpu_custom_call" | custom-call | flops 1000000 | bytes 1000000 | tf_op jit(solution)/shard_map/operator_update/pallas_call | solution.py:166
  55.1 1.2 %entity_update.1 = (f32[200,1024]{1,0:T(8,128)}, f32[1,1024]{1,0:T(1,128)}) custom-call(f32[200,1024]{1,0:T(8,128)S(1)} %sources.1.source_total, bf16[200,512]{1,0:T(8,128)(2,1)S(1)} %collective-permute-done.17.mine, bf16[200,512]{1,0:T(8,128)(2,1)S(1)} %collective-permute-done.18.other, f32[200,1024]{1,0:T(8,128)S(1)} %bitcast.9, f32[1,1024]{1,0:T(1,128)S(1)} %bitcast.10), custom_call_target="tpu_custom_call" | custom-call | flops 1000000 | bytes 1000000 | tf_op jit(solution)/shard_map/entity_update/pallas_call | solution.py:166
  (41 shorter events, 5.9 us)
Async XLA Ops:
  1.7 8.2 %collective-permute-start = (bf16[2,200,200]{2,1,0:T(8,128)(2,1)S(1)}, bf16[2,200,200]{2,1,0:T(8,128)(2,1)S(1)}, u32[]{:S(2)}, u32[]{:S(2)}) collective-permute-start(bf16[2,200,200]{2,1,0:T(8,128)(2,1)S(1)} %convert_element_type.33.o0), channel_id=1, source_target_pairs={{0,8},{1,5},{2,10},{3,7},{4,0},{5,13},{6,2},{7,15},{8,16},{9,1},{1... | collective-permute-start | bytes 480008 | tf_op jit(solution)/shard_map/ppermute | solution.py:399
  5.6 3.1 %collective-permute-start.3 = (s32[8,256]{1,0:T(8,128)S(1)}, s32[8,256]{1,0:T(8,128)S(1)}, u32[]{:S(2)}, u32[]{:S(2)}) collective-permute-start(s32[8,256]{1,0:T(8,128)S(1)} %reshape.17.own), channel_id=1, source_target_pairs={{0,3},{1,2},{2,1},{3,0},{4,7},{5,6},{6,5},{7,4},{8,11},{9,10},{10,... | collective-permute-start | bytes 24584 | tf_op jit(solution)/shard_map/ppermute | solution.py:388
  6.1 3.7 %collective-permute-start.2 = (s32[8,256]{1,0:T(8,128)S(1)}, s32[8,256]{1,0:T(8,128)S(1)}, u32[]{:S(2)}, u32[]{:S(2)}) collective-permute-start(s32[8,256]{1,0:T(8,128)S(1)} %reshape.17.own), channel_id=1, source_target_pairs={{0,2},{1,3},{2,0},{3,1},{4,6},{5,7},{6,4},{7,5},{8,10},{9,11},{10,... | collective-permute-start | bytes 24584 | tf_op jit(solution)/shard_map/ppermute | solution.py:388
  7.1 2.7 %collective-permute-start.1 = (s32[8,256]{1,0:T(8,128)S(1)}, s32[8,256]{1,0:T(8,128)S(1)}, u32[]{:S(2)}, u32[]{:S(2)}) collective-permute-start(s32[8,256]{1,0:T(8,128)S(1)} %reshape.17.own), channel_id=1, source_target_pairs={{0,1},{1,0},{2,3},{3,2},{4,5},{5,4},{6,7},{7,6},{8,9},{9,8},{10,11... | collective-permute-start | bytes 24584 | tf_op jit(solution)/shard_map/ppermute | solution.py:388
  9.8 1.5 %collective-permute-start.5 = (bf16[2,200,200]{2,1,0:T(8,128)(2,1)S(1)}, bf16[2,200,200]{2,1,0:T(8,128)(2,1)S(1)}, u32[]{:S(2)}, u32[]{:S(2)}) collective-permute-start(bf16[2,200,200]{2,1,0:T(8,128)(2,1)S(1)} %collective-permute-done.a1), channel_id=1, source_target_pairs={{0,1},{1,0},{2,3},{3,2},{4,5},{5,4},{6,7},{7,6},{8,9},{9,8},{10,11... | collective-permute-start | bytes 480008 | tf_op jit(solution)/shard_map/ppermute | solution.py:388
  9.9 7.3 %collective-permute-start.4 = (bf16[2,200,200]{2,1,0:T(8,128)(2,1)S(1)}, bf16[2,200,200]{2,1,0:T(8,128)(2,1)S(1)}, u32[]{:S(2)}, u32[]{:S(2)}) collective-permute-start(bf16[2,200,200]{2,1,0:T(8,128)(2,1)S(1)} %collective-permute-done.a1), channel_id=1, source_target_pairs={{0,8},{1,5},{2,10},{3,7},{4,0},{5,13},{6,2},{7,15},{8,16},{9,1},{1... | collective-permute-start | bytes 480008 | tf_op jit(solution)/shard_map/ppermute | solution.py:399
  11.3 11.7 %collective-permute-start.8 = (bf16[200,512]{1,0:T(8,128)(2,1)S(1)}, bf16[200,512]{1,0:T(8,128)(2,1)S(1)}, u32[]{:S(2)}, u32[]{:S(2)}) collective-permute-start(bf16[200,512]{1,0:T(8,128)(2,1)S(1)} %fusion), channel_id=1, source_target_pairs={{0,28},{4,0},{8,4},{12,8},{16,12},{20,16},{24,20},{28,24},{1,29},{... | collective-permute-start | bytes 614408 | tf_op jit(solution)/shard_map/ppermute | solution.py:22
  17.2 3.3 %collective-permute-start.7 = (bf16[2,200,200]{2,1,0:T(8,128)(2,1)S(1)}, bf16[2,200,200]{2,1,0:T(8,128)(2,1)S(1)}, u32[]{:S(2)}, u32[]{:S(2)}) collective-permute-start(bf16[2,200,200]{2,1,0:T(8,128)(2,1)S(1)} %collective-permute-done.4.a2), channel_id=1, source_target_pairs={{0,1},{1,0},{2,3},{3,2},{4,5},{5,4},{6,7},{7,6},{8,9},{9,8},{10,11... | collective-permute-start | bytes 480008 | tf_op jit(solution)/shard_map/ppermute | solution.py:388
  17.2 5.8 %collective-permute-start.6 = (bf16[2,200,200]{2,1,0:T(8,128)(2,1)S(1)}, bf16[2,200,200]{2,1,0:T(8,128)(2,1)S(1)}, u32[]{:S(2)}, u32[]{:S(2)}) collective-permute-start(bf16[2,200,200]{2,1,0:T(8,128)(2,1)S(1)} %collective-permute-done.4.a2), channel_id=1, source_target_pairs={{0,8},{1,5},{2,10},{3,7},{4,0},{5,13},{6,2},{7,15},{8,16},{9,1},{1... | collective-permute-start | bytes 480008 | tf_op jit(solution)/shard_map/ppermute | solution.py:399
  23.0 4.7 %collective-permute-start.9 = (bf16[1,200,200]{2,1,0:T(8,128)(2,1)S(1)}, bf16[1,200,200]{2,1,0:T(8,128)(2,1)S(1)}, u32[]{:S(2)}, u32[]{:S(2)}) collective-permute-start(bf16[1,200,200]{2,1,0:T(8,128)(2,1)S(1)} %constant_dynamic-slice_fusion), channel_id=1, source_target_pairs={{0,8},{1,5},{2,10},{3,7},{4,0},{5,13},{6,2},{7,15},{8,16},{9,1},{1... | collective-permute-start | bytes 240008 | tf_op jit(solution)/shard_map/ppermute | solution.py:399
  24.3 5.0 %collective-permute-start.12 = (bf16[200,512]{1,0:T(8,128)(2,1)S(1)}, bf16[200,512]{1,0:T(8,128)(2,1)S(1)}, u32[]{:S(2)}, u32[]{:S(2)}) collective-permute-start(bf16[200,512]{1,0:T(8,128)(2,1)S(1)} %collective-permute-done.8.mine), channel_id=1, source_target_pairs={{0,1},{1,0},{2,3},{3,2},{4,5},{5,4},{6,7},{7,6},{8,9},{9,8},{10,11... | collective-permute-start | bytes 614408 | tf_op jit(solution)/shard_map/ppermute | solution.py:388
  27.7 1.6 %collective-permute-start.11 = (bf16[2,200,200]{2,1,0:T(8,128)(2,1)S(1)}, bf16[2,200,200]{2,1,0:T(8,128)(2,1)S(1)}, u32[]{:S(2)}, u32[]{:S(2)}) collective-permute-start(bf16[2,200,200]{2,1,0:T(8,128)(2,1)S(1)} %collective-permute-done.6.a3), channel_id=1, source_target_pairs={{0,1},{1,0},{2,3},{3,2},{4,5},{5,4},{6,7},{7,6},{8,9},{9,8},{10,11... | collective-permute-start | bytes 480008 | tf_op jit(solution)/shard_map/ppermute | solution.py:388
  27.7 1.6 %collective-permute-start.10 = (bf16[1,200,200]{2,1,0:T(8,128)(2,1)S(1)}, bf16[1,200,200]{2,1,0:T(8,128)(2,1)S(1)}, u32[]{:S(2)}, u32[]{:S(2)}) collective-permute-start(bf16[1,200,200]{2,1,0:T(8,128)(2,1)S(1)} %collective-permute-done.9.a4), channel_id=1, source_target_pairs={{0,1},{1,0},{2,3},{3,2},{4,5},{5,4},{6,7},{7,6},{8,9},{9,8},{10,11... | collective-permute-start | bytes 240008 | tf_op jit(solution)/shard_map/ppermute | solution.py:388
  33.5 13.0 %collective-permute-start.13 = (bf16[320,128]{1,0:T(8,128)(2,1)S(1)}, bf16[320,128]{1,0:T(8,128)(2,1)S(1)}, u32[]{:S(2)}, u32[]{:S(2)}) collective-permute-start(bf16[320,128]{1,0:T(8,128)(2,1)S(1)} %get-tuple-element.68), channel_id=1, source_target_pairs={{0,0},{1,1},{2,30},{3,31},{4,4},{5,5},{6,26},{7,27},{8,8},{9,9},{1... | collective-permute-start | bytes 245768 | tf_op jit(solution)/shard_map/ppermute | solution.py:399
  34.2 12.3 %collective-permute-start.14 = (bf16[320,128]{1,0:T(8,128)(2,1)S(1)}, bf16[320,128]{1,0:T(8,128)(2,1)S(1)}, u32[]{:S(2)}, u32[]{:S(2)}) collective-permute-start(bf16[320,128]{1,0:T(8,128)(2,1)S(1)} %get-tuple-element.69), channel_id=1, source_target_pairs={{0,20},{1,25},{2,6},{3,11},{4,28},{5,17},{6,14},{7,3},{8,12},{9,29... | collective-permute-start | bytes 245768 | tf_op jit(solution)/shard_map/ppermute | solution.py:399
  36.7 9.8 %collective-permute-start.15 = (bf16[320,128]{1,0:T(8,128)(2,1)S(1)}, bf16[320,128]{1,0:T(8,128)(2,1)S(1)}, u32[]{:S(2)}, u32[]{:S(2)}) collective-permute-start(bf16[320,128]{1,0:T(8,128)(2,1)S(1)} %get-tuple-element.70), channel_id=1, source_target_pairs={{0,24},{1,21},{2,10},{3,7},{4,16},{5,29},{6,2},{7,15},{8,28},{9,13... | collective-permute-start | bytes 245768 | tf_op jit(solution)/shard_map/ppermute | solution.py:399
  38.0 8.4 %collective-permute-start.16 = (bf16[320,128]{1,0:T(8,128)(2,1)S(1)}, bf16[320,128]{1,0:T(8,128)(2,1)S(1)}, u32[]{:S(2)}, u32[]{:S(2)}) collective-permute-start(bf16[320,128]{1,0:T(8,128)(2,1)S(1)} %get-tuple-element.71), channel_id=1, source_target_pairs={{0,12},{1,17},{2,18},{3,15},{4,20},{5,9},{6,10},{7,23},{8,4},{9,25... | collective-permute-start | bytes 245768 | tf_op jit(solution)/shard_map/ppermute | solution.py:399
  40.7 13.1 %copy-start.1 = (f32[2,200,200]{2,1,0:T(8,128)S(1)}, f32[2,200,200]{2,1,0:T(8,128)}, u32[]{:S(2)}) copy-start(f32[2,200,200]{2,1,0:T(8,128)} %operators.1) | copy-start | bytes 960004
  40.7 14.3 %copy-start = (f32[1024,200]{0,1:T(8,128)S(1)}, f32[1024,200]{0,1:T(8,128)}, u32[]{:S(2)}) copy-start(f32[1024,200]{0,1:T(8,128)} %param.8) | copy-start | bytes 2457604
  40.7 14.3 %copy-start.3 = (f32[1024]{0:T(1024)S(1)}, f32[1024]{0:T(1024)}, u32[]{:S(2)}) copy-start(f32[1024]{0:T(1024)} %param.9) | copy-start | bytes 12292
  40.7 10.8 %collective-permute-start.17 = (bf16[200,512]{1,0:T(8,128)(2,1)S(1)}, bf16[200,512]{1,0:T(8,128)(2,1)S(1)}, u32[]{:S(2)}, u32[]{:S(2)}) collective-permute-start(bf16[200,512]{1,0:T(8,128)(2,1)S(1)} %targets.1), channel_id=1, source_target_pairs={{0,4},{4,8},{8,12},{12,16},{16,20},{20,24},{24,28},{28,0},{1,5},{5... | collective-permute-start | bytes 614408 | tf_op jit(solution)/shard_map/ppermute | solution.py:22
  46.5 5.8 %collective-permute-start.19 = (bf16[320,128]{1,0:T(8,128)(2,1)S(1)}, bf16[320,128]{1,0:T(8,128)(2,1)S(1)}, u32[]{:S(2)}, u32[]{:S(2)}) collective-permute-start(bf16[320,128]{1,0:T(8,128)(2,1)S(1)} %add_convert_fusion), channel_id=1, source_target_pairs={{0,2},{1,3},{2,0},{3,1},{4,6},{5,7},{6,4},{7,5},{8,10},{9,11},{10,... | collective-permute-start | bytes 245768 | tf_op jit(solution)/shard_map/ppermute | solution.py:388
  51.5 3.6 %collective-permute-start.18 = (bf16[200,512]{1,0:T(8,128)(2,1)S(1)}, bf16[200,512]{1,0:T(8,128)(2,1)S(1)}, u32[]{:S(2)}, u32[]{:S(2)}) collective-permute-start(bf16[200,512]{1,0:T(8,128)(2,1)S(1)} %collective-permute-done.17.mine), channel_id=1, source_target_pairs={{0,1},{1,0},{2,3},{3,2},{4,5},{5,4},{6,7},{7,6},{8,9},{9,8},{10,11... | collective-permute-start | bytes 614408 | tf_op jit(solution)/shard_map/ppermute | solution.py:388
  52.4 1.5 %collective-permute-start.20 = (f32[320,128]{1,0:T(8,128)S(1)}, f32[320,128]{1,0:T(8,128)S(1)}, u32[]{:S(2)}, u32[]{:S(2)}) collective-permute-start(f32[320,128]{1,0:T(8,128)S(1)} %convert_add_fusion.own), channel_id=1, source_target_pairs={{0,1},{1,0},{2,3},{3,2},{4,5},{5,4},{6,7},{7,6},{8,9},{9,8},{10,11... | collective-permute-start | bytes 491528 | tf_op jit(solution)/shard_map/ppermute | solution.py:388
  (1 other events, 13.1 us)

commit v5 on v4

--- a/solution.py
+++ b/solution.py
@@ -444,14 +444,13 @@
     mine = passed_along(own_half, "ent", -1)
     a2, b1, late_table = lax.optimization_barrier((a2, b1, table))
     a3 = ring_step(a2)
+    a4 = along_ring(lax.dynamic_slice_in_dim(a2, core, 1, 0), lambda r: -2)
     b2 = rep_swapped(a2, 1)
     table_half = late_table.astype(bf16)
     slots = call(slot_kernel, slot_out, "slots", 10**8, 10**6, (ids, *others, table_half))
-    a3, b2, mine, *slots = lax.optimization_barrier((a3, b2, mine, *slots))
+    a3, a4, b2, mine, *slots = lax.optimization_barrier((a3, a4, b2, mine, *slots))
     slotted, rows, counts = slots
-    a4 = ring_step(lax.dynamic_slice_in_dim(a3, core, 1, 0))
     other = rep_swapped(mine, 1)
-    a4, a3 = lax.optimization_barrier((a4, a3))
     b3 = rep_swapped(a3, 1)
     b4 = rep_swapped(a4, 1)
     gathered = (operators_half, a1, a2, a3, a4, b4, b3, b2, b1)

time: 56.5 us -> 54.3 us (0.961)
  waiting for transfers between devices: 14.5 us -> 10.4 us
  starting transfers between devices: 23.1 us -> 25.1 us
    ppermute x8, waiting for transfers between devices: 8.22 us -> 4.47 us  [along_ring(): return lax.ppermute(array, ('ent', 'rep'), pairs)]
    ppermute x2, waiting for transfers between devices: 1.58 us -> 0.01 us  [passed_along(): lax.ppermute(array, axis, [(i, (i + by) % peers) for i in range(peers)])]
    ppermute x11, starting transfers between devices: 5.94 us -> 7.45 us  [rep_swapped(): return lax.ppermute(array, 'rep', [(i, i ^ by) for i in range(peers)])]
    ppermute x11, waiting for transfers between devices: 4.7 us -> 5.95 us  [rep_swapped(): return lax.ppermute(array, 'rep', [(i, i ^ by) for i in range(peers)])]
    ppermute x8, starting transfers between devices: 10.9 us -> 11.6 us  [along_ring(): return lax.ppermute(array, ('ent', 'rep'), pairs)]
  transfers between devices with their start and end apart: 21 -> 21, of which waited for: 9 -> 8; matrix products, arithmetic and copies ran while one was open for 6% -> 6% of each run, Pallas kernels for 15% -> 15%
where the time goes in v5:
time: 54.3 us; the launch traced here: 54.1 us
  starting transfers between devices  25.1 us (46%)
  Pallas kernels  13.6 us (25%)
  waiting for transfers between devices  10.4 us (19%)
  other arithmetic  2.29 us (4%)
  local copies, waits for them, and re-layouts  1.88 us (3%)
  between operations  0.78 us (1%)
    pallas_call x6, Pallas kernels, call(): pl.pallas_call(body, out_shape=outs, in_specs=[whole] * len(operands), ou...  13.6 us
    ppermute x8, starting transfers between devices, along_ring(): return lax.ppermute(array, ('ent', 'rep'), pairs)  11.6 us
    ppermute x11, starting transfers between devices, rep_swapped(): return lax.ppermute(array, 'rep', [(i, i ^ by) for i in range(peers)])  7.45 us
    ppermute x2, starting transfers between devices, passed_along(): lax.ppermute(array, axis, [(i, (i + by) % peers) for i in range(peers)])  6.04 us
    ppermute x11, waiting for transfers between devices, rep_swapped(): return lax.ppermute(array, 'rep', [(i, i ^ by) for i in range(peers)])  5.95 us
    ppermute x8, waiting for transfers between devices, along_ring(): return lax.ppermute(array, ('ent', 'rep'), pairs)  4.47 us
    convert_element_type x1, other arithmetic, gathered_shards(): table_half = late_table.astype(bf16)  1.2 us
  transfers between devices with their start and end apart: 21, of which 8 were waited for; matrix products, arithmetic and copies ran while one was open for 6% of the time, Pallas kernels for 15%

profile of v5, /device:TPU:0, one launch (start us, length us, event | category | flops | bytes accessed | tf_op | source)
XLA Modules:
  0.0 54.1 jit_solution(15959069574248507324)
XLA Ops:
  0.6 1.0 %convert_element_type.33.o0 = bf16[2,200,200]{2,1,0:T(8,128)(2,1)S(1)} convert(f32[2,200,200]{2,1,0:T(8,128)} %operators.1) | non-fusion elementwise | flops 80000 | bytes 480000 | tf_op jit(solution)/shard_map/convert_element_type | solution.py:420
  1.7 3.1 %collective-permute-start = (bf16[2,200,200]{2,1,0:T(8,128)(2,1)S(1)}, bf16[2,200,200]{2,1,0:T(8,128)(2,1)S(1)}, u32[]{:S(2)}, u32[]{:S(2)}) collective-permute-start(bf16[2,200,200]{2,1,0:T(8,128)(2,1)S(1)} %convert_element_type.33.o0), channel_id=1, source_target_pairs={{0,8},{1,5},{2,10},{3,7},{4,0},{5,13},{6,2},{7,15},{8,16},{9,1},{1... | collective-permute-start | bytes 480008 | tf_op jit(solution)/shard_map/ppermute | solution.py:399
  6.1 1.0 %collective-permute-start.2 = (s32[8,256]{1,0:T(8,128)S(1)}, s32[8,256]{1,0:T(8,128)S(1)}, u32[]{:S(2)}, u32[]{:S(2)}) collective-permute-start(s32[8,256]{1,0:T(8,128)S(1)} %reshape.17.own), channel_id=1, source_target_pairs={{0,2},{1,3},{2,0},{3,1},{4,6},{5,7},{6,4},{7,5},{8,10},{9,11},{10,... | collective-permute-start | bytes 24584 | tf_op jit(solution)/shard_map/ppermute | solution.py:388
  7.4 1.0 %fusion = bf16[200,512]{1,0:T(8,128)(2,1)S(1)} fusion(f32[1024,200]{0,1:T(8,128)} %param.8, s32[]{:T(128)S(6)} %select_n.14), kind=kLoop, calls=%fused_computation.1 | loop fusion | bytes 409604 | tf_op jit(solution)/shard_map/convert_element_type | solution.py:439
  8.6 1.2 %collective-permute-done.2.far = s32[8,256]{1,0:T(8,128)S(1)} collective-permute-done((s32[8,256]{1,0:T(8,128)S(1)}, s32[8,256]{1,0:T(8,128)S(1)}, u32[]{:S(2)}, u32[]{:S(2)}) %collective-permute-start.2) | collective-permute-done | bytes 8224 | tf_op jit(solution)/shard_map/ppermute | solution.py:388
  9.9 1.3 %collective-permute-start.4 = (bf16[2,200,200]{2,1,0:T(8,128)(2,1)S(1)}, bf16[2,200,200]{2,1,0:T(8,128)(2,1)S(1)}, u32[]{:S(2)}, u32[]{:S(2)}) collective-permute-start(bf16[2,200,200]{2,1,0:T(8,128)(2,1)S(1)} %collective-permute-done.a1), channel_id=1, source_target_pairs={{0,8},{1,5},{2,10},{3,7},{4,0},{5,13},{6,2},{7,15},{8,16},{9,1},{1... | collective-permute-start | bytes 480008 | tf_op jit(solution)/shard_map/ppermute | solution.py:399
  11.3 3.7 %collective-permute-start.9 = (bf16[200,512]{1,0:T(8,128)(2,1)S(1)}, bf16[200,512]{1,0:T(8,128)(2,1)S(1)}, u32[]{:S(2)}, u32[]{:S(2)}) collective-permute-start(bf16[200,512]{1,0:T(8,128)(2,1)S(1)} %fusion), channel_id=1, source_target_pairs={{0,28},{4,0},{8,4},{12,8},{16,12},{20,16},{24,20},{28,24},{1,29},{... | collective-permute-start | bytes 614408 | tf_op jit(solution)/shard_map/ppermute | solution.py:22
  14.9 2.3 %collective-permute-done.4.a2 = bf16[2,200,200]{2,1,0:T(8,128)(2,1)S(1)} collective-permute-done((bf16[2,200,200]{2,1,0:T(8,128)(2,1)S(1)}, bf16[2,200,200]{2,1,0:T(8,128)(2,1)S(1)}, u32[]{:S(2)}, u32[]{:S(2)}) %collective-permute-start.4) | collective-permute-done | bytes 160032 | tf_op jit(solution)/shard_map/ppermute | solution.py:399
  17.2 2.4 %collective-permute-start.7 = (bf16[1,200,200]{2,1,0:T(8,128)(2,1)S(1)}, bf16[1,200,200]{2,1,0:T(8,128)(2,1)S(1)}, u32[]{:S(2)}, u32[]{:S(2)}) collective-permute-start(bf16[1,200,200]{2,1,0:T(8,128)(2,1)S(1)} %constant_dynamic-slice_fusion), channel_id=1, source_target_pairs={{0,16},{1,13},{2,18},{3,15},{4,8},{5,21},{6,10},{7,23},{8,24},{9,5... | collective-permute-start | bytes 240008 | tf_op jit(solution)/shard_map/ppermute | solution.py:399
  19.6 1.2 %convert_element_type.36.table = bf16[200,1024]{1,0:T(8,128)(2,1)S(1)} convert(f32[200,1024]{1,0:T(8,128)} %bitcast.8) | non-fusion elementwise | flops 204800 | bytes 1228800 | tf_op jit(solution)/shard_map/convert_element_type | solution.py:449
  20.8 2.0 %slots.1 = (bf16[4,16,32,200]{3,2,1,0:T(8,128)(2,1)S(1)}, f32[4,8,256]{2,1,0:T(8,128)S(1)}, f32[4,1,1024]{2,1,0:T(1,128)S(1)}) custom-call(s32[8,256]{1,0:T(8,128)S(1)} %reshape.17.own, s32[8,256]{1,0:T(8,128)S(1)} %collective-permute-done.1.near, s32[8,256]{1,0:T(8,128)S(1)} %collective-permute-done.2.far, s32[8,256]{1,0:T(8,128)S(1)} %collective-permute-done.3.across, ...), custom_call_target="tpu_custom_call" | custom-call | flops 100000000 | bytes 1000000 | tf_op jit(solution)/shard_map/slots/pallas_call | solution.py:166
  22.9 1.8 %collective-permute-done.7.a4 = bf16[1,200,200]{2,1,0:T(8,128)(2,1)S(1)} collective-permute-done((bf16[1,200,200]{2,1,0:T(8,128)(2,1)S(1)}, bf16[1,200,200]{2,1,0:T(8,128)(2,1)S(1)}, u32[]{:S(2)}, u32[]{:S(2)}) %collective-permute-start.7) | collective-permute-done | bytes 80032 | tf_op jit(solution)/shard_map/ppermute | solution.py:399
  25.3 1.3 %collective-permute-done.10.b4 = bf16[1,200,200]{2,1,0:T(8,128)(2,1)S(1)} collective-permute-done((bf16[1,200,200]{2,1,0:T(8,128)(2,1)S(1)}, bf16[1,200,200]{2,1,0:T(8,128)(2,1)S(1)}, u32[]{:S(2)}, u32[]{:S(2)}) %collective-permute-start.10) | collective-permute-done | bytes 80032 | tf_op jit(solution)/shard_map/ppermute | solution.py:388
  26.6 4.1 %scores.1 = (bf16[320,128]{1,0:T(8,128)(2,1)S(1)}, bf16[320,128]{1,0:T(8,128)(2,1)S(1)}, bf16[320,128]{1,0:T(8,128)(2,1)S(1)}, bf16[320,128]{1,0:T(8,128)(2,1)S(...) custom-call(bf16[2,200,200]{2,1,0:T(8,128)(2,1)S(1)} %convert_element_type, ...), custom_call_target="tpu_custom_call" | custom-call | flops 1000000000 | bytes 1000000 | tf_op jit(solution)/shard_map/scores/pallas_call | solution.py:166
  31.5 1.9 %collective-permute-start.14 = (bf16[320,128]{1,0:T(8,128)(2,1)S(1)}, bf16[320,128]{1,0:T(8,128)(2,1)S(1)}, u32[]{:S(2)}, u32[]{:S(2)}) collective-permute-start(bf16[320,128]{1,0:T(8,128)(2,1)S(1)} %get-tuple-element.67), channel_id=1, source_target_pairs={{0,20},{1,25},{2,6},{3,11},{4,28},{5,17},{6,14},{7,3},{8,12},{9,29... | collective-permute-start | bytes 245768 | tf_op jit(solution)/shard_map/ppermute | solution.py:399
  33.3 2.0 %collective-permute-start.15 = (bf16[320,128]{1,0:T(8,128)(2,1)S(1)}, bf16[320,128]{1,0:T(8,128)(2,1)S(1)}, u32[]{:S(2)}, u32[]{:S(2)}) collective-permute-start(bf16[320,128]{1,0:T(8,128)(2,1)S(1)} %get-tuple-element.68), channel_id=1, source_target_pairs={{0,24},{1,21},{2,10},{3,7},{4,16},{5,29},{6,2},{7,15},{8,28},{9,13... | collective-permute-start | bytes 245768 | tf_op jit(solution)/shard_map/ppermute | solution.py:399
  35.6 2.0 %targets.1 = bf16[200,512]{1,0:T(8,128)(2,1)S(1)} custom-call(f32[4,8,256]{2,1,0:T(8,128)S(1)} %get-tuple-element.58.rows, bf16[4,256,1024]{2,1,0:T(8,128)(2,1)S(1)} %get-tuple-element.63.weights, bf16[4,768,200]{2,1,0:T(8,128)(2,1)S(1)} %get-tuple-element.64.sides), custom_call_target="tpu_custom_call" | custom-call | flops 100000000 | bytes 1000000 | tf_op jit(solution)/shard_map/targets/pallas_call | solution.py:166
  37.6 2.4 %collective-permute-start.17 = (bf16[200,512]{1,0:T(8,128)(2,1)S(1)}, bf16[200,512]{1,0:T(8,128)(2,1)S(1)}, u32[]{:S(2)}, u32[]{:S(2)}) collective-permute-start(bf16[200,512]{1,0:T(8,128)(2,1)S(1)} %targets.1), channel_id=1, source_target_pairs={{0,4},{4,8},{8,12},{12,16},{16,20},{20,24},{24,28},{28,0},{1,5},{5... | collective-permute-start | bytes 614408 | tf_op jit(solution)/shard_map/ppermute | solution.py:22
  40.0 3.1 %sources.1.source_total = f32[200,1024]{1,0:T(8,128)S(1)} custom-call(bf16[2,200,200]{2,1,0:T(8,128)(2,1)S(1)} %convert_element_type.33.o0, bf16[2,200,200]{2,1,0:T(8,128)(2,1)S(1)} %collective-permute-done.a1, bf16[2,200,200]{2,1,0:T(8,128)(2,1)S(1)} %collective-permute-done.4.a2, bf16[2,200,200]{2,1,0:T(8,128)(2,1)S(1)} %collective-permute-done.6.a3, ...), custom_call_target="tpu_custom_call" | custom-call | flops 100000000 | bytes 1000000 | tf_op jit(solution)/shard_map/sources/pallas_call | solution.py:166
  43.6 4.2 %collective-permute-start.19 = (bf16[320,128]{1,0:T(8,128)(2,1)S(1)}, bf16[320,128]{1,0:T(8,128)(2,1)S(1)}, u32[]{:S(2)}, u32[]{:S(2)}) collective-permute-start(bf16[320,128]{1,0:T(8,128)(2,1)S(1)} %add_convert_fusion), channel_id=1, source_target_pairs={{0,2},{1,3},{2,0},{3,1},{4,6},{5,7},{6,4},{7,5},{8,10},{9,11},{10,... | collective-permute-start | bytes 245768 | tf_op jit(solution)/shard_map/ppermute | solution.py:388
  48.3 1.9 %collective-permute-done.19 = bf16[320,128]{1,0:T(8,128)(2,1)S(1)} collective-permute-done((bf16[320,128]{1,0:T(8,128)(2,1)S(1)}, bf16[320,128]{1,0:T(8,128)(2,1)S(1)}, u32[]{:S(2)}, u32[]{:S(2)}) %collective-permute-start.19) | collective-permute-done | bytes 81952 | tf_op jit(solution)/shard_map/ppermute | solution.py:388
  50.3 1.4 %collective-permute-done.20.other = f32[320,128]{1,0:T(8,128)S(1)} collective-permute-done((f32[320,128]{1,0:T(8,128)S(1)}, f32[320,128]{1,0:T(8,128)S(1)}, u32[]{:S(2)}, u32[]{:S(2)}) %collective-permute-start.20) | collective-permute-done | bytes 163872 | tf_op jit(solution)/shard_map/ppermute | solution.py:388
  51.7 1.2 %operator_update.1 = (f32[2,200,200]{2,1,0:T(8,128)}, f32[2,200,200]{2,1,0:T(8,128)}) custom-call(f32[320,128]{1,0:T(8,128)S(1)} %convert_add_fusion.own, f32[320,128]{1,0:T(8,128)S(1)} %collective-permute-done.20.other, f32[2,200,200]{2,1,0:T(8,128)S(1)} %copy-done.1, f32[2,200,200]{2,1,0:T(8,128)S(1)} %copy-done.2), custom_call_target="tpu_custom_call" | custom-call | flops 1000000 | bytes 1000000 | tf_op jit(solution)/shard_map/operator_update/pallas_call | solution.py:166
  52.9 1.2 %entity_update.1 = (f32[200,1024]{1,0:T(8,128)}, f32[1,1024]{1,0:T(1,128)}) custom-call(f32[200,1024]{1,0:T(8,128)S(1)} %sources.1.source_total, bf16[200,512]{1,0:T(8,128)(2,1)S(1)} %collective-permute-done.17.mine, bf16[200,512]{1,0:T(8,128)(2,1)S(1)} %collective-permute-done.18.other, f32[200,1024]{1,0:T(8,128)S(1)} %bitcast.9, f32[1,1024]{1,0:T(1,128)S(1)} %bitcast.10), custom_call_target="tpu_custom_call" | custom-call | flops 1000000 | bytes 1000000 | tf_op jit(solution)/shard_map/entity_update/pallas_call | solution.py:166
  (41 shorter events, 4.7 us)
Async XLA Ops:
  1.7 8.2 %collective-permute-start = (bf16[2,200,200]{2,1,0:T(8,128)(2,1)S(1)}, bf16[2,200,200]{2,1,0:T(8,128)(2,1)S(1)}, u32[]{:S(2)}, u32[]{:S(2)}) collective-permute-start(bf16[2,200,200]{2,1,0:T(8,128)(2,1)S(1)} %convert_element_type.33.o0), channel_id=1, source_target_pairs={{0,8},{1,5},{2,10},{3,7},{4,0},{5,13},{6,2},{7,15},{8,16},{9,1},{1... | collective-permute-start | bytes 480008 | tf_op jit(solution)/shard_map/ppermute | solution.py:399
  5.6 3.1 %collective-permute-start.3 = (s32[8,256]{1,0:T(8,128)S(1)}, s32[8,256]{1,0:T(8,128)S(1)}, u32[]{:S(2)}, u32[]{:S(2)}) collective-permute-start(s32[8,256]{1,0:T(8,128)S(1)} %reshape.17.own), channel_id=1, source_target_pairs={{0,3},{1,2},{2,1},{3,0},{4,7},{5,6},{6,5},{7,4},{8,11},{9,10},{10,... | collective-permute-start | bytes 24584 | tf_op jit(solution)/shard_map/ppermute | solution.py:388
  6.1 3.7 %collective-permute-start.2 = (s32[8,256]{1,0:T(8,128)S(1)}, s32[8,256]{1,0:T(8,128)S(1)}, u32[]{:S(2)}, u32[]{:S(2)}) collective-permute-start(s32[8,256]{1,0:T(8,128)S(1)} %reshape.17.own), channel_id=1, source_target_pairs={{0,2},{1,3},{2,0},{3,1},{4,6},{5,7},{6,4},{7,5},{8,10},{9,11},{10,... | collective-permute-start | bytes 24584 | tf_op jit(solution)/shard_map/ppermute | solution.py:388
  7.1 2.7 %collective-permute-start.1 = (s32[8,256]{1,0:T(8,128)S(1)}, s32[8,256]{1,0:T(8,128)S(1)}, u32[]{:S(2)}, u32[]{:S(2)}) collective-permute-start(s32[8,256]{1,0:T(8,128)S(1)} %reshape.17.own), channel_id=1, source_target_pairs={{0,1},{1,0},{2,3},{3,2},{4,5},{5,4},{6,7},{7,6},{8,9},{9,8},{10,11... | collective-permute-start | bytes 24584 | tf_op jit(solution)/shard_map/ppermute | solution.py:388
  9.8 1.5 %collective-permute-start.5 = (bf16[2,200,200]{2,1,0:T(8,128)(2,1)S(1)}, bf16[2,200,200]{2,1,0:T(8,128)(2,1)S(1)}, u32[]{:S(2)}, u32[]{:S(2)}) collective-permute-start(bf16[2,200,200]{2,1,0:T(8,128)(2,1)S(1)} %collective-permute-done.a1), channel_id=1, source_target_pairs={{0,1},{1,0},{2,3},{3,2},{4,5},{5,4},{6,7},{7,6},{8,9},{9,8},{10,11... | collective-permute-start | bytes 480008 | tf_op jit(solution)/shard_map/ppermute | solution.py:388
  9.9 7.3 %collective-permute-start.4 = (bf16[2,200,200]{2,1,0:T(8,128)(2,1)S(1)}, bf16[2,200,200]{2,1,0:T(8,128)(2,1)S(1)}, u32[]{:S(2)}, u32[]{:S(2)}) collective-permute-start(bf16[2,200,200]{2,1,0:T(8,128)(2,1)S(1)} %collective-permute-done.a1), channel_id=1, source_target_pairs={{0,8},{1,5},{2,10},{3,7},{4,0},{5,13},{6,2},{7,15},{8,16},{9,1},{1... | collective-permute-start | bytes 480008 | tf_op jit(solution)/shard_map/ppermute | solution.py:399
  11.3 13.4 %collective-permute-start.9 = (bf16[200,512]{1,0:T(8,128)(2,1)S(1)}, bf16[200,512]{1,0:T(8,128)(2,1)S(1)}, u32[]{:S(2)}, u32[]{:S(2)}) collective-permute-start(bf16[200,512]{1,0:T(8,128)(2,1)S(1)} %fusion), channel_id=1, source_target_pairs={{0,28},{4,0},{8,4},{12,8},{16,12},{20,16},{24,20},{28,24},{1,29},{... | collective-permute-start | bytes 614408 | tf_op jit(solution)/shard_map/ppermute | solution.py:22
  17.2 7.4 %collective-permute-start.8 = (bf16[2,200,200]{2,1,0:T(8,128)(2,1)S(1)}, bf16[2,200,200]{2,1,0:T(8,128)(2,1)S(1)}, u32[]{:S(2)}, u32[]{:S(2)}) collective-permute-start(bf16[2,200,200]{2,1,0:T(8,128)(2,1)S(1)} %collective-permute-done.4.a2), channel_id=1, source_target_pairs={{0,1},{1,0},{2,3},{3,2},{4,5},{5,4},{6,7},{7,6},{8,9},{9,8},{10,11... | collective-permute-start | bytes 480008 | tf_op jit(solution)/shard_map/ppermute | solution.py:388
  17.2 7.4 %collective-permute-start.6 = (bf16[2,200,200]{2,1,0:T(8,128)(2,1)S(1)}, bf16[2,200,200]{2,1,0:T(8,128)(2,1)S(1)}, u32[]{:S(2)}, u32[]{:S(2)}) collective-permute-start(bf16[2,200,200]{2,1,0:T(8,128)(2,1)S(1)} %collective-permute-done.4.a2), channel_id=1, source_target_pairs={{0,8},{1,5},{2,10},{3,7},{4,0},{5,13},{6,2},{7,15},{8,16},{9,1},{1... | collective-permute-start | bytes 480008 | tf_op jit(solution)/shard_map/ppermute | solution.py:399
  17.2 7.4 %collective-permute-start.7 = (bf16[1,200,200]{2,1,0:T(8,128)(2,1)S(1)}, bf16[1,200,200]{2,1,0:T(8,128)(2,1)S(1)}, u32[]{:S(2)}, u32[]{:S(2)}) collective-permute-start(bf16[1,200,200]{2,1,0:T(8,128)(2,1)S(1)} %constant_dynamic-slice_fusion), channel_id=1, source_target_pairs={{0,16},{1,13},{2,18},{3,15},{4,8},{5,21},{6,10},{7,23},{8,24},{9,5... | collective-permute-start | bytes 240008 | tf_op jit(solution)/shard_map/ppermute | solution.py:399
  24.7 2.0 %collective-permute-start.12 = (bf16[200,512]{1,0:T(8,128)(2,1)S(1)}, bf16[200,512]{1,0:T(8,128)(2,1)S(1)}, u32[]{:S(2)}, u32[]{:S(2)}) collective-permute-start(bf16[200,512]{1,0:T(8,128)(2,1)S(1)} %collective-permute-done.9.mine), channel_id=1, source_target_pairs={{0,1},{1,0},{2,3},{3,2},{4,5},{5,4},{6,7},{7,6},{8,9},{9,8},{10,11... | collective-permute-start | bytes 614408 | tf_op jit(solution)/shard_map/ppermute | solution.py:388
  24.7 1.9 %collective-permute-start.11 = (bf16[2,200,200]{2,1,0:T(8,128)(2,1)S(1)}, bf16[2,200,200]{2,1,0:T(8,128)(2,1)S(1)}, u32[]{:S(2)}, u32[]{:S(2)}) collective-permute-start(bf16[2,200,200]{2,1,0:T(8,128)(2,1)S(1)} %collective-permute-done.6.a3), channel_id=1, source_target_pairs={{0,1},{1,0},{2,3},{3,2},{4,5},{5,4},{6,7},{7,6},{8,9},{9,8},{10,11... | collective-permute-start | bytes 480008 | tf_op jit(solution)/shard_map/ppermute | solution.py:388
  25.2 1.4 %collective-permute-start.10 = (bf16[1,200,200]{2,1,0:T(8,128)(2,1)S(1)}, bf16[1,200,200]{2,1,0:T(8,128)(2,1)S(1)}, u32[]{:S(2)}, u32[]{:S(2)}) collective-permute-start(bf16[1,200,200]{2,1,0:T(8,128)(2,1)S(1)} %collective-permute-done.7.a4), channel_id=1, source_target_pairs={{0,1},{1,0},{2,3},{3,2},{4,5},{5,4},{6,7},{7,6},{8,9},{9,8},{10,11... | collective-permute-start | bytes 240008 | tf_op jit(solution)/shard_map/ppermute | solution.py:388
  30.8 12.3 %collective-permute-start.13 = (bf16[320,128]{1,0:T(8,128)(2,1)S(1)}, bf16[320,128]{1,0:T(8,128)(2,1)S(1)}, u32[]{:S(2)}, u32[]{:S(2)}) collective-permute-start(bf16[320,128]{1,0:T(8,128)(2,1)S(1)} %get-tuple-element.66), channel_id=1, source_target_pairs={{0,0},{1,1},{2,30},{3,31},{4,4},{5,5},{6,26},{7,27},{8,8},{9,9},{1... | collective-permute-start | bytes 245768 | tf_op jit(solution)/shard_map/ppermute | solution.py:399
  31.5 11.7 %collective-permute-start.14 = (bf16[320,128]{1,0:T(8,128)(2,1)S(1)}, bf16[320,128]{1,0:T(8,128)(2,1)S(1)}, u32[]{:S(2)}, u32[]{:S(2)}) collective-permute-start(bf16[320,128]{1,0:T(8,128)(2,1)S(1)} %get-tuple-element.67), channel_id=1, source_target_pairs={{0,20},{1,25},{2,6},{3,11},{4,28},{5,17},{6,14},{7,3},{8,12},{9,29... | collective-permute-start | bytes 245768 | tf_op jit(solution)/shard_map/ppermute | solution.py:399
  33.3 9.8 %collective-permute-start.15 = (bf16[320,128]{1,0:T(8,128)(2,1)S(1)}, bf16[320,128]{1,0:T(8,128)(2,1)S(1)}, u32[]{:S(2)}, u32[]{:S(2)}) collective-permute-start(bf16[320,128]{1,0:T(8,128)(2,1)S(1)} %get-tuple-element.68), channel_id=1, source_target_pairs={{0,24},{1,21},{2,10},{3,7},{4,16},{5,29},{6,2},{7,15},{8,28},{9,13... | collective-permute-start | bytes 245768 | tf_op jit(solution)/shard_map/ppermute | solution.py:399
  35.3 8.2 %collective-permute-start.16 = (bf16[320,128]{1,0:T(8,128)(2,1)S(1)}, bf16[320,128]{1,0:T(8,128)(2,1)S(1)}, u32[]{:S(2)}, u32[]{:S(2)}) collective-permute-start(bf16[320,128]{1,0:T(8,128)(2,1)S(1)} %get-tuple-element.69), channel_id=1, source_target_pairs={{0,12},{1,17},{2,18},{3,15},{4,20},{5,9},{6,10},{7,23},{8,4},{9,25... | collective-permute-start | bytes 245768 | tf_op jit(solution)/shard_map/ppermute | solution.py:399
  37.6 14.1 %copy-start.1 = (f32[2,200,200]{2,1,0:T(8,128)S(1)}, f32[2,200,200]{2,1,0:T(8,128)}, u32[]{:S(2)}) copy-start(f32[2,200,200]{2,1,0:T(8,128)} %operators.1) | copy-start | bytes 960004
  37.6 15.3 %copy-start = (f32[1024,200]{0,1:T(8,128)S(1)}, f32[1024,200]{0,1:T(8,128)}, u32[]{:S(2)}) copy-start(f32[1024,200]{0,1:T(8,128)} %param.8) | copy-start | bytes 2457604
  37.6 15.3 %copy-start.3 = (f32[1024]{0:T(1024)S(1)}, f32[1024]{0:T(1024)}, u32[]{:S(2)}) copy-start(f32[1024]{0:T(1024)} %param.9) | copy-start | bytes 12292
  37.6 10.2 %collective-permute-start.17 = (bf16[200,512]{1,0:T(8,128)(2,1)S(1)}, bf16[200,512]{1,0:T(8,128)(2,1)S(1)}, u32[]{:S(2)}, u32[]{:S(2)}) collective-permute-start(bf16[200,512]{1,0:T(8,128)(2,1)S(1)} %targets.1), channel_id=1, source_target_pairs={{0,4},{4,8},{8,12},{12,16},{16,20},{20,24},{24,28},{28,0},{1,5},{5... | collective-permute-start | bytes 614408 | tf_op jit(solution)/shard_map/ppermute | solution.py:22
  43.6 6.6 %collective-permute-start.19 = (bf16[320,128]{1,0:T(8,128)(2,1)S(1)}, bf16[320,128]{1,0:T(8,128)(2,1)S(1)}, u32[]{:S(2)}, u32[]{:S(2)}) collective-permute-start(bf16[320,128]{1,0:T(8,128)(2,1)S(1)} %add_convert_fusion), channel_id=1, source_target_pairs={{0,2},{1,3},{2,0},{3,1},{4,6},{5,7},{6,4},{7,5},{8,10},{9,11},{10,... | collective-permute-start | bytes 245768 | tf_op jit(solution)/shard_map/ppermute | solution.py:388
  47.8 5.1 %collective-permute-start.18 = (bf16[200,512]{1,0:T(8,128)(2,1)S(1)}, bf16[200,512]{1,0:T(8,128)(2,1)S(1)}, u32[]{:S(2)}, u32[]{:S(2)}) collective-permute-start(bf16[200,512]{1,0:T(8,128)(2,1)S(1)} %collective-permute-done.17.mine), channel_id=1, source_target_pairs={{0,1},{1,0},{2,3},{3,2},{4,5},{5,4},{6,7},{7,6},{8,9},{9,8},{10,11... | collective-permute-start | bytes 614408 | tf_op jit(solution)/shard_map/ppermute | solution.py:388
  50.2 1.5 %collective-permute-start.20 = (f32[320,128]{1,0:T(8,128)S(1)}, f32[320,128]{1,0:T(8,128)S(1)}, u32[]{:S(2)}, u32[]{:S(2)}) collective-permute-start(f32[320,128]{1,0:T(8,128)S(1)} %convert_add_fusion.own), channel_id=1, source_target_pairs={{0,1},{1,0},{2,3},{3,2},{4,5},{5,4},{6,7},{7,6},{8,9},{9,8},{10,11... | collective-permute-start | bytes 491528 | tf_op jit(solution)/shard_map/ppermute | solution.py:388
  (1 other events, 14.1 us)

commit v6 on v5

--- a/solution.py
+++ b/solution.py
@@ -239,20 +239,48 @@
         slotted[lax.bitwise_xor(me, m)] = given.reshape(places, SLOTS, -1)
 
 
+def join(table, mine, other):
+    half = mine.shape[1]
+    core, *_ = position()
+    table[:, pl.ds(pl.multiple_of(core * half, half), half)] = mine[...]
+    table[:, pl.ds(pl.multiple_of((1 - core) * half, half), half)] = other[...]
+
+
+LATE = (6, 12)
+
+
+def transform(moved, slotted, place, at, op):
+    reps, _, _, width = slotted.shape
+    given = slotted[:, place].reshape(reps * SLOTS, width)
+    moved[:, at] = dot(given, op).astype(bf16).reshape(reps, SLOTS, width)
+
+
+def ready_kernel(o0, a1, a2, b2, b1, slotted, rows, made_early, moved):
+    reps, _, edges = rows.shape
+    places, width = slotted.shape[1], slotted.shape[3]
+    moved[:, LATE[0] : LATE[1]] = jnp.zeros((reps, LATE[1] - LATE[0], SLOTS, width), bf16)
+    for place, op in enumerate(operator_list(o0, a1, a2, None, None, None, None, b2, b1)):
+        if op is not None:
+            transform(moved, slotted, place, place, op())
+    for b in range(reps):
+        slot = rows[b].T[:, 2:3].astype(jnp.int32)
+        out_of = one_hot(lanes_of((edges, places * SLOTS)) == slot)
+        made = dot(out_of, moved[b].reshape(places * SLOTS, width))
+        made_early[b * edges : (b + 1) * edges] = made.astype(bf16)
+
+
 def score_kernel(
-    negative_count, o0, a1, a2, a3, a4, b4, b3, b2, b1, slotted, rows, counts, mine, other,
+    negative_count, a3, a4, b4, b3, slotted, rows, counts, mine, other, made_early,
     s0, s1, s2, s3, weights, sides, query, table, moved, asking,
 ):
     core, me, *_ = position()
     reps, places = slotted.shape[:2]
     width, entities = table.shape
-    half = mine.shape[1]
     edges = rows.shape[2]
-    table[:, pl.ds(pl.multiple_of(core * half, half), half)] = mine[...]
-    table[:, pl.ds(pl.multiple_of((1 - core) * half, half), half)] = other[...]
-    for place, op in enumerate(operator_list(o0, a1, a2, a3, a4, b4, b3, b2, b1)):
-        given = slotted[:, place].reshape(reps * SLOTS, width)
-        moved[:, place] = dot(given, op()).astype(bf16).reshape(reps, SLOTS, width)
+    join(table, mine, other)
+    for place, op in enumerate(operator_list(None, None, None, a3, a4, b4, b3, None, None)):
+        if op is not None:
+            transform(moved, slotted, place, place - LATE[0], op())
     sent = (s0, s1, s2, s3)
     handed = []
     for near, far in OFFSETS:
@@ -262,9 +290,10 @@
     standing = [block.T.astype(jnp.int32) for block in lying]
     made = []
     for b in range(reps):
-        out_of = one_hot(lanes_of((edges, places * SLOTS)) == standing[b][:, 2:3])
-        made.append(dot(out_of, moved[b].reshape(places * SLOTS, width)))
-    made = jnp.concatenate(made, axis=0)
+        late = (LATE[1] - LATE[0]) * SLOTS
+        out_of = one_hot(lanes_of((edges, late)) + LATE[0] * SLOTS == standing[b][:, 2:3])
+        made.append(dot(out_of, moved[b].reshape(late, width)))
+    made = jnp.concatenate(made, axis=0) + made_early[...].astype(f32)
     made_half = made.astype(bf16)
     scores = dot(made_half, table[...])
     aimed = lanes_of((reps * edges, entities)) == jnp.concatenate(
@@ -324,7 +353,7 @@
     listed += [(a4, 0), (b4, 0)]
     for ref in (b3, b2, b1):
         listed += [(ref, 0), (ref, 1)]
-    return [lambda ref=ref, i=i: ref[i] for ref, i in listed]
+    return [None if ref is None else lambda ref=ref, i=i: ref[i] for ref, i in listed]
 
 
 def target_kernel(rows, weights, sides, target_half, total):
@@ -453,6 +482,12 @@
     other = rep_swapped(mine, 1)
     b3 = rep_swapped(a3, 1)
     b4 = rep_swapped(a4, 1)
+    (made_early,) = call(
+        ready_kernel,
+        [jax.ShapeDtypeStruct((reps * edges, width), bf16)],
+        "ready", 10**8, 10**6, (operators_half, a1, a2, b2, b1, slotted, rows),
+        scratch=[VMEM((reps, places, SLOTS, width), bf16)],
+    )
     gathered = (operators_half, a1, a2, a3, a4, b4, b3, b2, b1)
 
     score_out = [jax.ShapeDtypeStruct((width + SIDE + 16, LANES), bf16)] * len(OFFSETS) + [
@@ -462,10 +497,10 @@
     ]
     *handed, weights, sides, query = call(
         functools.partial(score_kernel, negatives.shape[1]), score_out, "scores", 10**9, 10**6,
-        (*gathered, slotted, rows, counts, mine, other),
+        (a3, a4, b4, b3, slotted, rows, counts, mine, other, made_early),
         scratch=[
             VMEM((width, entities), bf16),
-            VMEM((reps, places, SLOTS, width), bf16),
+            VMEM((reps, LATE[1] - LATE[0], SLOTS, width), bf16),
             VMEM((reps, len(OFFSETS), SLOTS, width), bf16),
         ],
     )
@@ -498,6 +533,9 @@
         "entity_update", 10**6, 10**6,
         (source_total, home_mine, home_other, table, entity_state.reshape(1, -1)),
     )
+    other_relation, new_table, new_state = lax.optimization_barrier(
+        (other_relation, new_table, new_state)
+    )
     new_operators, new_operator_state = call(
         operator_kernel,
         [jax.ShapeDtypeStruct(operators.shape, f32)] * 2,

time: 54.3 us -> 53.3 us (0.982)
  waiting for transfers between devices: 10.4 us -> 8.4 us
  Pallas kernels: 13.6 us -> 14.2 us
    ppermute x11, waiting for transfers between devices: 5.95 us -> 3.92 us  [rep_swapped(): return lax.ppermute(array, 'rep', [(i, i ^ by) for i in range(peers)])]
    pallas_call x6 -> x7, Pallas kernels: 13.6 us -> 14.2 us  [call(): pl.pallas_call(body, out_shape=outs, in_specs=[whole] * len(operands), ou...]
  transfers between devices with their start and end apart: 21 -> 21, of which waited for: 8 -> 8; matrix products, arithmetic and copies ran while one was open for 6% -> 6% of each run, Pallas kernels for 15% -> 17%
where the time goes in v6:
time: 53.3 us; the launch traced here: 52.7 us
  starting transfers between devices  25 us (47%)
  Pallas kernels  14.2 us (27%)
  waiting for transfers between devices  8.4 us (16%)
  other arithmetic  2.29 us (4%)
  local copies, waits for them, and re-layouts  1.88 us (4%)
  between operations  0.81 us (2%)
    pallas_call x7, Pallas kernels, call(): pl.pallas_call(body, out_shape=outs, in_specs=[whole] * len(operands), ou...  14.2 us
    ppermute x8, starting transfers between devices, along_ring(): return lax.ppermute(array, ('ent', 'rep'), pairs)  11.6 us
    ppermute x11, starting transfers between devices, rep_swapped(): return lax.ppermute(array, 'rep', [(i, i ^ by) for i in range(peers)])  7.43 us
    ppermute x2, starting transfers between devices, passed_along(): lax.ppermute(array, axis, [(i, (i + by) % peers) for i in range(peers)])  6.04 us
    ppermute x8, waiting for transfers between devices, along_ring(): return lax.ppermute(array, ('ent', 'rep'), pairs)  4.47 us
    ppermute x11, waiting for transfers between devices, rep_swapped(): return lax.ppermute(array, 'rep', [(i, i ^ by) for i in range(peers)])  3.92 us
    convert_element_type x1, other arithmetic, gathered_shards(): table_half = late_table.astype(bf16)  1.2 us
  transfers between devices with their start and end apart: 21, of which 8 were waited for; matrix products, arithmetic and copies ran while one was open for 6% of the time, Pallas kernels for 17%

profile of v6, /device:TPU:0, one launch (start us, length us, event | category | flops | bytes accessed | tf_op | source)
XLA Modules:
  0.0 52.7 jit_solution(17782224212070161657)
XLA Ops:
  0.6 1.0 %convert_element_type.33.o0 = bf16[2,200,200]{2,1,0:T(8,128)(2,1)S(1)} convert(f32[2,200,200]{2,1,0:T(8,128)} %operators.1) | non-fusion elementwise | flops 80000 | bytes 480000 | tf_op jit(solution)/shard_map/convert_element_type | solution.py:449
  1.7 3.1 %collective-permute-start = (bf16[2,200,200]{2,1,0:T(8,128)(2,1)S(1)}, bf16[2,200,200]{2,1,0:T(8,128)(2,1)S(1)}, u32[]{:S(2)}, u32[]{:S(2)}) collective-permute-start(bf16[2,200,200]{2,1,0:T(8,128)(2,1)S(1)} %convert_element_type.33.o0), channel_id=1, source_target_pairs={{0,8},{1,5},{2,10},{3,7},{4,0},{5,13},{6,2},{7,15},{8,16},{9,1},{1... | collective-permute-start | bytes 480008 | tf_op jit(solution)/shard_map/ppermute | solution.py:428
  4.7 0.8 %concatenate.3 = s32[2048]{0:T(1024)S(1)} concatenate(s32[256]{0:T(256)} %param.12, s32[256]{0:T(256)} %param.13, s32[256]{0:T(256)} %bitcast.12, s32[1000]{0:T(1024)} %bitcast.11, s32[280]{0:T(512)S(1)} %broadcast_in_dim.3), dimensions={0} | concatenate | bytes 16384 | tf_op jit(solution)/shard_map/concatenate | solution.py:451
  6.1 1.0 %collective-permute-start.2 = (s32[8,256]{1,0:T(8,128)S(1)}, s32[8,256]{1,0:T(8,128)S(1)}, u32[]{:S(2)}, u32[]{:S(2)}) collective-permute-start(s32[8,256]{1,0:T(8,128)S(1)} %reshape.17.own), channel_id=1, source_target_pairs={{0,2},{1,3},{2,0},{3,1},{4,6},{5,7},{6,4},{7,5},{8,10},{9,11},{10,... | collective-permute-start | bytes 24584 | tf_op jit(solution)/shard_map/ppermute | solution.py:417
  7.4 1.0 %fusion = bf16[200,512]{1,0:T(8,128)(2,1)S(1)} fusion(f32[1024,200]{0,1:T(8,128)} %param.8, s32[]{:T(128)S(6)} %select_n.14), kind=kLoop, calls=%fused_computation.1 | loop fusion | bytes 409604 | tf_op jit(solution)/shard_map/convert_element_type | solution.py:468
  8.6 1.2 %collective-permute-done.2.far = s32[8,256]{1,0:T(8,128)S(1)} collective-permute-done((s32[8,256]{1,0:T(8,128)S(1)}, s32[8,256]{1,0:T(8,128)S(1)}, u32[]{:S(2)}, u32[]{:S(2)}) %collective-permute-start.2) | collective-permute-done | bytes 8224 | tf_op jit(solution)/shard_map/ppermute | solution.py:417
  9.9 1.3 %collective-permute-start.4 = (bf16[2,200,200]{2,1,0:T(8,128)(2,1)S(1)}, bf16[2,200,200]{2,1,0:T(8,128)(2,1)S(1)}, u32[]{:S(2)}, u32[]{:S(2)}) collective-permute-start(bf16[2,200,200]{2,1,0:T(8,128)(2,1)S(1)} %collective-permute-done.a1), channel_id=1, source_target_pairs={{0,8},{1,5},{2,10},{3,7},{4,0},{5,13},{6,2},{7,15},{8,16},{9,1},{1... | collective-permute-start | bytes 480008 | tf_op jit(solution)/shard_map/ppermute | solution.py:428
  11.3 3.7 %collective-permute-start.9 = (bf16[200,512]{1,0:T(8,128)(2,1)S(1)}, bf16[200,512]{1,0:T(8,128)(2,1)S(1)}, u32[]{:S(2)}, u32[]{:S(2)}) collective-permute-start(bf16[200,512]{1,0:T(8,128)(2,1)S(1)} %fusion), channel_id=1, source_target_pairs={{0,28},{4,0},{8,4},{12,8},{16,12},{20,16},{24,20},{28,24},{1,29},{... | collective-permute-start | bytes 614408 | tf_op jit(solution)/shard_map/ppermute | solution.py:22
  14.9 2.3 %collective-permute-done.4.a2 = bf16[2,200,200]{2,1,0:T(8,128)(2,1)S(1)} collective-permute-done((bf16[2,200,200]{2,1,0:T(8,128)(2,1)S(1)}, bf16[2,200,200]{2,1,0:T(8,128)(2,1)S(1)}, u32[]{:S(2)}, u32[]{:S(2)}) %collective-permute-start.4) | collective-permute-done | bytes 160032 | tf_op jit(solution)/shard_map/ppermute | solution.py:428
  17.2 2.4 %collective-permute-start.7 = (bf16[1,200,200]{2,1,0:T(8,128)(2,1)S(1)}, bf16[1,200,200]{2,1,0:T(8,128)(2,1)S(1)}, u32[]{:S(2)}, u32[]{:S(2)}) collective-permute-start(bf16[1,200,200]{2,1,0:T(8,128)(2,1)S(1)} %constant_dynamic-slice_fusion), channel_id=1, source_target_pairs={{0,16},{1,13},{2,18},{3,15},{4,8},{5,21},{6,10},{7,23},{8,24},{9,5... | collective-permute-start | bytes 240008 | tf_op jit(solution)/shard_map/ppermute | solution.py:428
  19.6 1.2 %convert_element_type.36.table = bf16[200,1024]{1,0:T(8,128)(2,1)S(1)} convert(f32[200,1024]{1,0:T(8,128)} %bitcast.8) | non-fusion elementwise | flops 204800 | bytes 1228800 | tf_op jit(solution)/shard_map/convert_element_type | solution.py:478
  20.8 2.0 %slots.1 = (bf16[4,16,32,200]{3,2,1,0:T(8,128)(2,1)S(1)}, f32[4,8,256]{2,1,0:T(8,128)S(1)}, f32[4,1,1024]{2,1,0:T(1,128)S(1)}) custom-call(s32[8,256]{1,0:T(8,128)S(1)} %reshape.17.own, s32[8,256]{1,0:T(8,128)S(1)} %collective-permute-done.1.near, s32[8,256]{1,0:T(8,128)S(1)} %collective-permute-done.2.far, s32[8,256]{1,0:T(8,128)S(1)} %collective-permute-done.3.across, ...), custom_call_target="tpu_custom_call" | custom-call | flops 100000000 | bytes 1000000 | tf_op jit(solution)/shard_map/slots/pallas_call | solution.py:166
  22.9 1.8 %collective-permute-done.7.a4 = bf16[1,200,200]{2,1,0:T(8,128)(2,1)S(1)} collective-permute-done((bf16[1,200,200]{2,1,0:T(8,128)(2,1)S(1)}, bf16[1,200,200]{2,1,0:T(8,128)(2,1)S(1)}, u32[]{:S(2)}, u32[]{:S(2)}) %collective-permute-start.7) | collective-permute-done | bytes 80032 | tf_op jit(solution)/shard_map/ppermute | solution.py:428
  25.3 0.9 %ready.1.made_early = bf16[1024,200]{1,0:T(8,128)(2,1)S(1)} custom-call(bf16[2,200,200]{2,1,0:T(8,128)(2,1)S(1)} %convert_element_type.33.o0, bf16[2,200,200]{2,1,0:T(8,128)(2,1)S(1)} %collective-permute-done.a1, bf16[2,200,200]{2,1,0:T(8,128)(2,1)S(1)} %collective-permute-done.4.a2, bf16[2,200,200]{2,1,0:T(8,128)(2,1)S(1)} %collective-permute-done.8.b2, ...), custom_call_target="tpu_custom_call" | custom-call | flops 100000000 | bytes 1000000 | tf_op jit(solution)/shard_map/ready/pallas_call | solution.py:166
  26.6 3.9 %scores.1 = (bf16[320,128]{1,0:T(8,128)(2,1)S(1)}, bf16[320,128]{1,0:T(8,128)(2,1)S(1)}, bf16[320,128]{1,0:T(8,128)(2,1)S(1)}, bf16[320,128]{1,0:T(8,128)(2,1)S(...) custom-call(bf16[2,200,200]{2,1,0:T(8,128)(2,1)S(1)} %collective-permute-d, ...), custom_call_target="tpu_custom_call" | custom-call | flops 1000000000 | bytes 1000000 | tf_op jit(solution)/shard_map/scores/pallas_call | solution.py:166
  31.2 1.9 %collective-permute-start.14 = (bf16[320,128]{1,0:T(8,128)(2,1)S(1)}, bf16[320,128]{1,0:T(8,128)(2,1)S(1)}, u32[]{:S(2)}, u32[]{:S(2)}) collective-permute-start(bf16[320,128]{1,0:T(8,128)(2,1)S(1)} %get-tuple-element.70), channel_id=1, source_target_pairs={{0,20},{1,25},{2,6},{3,11},{4,28},{5,17},{6,14},{7,3},{8,12},{9,29... | collective-permute-start | bytes 245768 | tf_op jit(solution)/shard_map/ppermute | solution.py:428
  33.1 2.0 %collective-permute-start.15 = (bf16[320,128]{1,0:T(8,128)(2,1)S(1)}, bf16[320,128]{1,0:T(8,128)(2,1)S(1)}, u32[]{:S(2)}, u32[]{:S(2)}) collective-permute-start(bf16[320,128]{1,0:T(8,128)(2,1)S(1)} %get-tuple-element.71), channel_id=1, source_target_pairs={{0,24},{1,21},{2,10},{3,7},{4,16},{5,29},{6,2},{7,15},{8,28},{9,13... | collective-permute-start | bytes 245768 | tf_op jit(solution)/shard_map/ppermute | solution.py:428
  35.3 2.0 %targets.1 = bf16[200,512]{1,0:T(8,128)(2,1)S(1)} custom-call(f32[4,8,256]{2,1,0:T(8,128)S(1)} %get-tuple-element.61.rows, bf16[4,256,1024]{2,1,0:T(8,128)(2,1)S(1)} %get-tuple-element.66.weights, bf16[4,768,200]{2,1,0:T(8,128)(2,1)S(1)} %get-tuple-element.67.sides), custom_call_target="tpu_custom_call" | custom-call | flops 100000000 | bytes 1000000 | tf_op jit(solution)/shard_map/targets/pallas_call | solution.py:166
  37.4 2.4 %collective-permute-start.19 = (bf16[200,512]{1,0:T(8,128)(2,1)S(1)}, bf16[200,512]{1,0:T(8,128)(2,1)S(1)}, u32[]{:S(2)}, u32[]{:S(2)}) collective-permute-start(bf16[200,512]{1,0:T(8,128)(2,1)S(1)} %targets.1), channel_id=1, source_target_pairs={{0,4},{4,8},{8,12},{12,16},{16,20},{20,24},{24,28},{28,0},{1,5},{5... | collective-permute-start | bytes 614408 | tf_op jit(solution)/shard_map/ppermute | solution.py:22
  39.7 3.1 %sources.1.source_total = f32[200,1024]{1,0:T(8,128)S(1)} custom-call(bf16[2,200,200]{2,1,0:T(8,128)(2,1)S(1)} %convert_element_type.33.o0, bf16[2,200,200]{2,1,0:T(8,128)(2,1)S(1)} %collective-permute-done.a1, bf16[2,200,200]{2,1,0:T(8,128)(2,1)S(1)} %collective-permute-done.4.a2, bf16[2,200,200]{2,1,0:T(8,128)(2,1)S(1)} %collective-permute-done.6.a3, ...), custom_call_target="tpu_custom_call" | custom-call | flops 100000000 | bytes 1000000 | tf_op jit(solution)/shard_map/sources/pallas_call | solution.py:166
  43.3 4.2 %collective-permute-start.17 = (bf16[320,128]{1,0:T(8,128)(2,1)S(1)}, bf16[320,128]{1,0:T(8,128)(2,1)S(1)}, u32[]{:S(2)}, u32[]{:S(2)}) collective-permute-start(bf16[320,128]{1,0:T(8,128)(2,1)S(1)} %add_convert_fusion), channel_id=1, source_target_pairs={{0,2},{1,3},{2,0},{3,1},{4,6},{5,7},{6,4},{7,5},{8,10},{9,11},{10,... | collective-permute-start | bytes 245768 | tf_op jit(solution)/shard_map/ppermute | solution.py:417
  48.1 1.9 %collective-permute-done.17 = bf16[320,128]{1,0:T(8,128)(2,1)S(1)} collective-permute-done((bf16[320,128]{1,0:T(8,128)(2,1)S(1)}, bf16[320,128]{1,0:T(8,128)(2,1)S(1)}, u32[]{:S(2)}, u32[]{:S(2)}) %collective-permute-start.17) | collective-permute-done | bytes 81952 | tf_op jit(solution)/shard_map/ppermute | solution.py:417
  50.1 1.2 %entity_update.1 = (f32[200,1024]{1,0:T(8,128)}, f32[1,1024]{1,0:T(1,128)}) custom-call(f32[200,1024]{1,0:T(8,128)S(1)} %sources.1.source_total, bf16[200,512]{1,0:T(8,128)(2,1)S(1)} %collective-permute-done.19.mine, bf16[200,512]{1,0:T(8,128)(2,1)S(1)} %collective-permute-done.20.other, f32[200,1024]{1,0:T(8,128)S(1)} %bitcast.9, f32[1,1024]{1,0:T(1,128)S(1)} %bitcast.10), custom_call_target="tpu_custom_call" | custom-call | flops 1000000 | bytes 1000000 | tf_op jit(solution)/shard_map/entity_update/pallas_call | solution.py:166
  51.4 1.2 %operator_update.1 = (f32[2,200,200]{2,1,0:T(8,128)}, f32[2,200,200]{2,1,0:T(8,128)}) custom-call(f32[320,128]{1,0:T(8,128)S(1)} %convert_add_fusion.own, f32[320,128]{1,0:T(8,128)S(1)} %collective-permute-done.18.other, f32[2,200,200]{2,1,0:T(8,128)S(1)} %copy-done.1, f32[2,200,200]{2,1,0:T(8,128)S(1)} %copy-done.2), custom_call_target="tpu_custom_call" | custom-call | flops 1000000 | bytes 1000000 | tf_op jit(solution)/shard_map/operator_update/pallas_call | solution.py:166
  (42 shorter events, 4.5 us)
Async XLA Ops:
  1.7 8.2 %collective-permute-start = (bf16[2,200,200]{2,1,0:T(8,128)(2,1)S(1)}, bf16[2,200,200]{2,1,0:T(8,128)(2,1)S(1)}, u32[]{:S(2)}, u32[]{:S(2)}) collective-permute-start(bf16[2,200,200]{2,1,0:T(8,128)(2,1)S(1)} %convert_element_type.33.o0), channel_id=1, source_target_pairs={{0,8},{1,5},{2,10},{3,7},{4,0},{5,13},{6,2},{7,15},{8,16},{9,1},{1... | collective-permute-start | bytes 480008 | tf_op jit(solution)/shard_map/ppermute | solution.py:428
  5.6 3.1 %collective-permute-start.3 = (s32[8,256]{1,0:T(8,128)S(1)}, s32[8,256]{1,0:T(8,128)S(1)}, u32[]{:S(2)}, u32[]{:S(2)}) collective-permute-start(s32[8,256]{1,0:T(8,128)S(1)} %reshape.17.own), channel_id=1, source_target_pairs={{0,3},{1,2},{2,1},{3,0},{4,7},{5,6},{6,5},{7,4},{8,11},{9,10},{10,... | collective-permute-start | bytes 24584 | tf_op jit(solution)/shard_map/ppermute | solution.py:417
  6.1 3.7 %collective-permute-start.2 = (s32[8,256]{1,0:T(8,128)S(1)}, s32[8,256]{1,0:T(8,128)S(1)}, u32[]{:S(2)}, u32[]{:S(2)}) collective-permute-start(s32[8,256]{1,0:T(8,128)S(1)} %reshape.17.own), channel_id=1, source_target_pairs={{0,2},{1,3},{2,0},{3,1},{4,6},{5,7},{6,4},{7,5},{8,10},{9,11},{10,... | collective-permute-start | bytes 24584 | tf_op jit(solution)/shard_map/ppermute | solution.py:417
  7.1 2.7 %collective-permute-start.1 = (s32[8,256]{1,0:T(8,128)S(1)}, s32[8,256]{1,0:T(8,128)S(1)}, u32[]{:S(2)}, u32[]{:S(2)}) collective-permute-start(s32[8,256]{1,0:T(8,128)S(1)} %reshape.17.own), channel_id=1, source_target_pairs={{0,1},{1,0},{2,3},{3,2},{4,5},{5,4},{6,7},{7,6},{8,9},{9,8},{10,11... | collective-permute-start | bytes 24584 | tf_op jit(solution)/shard_map/ppermute | solution.py:417
  9.8 1.5 %collective-permute-start.5 = (bf16[2,200,200]{2,1,0:T(8,128)(2,1)S(1)}, bf16[2,200,200]{2,1,0:T(8,128)(2,1)S(1)}, u32[]{:S(2)}, u32[]{:S(2)}) collective-permute-start(bf16[2,200,200]{2,1,0:T(8,128)(2,1)S(1)} %collective-permute-done.a1), channel_id=1, source_target_pairs={{0,1},{1,0},{2,3},{3,2},{4,5},{5,4},{6,7},{7,6},{8,9},{9,8},{10,11... | collective-permute-start | bytes 480008 | tf_op jit(solution)/shard_map/ppermute | solution.py:417
  9.9 7.3 %collective-permute-start.4 = (bf16[2,200,200]{2,1,0:T(8,128)(2,1)S(1)}, bf16[2,200,200]{2,1,0:T(8,128)(2,1)S(1)}, u32[]{:S(2)}, u32[]{:S(2)}) collective-permute-start(bf16[2,200,200]{2,1,0:T(8,128)(2,1)S(1)} %collective-permute-done.a1), channel_id=1, source_target_pairs={{0,8},{1,5},{2,10},{3,7},{4,0},{5,13},{6,2},{7,15},{8,16},{9,1},{1... | collective-permute-start | bytes 480008 | tf_op jit(solution)/shard_map/ppermute | solution.py:428
  11.3 13.4 %collective-permute-start.9 = (bf16[200,512]{1,0:T(8,128)(2,1)S(1)}, bf16[200,512]{1,0:T(8,128)(2,1)S(1)}, u32[]{:S(2)}, u32[]{:S(2)}) collective-permute-start(bf16[200,512]{1,0:T(8,128)(2,1)S(1)} %fusion), channel_id=1, source_target_pairs={{0,28},{4,0},{8,4},{12,8},{16,12},{20,16},{24,20},{28,24},{1,29},{... | collective-permute-start | bytes 614408 | tf_op jit(solution)/shard_map/ppermute | solution.py:22
  17.2 7.4 %collective-permute-start.8 = (bf16[2,200,200]{2,1,0:T(8,128)(2,1)S(1)}, bf16[2,200,200]{2,1,0:T(8,128)(2,1)S(1)}, u32[]{:S(2)}, u32[]{:S(2)}) collective-permute-start(bf16[2,200,200]{2,1,0:T(8,128)(2,1)S(1)} %collective-permute-done.4.a2), channel_id=1, source_target_pairs={{0,1},{1,0},{2,3},{3,2},{4,5},{5,4},{6,7},{7,6},{8,9},{9,8},{10,11... | collective-permute-start | bytes 480008 | tf_op jit(solution)/shard_map/ppermute | solution.py:417
  17.2 7.4 %collective-permute-start.6 = (bf16[2,200,200]{2,1,0:T(8,128)(2,1)S(1)}, bf16[2,200,200]{2,1,0:T(8,128)(2,1)S(1)}, u32[]{:S(2)}, u32[]{:S(2)}) collective-permute-start(bf16[2,200,200]{2,1,0:T(8,128)(2,1)S(1)} %collective-permute-done.4.a2), channel_id=1, source_target_pairs={{0,8},{1,5},{2,10},{3,7},{4,0},{5,13},{6,2},{7,15},{8,16},{9,1},{1... | collective-permute-start | bytes 480008 | tf_op jit(solution)/shard_map/ppermute | solution.py:428
  17.2 7.4 %collective-permute-start.7 = (bf16[1,200,200]{2,1,0:T(8,128)(2,1)S(1)}, bf16[1,200,200]{2,1,0:T(8,128)(2,1)S(1)}, u32[]{:S(2)}, u32[]{:S(2)}) collective-permute-start(bf16[1,200,200]{2,1,0:T(8,128)(2,1)S(1)} %constant_dynamic-slice_fusion), channel_id=1, source_target_pairs={{0,16},{1,13},{2,18},{3,15},{4,8},{5,21},{6,10},{7,23},{8,24},{9,5... | collective-permute-start | bytes 240008 | tf_op jit(solution)/shard_map/ppermute | solution.py:428
  24.7 2.0 %collective-permute-start.12 = (bf16[200,512]{1,0:T(8,128)(2,1)S(1)}, bf16[200,512]{1,0:T(8,128)(2,1)S(1)}, u32[]{:S(2)}, u32[]{:S(2)}) collective-permute-start(bf16[200,512]{1,0:T(8,128)(2,1)S(1)} %collective-permute-done.9.mine), channel_id=1, source_target_pairs={{0,1},{1,0},{2,3},{3,2},{4,5},{5,4},{6,7},{7,6},{8,9},{9,8},{10,11... | collective-permute-start | bytes 614408 | tf_op jit(solution)/shard_map/ppermute | solution.py:417
  24.7 1.9 %collective-permute-start.11 = (bf16[2,200,200]{2,1,0:T(8,128)(2,1)S(1)}, bf16[2,200,200]{2,1,0:T(8,128)(2,1)S(1)}, u32[]{:S(2)}, u32[]{:S(2)}) collective-permute-start(bf16[2,200,200]{2,1,0:T(8,128)(2,1)S(1)} %collective-permute-done.6.a3), channel_id=1, source_target_pairs={{0,1},{1,0},{2,3},{3,2},{4,5},{5,4},{6,7},{7,6},{8,9},{9,8},{10,11... | collective-permute-start | bytes 480008 | tf_op jit(solution)/shard_map/ppermute | solution.py:417
  25.2 1.4 %collective-permute-start.10 = (bf16[1,200,200]{2,1,0:T(8,128)(2,1)S(1)}, bf16[1,200,200]{2,1,0:T(8,128)(2,1)S(1)}, u32[]{:S(2)}, u32[]{:S(2)}) collective-permute-start(bf16[1,200,200]{2,1,0:T(8,128)(2,1)S(1)} %collective-permute-done.7.a4), channel_id=1, source_target_pairs={{0,1},{1,0},{2,3},{3,2},{4,5},{5,4},{6,7},{7,6},{8,9},{9,8},{10,11... | collective-permute-start | bytes 240008 | tf_op jit(solution)/shard_map/ppermute | solution.py:417
  30.6 12.3 %collective-permute-start.13 = (bf16[320,128]{1,0:T(8,128)(2,1)S(1)}, bf16[320,128]{1,0:T(8,128)(2,1)S(1)}, u32[]{:S(2)}, u32[]{:S(2)}) collective-permute-start(bf16[320,128]{1,0:T(8,128)(2,1)S(1)} %get-tuple-element.69), channel_id=1, source_target_pairs={{0,0},{1,1},{2,30},{3,31},{4,4},{5,5},{6,26},{7,27},{8,8},{9,9},{1... | collective-permute-start | bytes 245768 | tf_op jit(solution)/shard_map/ppermute | solution.py:428
  31.2 11.6 %collective-permute-start.14 = (bf16[320,128]{1,0:T(8,128)(2,1)S(1)}, bf16[320,128]{1,0:T(8,128)(2,1)S(1)}, u32[]{:S(2)}, u32[]{:S(2)}) collective-permute-start(bf16[320,128]{1,0:T(8,128)(2,1)S(1)} %get-tuple-element.70), channel_id=1, source_target_pairs={{0,20},{1,25},{2,6},{3,11},{4,28},{5,17},{6,14},{7,3},{8,12},{9,29... | collective-permute-start | bytes 245768 | tf_op jit(solution)/shard_map/ppermute | solution.py:428
  33.1 9.8 %collective-permute-start.15 = (bf16[320,128]{1,0:T(8,128)(2,1)S(1)}, bf16[320,128]{1,0:T(8,128)(2,1)S(1)}, u32[]{:S(2)}, u32[]{:S(2)}) collective-permute-start(bf16[320,128]{1,0:T(8,128)(2,1)S(1)} %get-tuple-element.71), channel_id=1, source_target_pairs={{0,24},{1,21},{2,10},{3,7},{4,16},{5,29},{6,2},{7,15},{8,28},{9,13... | collective-permute-start | bytes 245768 | tf_op jit(solution)/shard_map/ppermute | solution.py:428
  35.1 8.2 %collective-permute-start.16 = (bf16[320,128]{1,0:T(8,128)(2,1)S(1)}, bf16[320,128]{1,0:T(8,128)(2,1)S(1)}, u32[]{:S(2)}, u32[]{:S(2)}) collective-permute-start(bf16[320,128]{1,0:T(8,128)(2,1)S(1)} %get-tuple-element.72), channel_id=1, source_target_pairs={{0,12},{1,17},{2,18},{3,15},{4,20},{5,9},{6,10},{7,23},{8,4},{9,25... | collective-permute-start | bytes 245768 | tf_op jit(solution)/shard_map/ppermute | solution.py:428
  37.3 12.7 %copy-start = (f32[1024,200]{0,1:T(8,128)S(1)}, f32[1024,200]{0,1:T(8,128)}, u32[]{:S(2)}) copy-start(f32[1024,200]{0,1:T(8,128)} %param.8) | copy-start | bytes 2457604
  37.3 12.7 %copy-start.3 = (f32[1024]{0:T(1024)S(1)}, f32[1024]{0:T(1024)}, u32[]{:S(2)}) copy-start(f32[1024]{0:T(1024)} %param.9) | copy-start | bytes 12292
  37.4 10.2 %collective-permute-start.19 = (bf16[200,512]{1,0:T(8,128)(2,1)S(1)}, bf16[200,512]{1,0:T(8,128)(2,1)S(1)}, u32[]{:S(2)}, u32[]{:S(2)}) collective-permute-start(bf16[200,512]{1,0:T(8,128)(2,1)S(1)} %targets.1), channel_id=1, source_target_pairs={{0,4},{4,8},{8,12},{12,16},{16,20},{20,24},{24,28},{28,0},{1,5},{5... | collective-permute-start | bytes 614408 | tf_op jit(solution)/shard_map/ppermute | solution.py:22
  42.8 8.6 %copy-start.1 = (f32[2,200,200]{2,1,0:T(8,128)S(1)}, f32[2,200,200]{2,1,0:T(8,128)}, u32[]{:S(2)}) copy-start(f32[2,200,200]{2,1,0:T(8,128)} %operators.1) | copy-start | bytes 960004
  43.3 6.6 %collective-permute-start.17 = (bf16[320,128]{1,0:T(8,128)(2,1)S(1)}, bf16[320,128]{1,0:T(8,128)(2,1)S(1)}, u32[]{:S(2)}, u32[]{:S(2)}) collective-permute-start(bf16[320,128]{1,0:T(8,128)(2,1)S(1)} %add_convert_fusion), channel_id=1, source_target_pairs={{0,2},{1,3},{2,0},{3,1},{4,6},{5,7},{6,4},{7,5},{8,10},{9,11},{10,... | collective-permute-start | bytes 245768 | tf_op jit(solution)/shard_map/ppermute | solution.py:417
  47.5 2.5 %collective-permute-start.20 = (bf16[200,512]{1,0:T(8,128)(2,1)S(1)}, bf16[200,512]{1,0:T(8,128)(2,1)S(1)}, u32[]{:S(2)}, u32[]{:S(2)}) collective-permute-start(bf16[200,512]{1,0:T(8,128)(2,1)S(1)} %collective-permute-done.19.mine), channel_id=1, source_target_pairs={{0,1},{1,0},{2,3},{3,2},{4,5},{5,4},{6,7},{7,6},{8,9},{9,8},{10,11... | collective-permute-start | bytes 614408 | tf_op jit(solution)/shard_map/ppermute | solution.py:417
  50.0 1.5 %collective-permute-start.18 = (f32[320,128]{1,0:T(8,128)S(1)}, f32[320,128]{1,0:T(8,128)S(1)}, u32[]{:S(2)}, u32[]{:S(2)}) collective-permute-start(f32[320,128]{1,0:T(8,128)S(1)} %convert_add_fusion.own), channel_id=1, source_target_pairs={{0,1},{1,0},{2,3},{3,2},{4,5},{5,4},{6,7},{7,6},{8,9},{9,8},{10,11... | collective-permute-start | bytes 491528 | tf_op jit(solution)/shard_map/ppermute | solution.py:417
  (1 other events, 8.6 us)

commit v7 on v6

--- a/solution.py
+++ b/solution.py
@@ -139,7 +139,7 @@
 PLACE = tuple(RING.index(e) for e in range(8))
 SLOTS = 32
 SIDE = 104
-OFFSETS = ((0, 4), (3, 1), (5, 7), (2, 6))
+OFFSETS = ((3, 4), (5, 6), (2, 1), (0, 7))
 VMEM = pltpu.VMEM
 NT = (((1,), (1,)), ((), ()))
 TN = (((0,), (0,)), ((), ()))
@@ -356,18 +356,19 @@
     return [None if ref is None else lambda ref=ref, i=i: ref[i] for ref, i in listed]
 
 
-def target_kernel(rows, weights, sides, target_half, total):
+def target_kernel(rows, weights, sides, target_half):
     core, *_ = position()
-    reps, edges, entities = weights.shape
+    reps, edges, _ = weights.shape
     half = target_half.shape[1]
+    at = pl.ds(pl.multiple_of(core * half, half), half)
+    grown = jnp.zeros(target_half.shape, f32)
     for b in range(reps):
-        aimed = one_hot(lanes_of((edges, entities)) == rows[b].T[:, 1:2].astype(jnp.int32))
-        grown = dot(sides[b], jnp.concatenate([weights[b], aimed, aimed], axis=0), TN)
-        if b == 0:
-            total[...] = grown
-        else:
-            total[...] += grown
-    target_half[...] = total[:, pl.ds(pl.multiple_of(core * half, half), half)].astype(bf16)
+        aimed = one_hot(
+            lanes_of((edges, half)) + core * half == rows[b].T[:, 1:2].astype(jnp.int32)
+        )
+        faces = jnp.concatenate([weights[b, :, at], aimed, aimed], axis=0)
+        grown = grown + dot(sides[b], faces, TN)
+    target_half[...] = grown.astype(bf16)
 
 
 def source_kernel(o0, a1, a2, a3, a4, b4, b3, b2, b1, rows, query, source_total, held):
@@ -509,7 +510,6 @@
         target_kernel,
         [jax.ShapeDtypeStruct((width, half), bf16)],
         "targets", 10**8, 10**6, (rows, weights, sides),
-        scratch=[VMEM((width, entities), f32)],
     )
     query, target_half = lax.optimization_barrier((query, target_half))
     (source_total,) = call(

time: 53.3 us -> 52.4 us (0.983)
  Pallas kernels: 14.2 us -> 13.4 us
    pallas_call x7, Pallas kernels: 14.2 us -> 13.4 us  [call(): pl.pallas_call(body, out_shape=outs, in_specs=[whole] * len(operands), ou...]
  transfers between devices with their start and end apart: 21 -> 21, of which waited for: 8 -> 8; matrix products, arithmetic and copies ran while one was open for 6% -> 6% of each run, Pallas kernels for 17% -> 16%
where the time goes in v7:
time: 52.4 us; the launch traced here: 51.8 us
  starting transfers between devices  24.8 us (47%)
  Pallas kernels  13.4 us (26%)
  waiting for transfers between devices  8.58 us (16%)
  other arithmetic  2.29 us (4%)
  local copies, waits for them, and re-layouts  1.88 us (4%)
  between operations  0.8 us (2%)
    pallas_call x7, Pallas kernels, call(): pl.pallas_call(body, out_shape=outs, in_specs=[whole] * len(operands), ou...  13.4 us
    ppermute x8, starting transfers between devices, along_ring(): return lax.ppermute(array, ('ent', 'rep'), pairs)  11.5 us
    ppermute x11, starting transfers between devices, rep_swapped(): return lax.ppermute(array, 'rep', [(i, i ^ by) for i in range(peers)])  7.26 us
    ppermute x2, starting transfers between devices, passed_along(): lax.ppermute(array, axis, [(i, (i + by) % peers) for i in range(peers)])  6.04 us
    ppermute x8, waiting for transfers between devices, along_ring(): return lax.ppermute(array, ('ent', 'rep'), pairs)  4.66 us
    ppermute x11, waiting for transfers between devices, rep_swapped(): return lax.ppermute(array, 'rep', [(i, i ^ by) for i in range(peers)])  3.92 us
    convert_element_type x1, other arithmetic, gathered_shards(): table_half = late_table.astype(bf16)  1.2 us
  transfers between devices with their start and end apart: 21, of which 8 were waited for; matrix products, arithmetic and copies ran while one was open for 6% of the time, Pallas kernels for 16%

profile of v7, /device:TPU:0, one launch (start us, length us, event | category | flops | bytes accessed | tf_op | source)
XLA Modules:
  0.0 51.8 jit_solution(15607339107971728969)
XLA Ops:
  0.6 1.0 %convert_element_type.33.o0 = bf16[2,200,200]{2,1,0:T(8,128)(2,1)S(1)} convert(f32[2,200,200]{2,1,0:T(8,128)} %operators.1) | non-fusion elementwise | flops 80000 | bytes 480000 | tf_op jit(solution)/shard_map/convert_element_type | solution.py:450
  1.7 3.1 %collective-permute-start = (bf16[2,200,200]{2,1,0:T(8,128)(2,1)S(1)}, bf16[2,200,200]{2,1,0:T(8,128)(2,1)S(1)}, u32[]{:S(2)}, u32[]{:S(2)}) collective-permute-start(bf16[2,200,200]{2,1,0:T(8,128)(2,1)S(1)} %convert_element_type.33.o0), channel_id=1, source_target_pairs={{0,8},{1,5},{2,10},{3,7},{4,0},{5,13},{6,2},{7,15},{8,16},{9,1},{1... | collective-permute-start | bytes 480008 | tf_op jit(solution)/shard_map/ppermute | solution.py:429
  4.7 0.8 %concatenate.3 = s32[2048]{0:T(1024)S(1)} concatenate(s32[256]{0:T(256)} %param.12, s32[256]{0:T(256)} %param.13, s32[256]{0:T(256)} %bitcast.12, s32[1000]{0:T(1024)} %bitcast.11, s32[280]{0:T(512)S(1)} %broadcast_in_dim.3), dimensions={0} | concatenate | bytes 16384 | tf_op jit(solution)/shard_map/concatenate | solution.py:452
  6.1 1.0 %collective-permute-start.2 = (s32[8,256]{1,0:T(8,128)S(1)}, s32[8,256]{1,0:T(8,128)S(1)}, u32[]{:S(2)}, u32[]{:S(2)}) collective-permute-start(s32[8,256]{1,0:T(8,128)S(1)} %reshape.17.own), channel_id=1, source_target_pairs={{0,2},{1,3},{2,0},{3,1},{4,6},{5,7},{6,4},{7,5},{8,10},{9,11},{10,... | collective-permute-start | bytes 24584 | tf_op jit(solution)/shard_map/ppermute | solution.py:418
  7.4 1.0 %fusion = bf16[200,512]{1,0:T(8,128)(2,1)S(1)} fusion(f32[1024,200]{0,1:T(8,128)} %param.8, s32[]{:T(128)S(6)} %select_n.14), kind=kLoop, calls=%fused_computation.1 | loop fusion | bytes 409604 | tf_op jit(solution)/shard_map/convert_element_type | solution.py:469
  8.6 1.2 %collective-permute-done.2.far = s32[8,256]{1,0:T(8,128)S(1)} collective-permute-done((s32[8,256]{1,0:T(8,128)S(1)}, s32[8,256]{1,0:T(8,128)S(1)}, u32[]{:S(2)}, u32[]{:S(2)}) %collective-permute-start.2) | collective-permute-done | bytes 8224 | tf_op jit(solution)/shard_map/ppermute | solution.py:418
  9.9 1.3 %collective-permute-start.4 = (bf16[2,200,200]{2,1,0:T(8,128)(2,1)S(1)}, bf16[2,200,200]{2,1,0:T(8,128)(2,1)S(1)}, u32[]{:S(2)}, u32[]{:S(2)}) collective-permute-start(bf16[2,200,200]{2,1,0:T(8,128)(2,1)S(1)} %collective-permute-done.a1), channel_id=1, source_target_pairs={{0,8},{1,5},{2,10},{3,7},{4,0},{5,13},{6,2},{7,15},{8,16},{9,1},{1... | collective-permute-start | bytes 480008 | tf_op jit(solution)/shard_map/ppermute | solution.py:429
  11.3 3.7 %collective-permute-start.9 = (bf16[200,512]{1,0:T(8,128)(2,1)S(1)}, bf16[200,512]{1,0:T(8,128)(2,1)S(1)}, u32[]{:S(2)}, u32[]{:S(2)}) collective-permute-start(bf16[200,512]{1,0:T(8,128)(2,1)S(1)} %fusion), channel_id=1, source_target_pairs={{0,28},{4,0},{8,4},{12,8},{16,12},{20,16},{24,20},{28,24},{1,29},{... | collective-permute-start | bytes 614408 | tf_op jit(solution)/shard_map/ppermute | solution.py:22
  14.9 2.3 %collective-permute-done.4.a2 = bf16[2,200,200]{2,1,0:T(8,128)(2,1)S(1)} collective-permute-done((bf16[2,200,200]{2,1,0:T(8,128)(2,1)S(1)}, bf16[2,200,200]{2,1,0:T(8,128)(2,1)S(1)}, u32[]{:S(2)}, u32[]{:S(2)}) %collective-permute-start.4) | collective-permute-done | bytes 160032 | tf_op jit(solution)/shard_map/ppermute | solution.py:429
  17.2 2.4 %collective-permute-start.7 = (bf16[1,200,200]{2,1,0:T(8,128)(2,1)S(1)}, bf16[1,200,200]{2,1,0:T(8,128)(2,1)S(1)}, u32[]{:S(2)}, u32[]{:S(2)}) collective-permute-start(bf16[1,200,200]{2,1,0:T(8,128)(2,1)S(1)} %constant_dynamic-slice_fusion), channel_id=1, source_target_pairs={{0,16},{1,13},{2,18},{3,15},{4,8},{5,21},{6,10},{7,23},{8,24},{9,5... | collective-permute-start | bytes 240008 | tf_op jit(solution)/shard_map/ppermute | solution.py:429
  19.6 1.2 %convert_element_type.36.table = bf16[200,1024]{1,0:T(8,128)(2,1)S(1)} convert(f32[200,1024]{1,0:T(8,128)} %bitcast.8) | non-fusion elementwise | flops 204800 | bytes 1228800 | tf_op jit(solution)/shard_map/convert_element_type | solution.py:479
  20.8 2.0 %slots.1 = (bf16[4,16,32,200]{3,2,1,0:T(8,128)(2,1)S(1)}, f32[4,8,256]{2,1,0:T(8,128)S(1)}, f32[4,1,1024]{2,1,0:T(1,128)S(1)}) custom-call(s32[8,256]{1,0:T(8,128)S(1)} %reshape.17.own, s32[8,256]{1,0:T(8,128)S(1)} %collective-permute-done.1.near, s32[8,256]{1,0:T(8,128)S(1)} %collective-permute-done.2.far, s32[8,256]{1,0:T(8,128)S(1)} %collective-permute-done.3.across, ...), custom_call_target="tpu_custom_call" | custom-call | flops 100000000 | bytes 1000000 | tf_op jit(solution)/shard_map/slots/pallas_call | solution.py:166
  22.9 1.8 %collective-permute-done.7.a4 = bf16[1,200,200]{2,1,0:T(8,128)(2,1)S(1)} collective-permute-done((bf16[1,200,200]{2,1,0:T(8,128)(2,1)S(1)}, bf16[1,200,200]{2,1,0:T(8,128)(2,1)S(1)}, u32[]{:S(2)}, u32[]{:S(2)}) %collective-permute-start.7) | collective-permute-done | bytes 80032 | tf_op jit(solution)/shard_map/ppermute | solution.py:429
  25.3 0.9 %ready.1.made_early = bf16[1024,200]{1,0:T(8,128)(2,1)S(1)} custom-call(bf16[2,200,200]{2,1,0:T(8,128)(2,1)S(1)} %convert_element_type.33.o0, bf16[2,200,200]{2,1,0:T(8,128)(2,1)S(1)} %collective-permute-done.a1, bf16[2,200,200]{2,1,0:T(8,128)(2,1)S(1)} %collective-permute-done.4.a2, bf16[2,200,200]{2,1,0:T(8,128)(2,1)S(1)} %collective-permute-done.8.b2, ...), custom_call_target="tpu_custom_call" | custom-call | flops 100000000 | bytes 1000000 | tf_op jit(solution)/shard_map/ready/pallas_call | solution.py:166
  26.6 3.9 %scores.1 = (bf16[320,128]{1,0:T(8,128)(2,1)S(1)}, bf16[320,128]{1,0:T(8,128)(2,1)S(1)}, bf16[320,128]{1,0:T(8,128)(2,1)S(1)}, bf16[320,128]{1,0:T(8,128)(2,1)S(...) custom-call(bf16[2,200,200]{2,1,0:T(8,128)(2,1)S(1)} %collective-permute-d, ...), custom_call_target="tpu_custom_call" | custom-call | flops 1000000000 | bytes 1000000 | tf_op jit(solution)/shard_map/scores/pallas_call | solution.py:166
  30.6 1.9 %collective-permute-start.13 = (bf16[320,128]{1,0:T(8,128)(2,1)S(1)}, bf16[320,128]{1,0:T(8,128)(2,1)S(1)}, u32[]{:S(2)}, u32[]{:S(2)}) collective-permute-start(bf16[320,128]{1,0:T(8,128)(2,1)S(1)} %get-tuple-element.69), channel_id=1, source_target_pairs={{0,20},{1,25},{2,30},{3,31},{4,28},{5,17},{6,26},{7,27},{8,12},{9,... | collective-permute-start | bytes 245768 | tf_op jit(solution)/shard_map/ppermute | solution.py:429
  32.4 2.0 %collective-permute-start.14 = (bf16[320,128]{1,0:T(8,128)(2,1)S(1)}, bf16[320,128]{1,0:T(8,128)(2,1)S(1)}, u32[]{:S(2)}, u32[]{:S(2)}) collective-permute-start(bf16[320,128]{1,0:T(8,128)(2,1)S(1)} %get-tuple-element.70), channel_id=1, source_target_pairs={{0,24},{1,21},{2,18},{3,15},{4,16},{5,29},{6,10},{7,23},{8,28},{9,... | collective-permute-start | bytes 245768 | tf_op jit(solution)/shard_map/ppermute | solution.py:429
  35.3 1.1 %targets.1 = bf16[200,512]{1,0:T(8,128)(2,1)S(1)} custom-call(f32[4,8,256]{2,1,0:T(8,128)S(1)} %get-tuple-element.61.rows, bf16[4,256,1024]{2,1,0:T(8,128)(2,1)S(1)} %get-tuple-element.66.weights, bf16[4,768,200]{2,1,0:T(8,128)(2,1)S(1)} %get-tuple-element.67.sides), custom_call_target="tpu_custom_call" | custom-call | flops 100000000 | bytes 1000000 | tf_op jit(solution)/shard_map/targets/pallas_call | solution.py:166
  36.5 2.4 %collective-permute-start.19 = (bf16[200,512]{1,0:T(8,128)(2,1)S(1)}, bf16[200,512]{1,0:T(8,128)(2,1)S(1)}, u32[]{:S(2)}, u32[]{:S(2)}) collective-permute-start(bf16[200,512]{1,0:T(8,128)(2,1)S(1)} %targets.1), channel_id=1, source_target_pairs={{0,4},{4,8},{8,12},{12,16},{16,20},{20,24},{24,28},{28,0},{1,5},{5... | collective-permute-start | bytes 614408 | tf_op jit(solution)/shard_map/ppermute | solution.py:22
  38.9 3.1 %sources.1.source_total = f32[200,1024]{1,0:T(8,128)S(1)} custom-call(bf16[2,200,200]{2,1,0:T(8,128)(2,1)S(1)} %convert_element_type.33.o0, bf16[2,200,200]{2,1,0:T(8,128)(2,1)S(1)} %collective-permute-done.a1, bf16[2,200,200]{2,1,0:T(8,128)(2,1)S(1)} %collective-permute-done.4.a2, bf16[2,200,200]{2,1,0:T(8,128)(2,1)S(1)} %collective-permute-done.6.a3, ...), custom_call_target="tpu_custom_call" | custom-call | flops 100000000 | bytes 1000000 | tf_op jit(solution)/shard_map/sources/pallas_call | solution.py:166
  42.6 4.0 %collective-permute-start.17 = (bf16[320,128]{1,0:T(8,128)(2,1)S(1)}, bf16[320,128]{1,0:T(8,128)(2,1)S(1)}, u32[]{:S(2)}, u32[]{:S(2)}) collective-permute-start(bf16[320,128]{1,0:T(8,128)(2,1)S(1)} %add_convert_fusion), channel_id=1, source_target_pairs={{0,2},{1,3},{2,0},{3,1},{4,6},{5,7},{6,4},{7,5},{8,10},{9,11},{10,... | collective-permute-start | bytes 245768 | tf_op jit(solution)/shard_map/ppermute | solution.py:418
  47.2 1.9 %collective-permute-done.17 = bf16[320,128]{1,0:T(8,128)(2,1)S(1)} collective-permute-done((bf16[320,128]{1,0:T(8,128)(2,1)S(1)}, bf16[320,128]{1,0:T(8,128)(2,1)S(1)}, u32[]{:S(2)}, u32[]{:S(2)}) %collective-permute-start.17) | collective-permute-done | bytes 81952 | tf_op jit(solution)/shard_map/ppermute | solution.py:418
  49.2 1.2 %entity_update.1 = (f32[200,1024]{1,0:T(8,128)}, f32[1,1024]{1,0:T(1,128)}) custom-call(f32[200,1024]{1,0:T(8,128)S(1)} %sources.1.source_total, bf16[200,512]{1,0:T(8,128)(2,1)S(1)} %collective-permute-done.19.mine, bf16[200,512]{1,0:T(8,128)(2,1)S(1)} %collective-permute-done.20.other, f32[200,1024]{1,0:T(8,128)S(1)} %bitcast.9, f32[1,1024]{1,0:T(1,128)S(1)} %bitcast.10), custom_call_target="tpu_custom_call" | custom-call | flops 1000000 | bytes 1000000 | tf_op jit(solution)/shard_map/entity_update/pallas_call | solution.py:166
  50.6 1.2 %operator_update.1 = (f32[2,200,200]{2,1,0:T(8,128)}, f32[2,200,200]{2,1,0:T(8,128)}) custom-call(f32[320,128]{1,0:T(8,128)S(1)} %convert_add_fusion.own, f32[320,128]{1,0:T(8,128)S(1)} %collective-permute-done.18.other, f32[2,200,200]{2,1,0:T(8,128)S(1)} %copy-done.1, f32[2,200,200]{2,1,0:T(8,128)S(1)} %copy-done.2), custom_call_target="tpu_custom_call" | custom-call | flops 1000000 | bytes 1000000 | tf_op jit(solution)/shard_map/operator_update/pallas_call | solution.py:166
  (42 shorter events, 4.7 us)
Async XLA Ops:
  1.7 8.2 %collective-permute-start = (bf16[2,200,200]{2,1,0:T(8,128)(2,1)S(1)}, bf16[2,200,200]{2,1,0:T(8,128)(2,1)S(1)}, u32[]{:S(2)}, u32[]{:S(2)}) collective-permute-start(bf16[2,200,200]{2,1,0:T(8,128)(2,1)S(1)} %convert_element_type.33.o0), channel_id=1, source_target_pairs={{0,8},{1,5},{2,10},{3,7},{4,0},{5,13},{6,2},{7,15},{8,16},{9,1},{1... | collective-permute-start | bytes 480008 | tf_op jit(solution)/shard_map/ppermute | solution.py:429
  5.6 3.1 %collective-permute-start.3 = (s32[8,256]{1,0:T(8,128)S(1)}, s32[8,256]{1,0:T(8,128)S(1)}, u32[]{:S(2)}, u32[]{:S(2)}) collective-permute-start(s32[8,256]{1,0:T(8,128)S(1)} %reshape.17.own), channel_id=1, source_target_pairs={{0,3},{1,2},{2,1},{3,0},{4,7},{5,6},{6,5},{7,4},{8,11},{9,10},{10,... | collective-permute-start | bytes 24584 | tf_op jit(solution)/shard_map/ppermute | solution.py:418
  6.1 3.7 %collective-permute-start.2 = (s32[8,256]{1,0:T(8,128)S(1)}, s32[8,256]{1,0:T(8,128)S(1)}, u32[]{:S(2)}, u32[]{:S(2)}) collective-permute-start(s32[8,256]{1,0:T(8,128)S(1)} %reshape.17.own), channel_id=1, source_target_pairs={{0,2},{1,3},{2,0},{3,1},{4,6},{5,7},{6,4},{7,5},{8,10},{9,11},{10,... | collective-permute-start | bytes 24584 | tf_op jit(solution)/shard_map/ppermute | solution.py:418
  7.1 2.7 %collective-permute-start.1 = (s32[8,256]{1,0:T(8,128)S(1)}, s32[8,256]{1,0:T(8,128)S(1)}, u32[]{:S(2)}, u32[]{:S(2)}) collective-permute-start(s32[8,256]{1,0:T(8,128)S(1)} %reshape.17.own), channel_id=1, source_target_pairs={{0,1},{1,0},{2,3},{3,2},{4,5},{5,4},{6,7},{7,6},{8,9},{9,8},{10,11... | collective-permute-start | bytes 24584 | tf_op jit(solution)/shard_map/ppermute | solution.py:418
  9.8 1.5 %collective-permute-start.5 = (bf16[2,200,200]{2,1,0:T(8,128)(2,1)S(1)}, bf16[2,200,200]{2,1,0:T(8,128)(2,1)S(1)}, u32[]{:S(2)}, u32[]{:S(2)}) collective-permute-start(bf16[2,200,200]{2,1,0:T(8,128)(2,1)S(1)} %collective-permute-done.a1), channel_id=1, source_target_pairs={{0,1},{1,0},{2,3},{3,2},{4,5},{5,4},{6,7},{7,6},{8,9},{9,8},{10,11... | collective-permute-start | bytes 480008 | tf_op jit(solution)/shard_map/ppermute | solution.py:418
  9.9 7.3 %collective-permute-start.4 = (bf16[2,200,200]{2,1,0:T(8,128)(2,1)S(1)}, bf16[2,200,200]{2,1,0:T(8,128)(2,1)S(1)}, u32[]{:S(2)}, u32[]{:S(2)}) collective-permute-start(bf16[2,200,200]{2,1,0:T(8,128)(2,1)S(1)} %collective-permute-done.a1), channel_id=1, source_target_pairs={{0,8},{1,5},{2,10},{3,7},{4,0},{5,13},{6,2},{7,15},{8,16},{9,1},{1... | collective-permute-start | bytes 480008 | tf_op jit(solution)/shard_map/ppermute | solution.py:429
  11.3 13.4 %collective-permute-start.9 = (bf16[200,512]{1,0:T(8,128)(2,1)S(1)}, bf16[200,512]{1,0:T(8,128)(2,1)S(1)}, u32[]{:S(2)}, u32[]{:S(2)}) collective-permute-start(bf16[200,512]{1,0:T(8,128)(2,1)S(1)} %fusion), channel_id=1, source_target_pairs={{0,28},{4,0},{8,4},{12,8},{16,12},{20,16},{24,20},{28,24},{1,29},{... | collective-permute-start | bytes 614408 | tf_op jit(solution)/shard_map/ppermute | solution.py:22
  17.2 7.4 %collective-permute-start.8 = (bf16[2,200,200]{2,1,0:T(8,128)(2,1)S(1)}, bf16[2,200,200]{2,1,0:T(8,128)(2,1)S(1)}, u32[]{:S(2)}, u32[]{:S(2)}) collective-permute-start(bf16[2,200,200]{2,1,0:T(8,128)(2,1)S(1)} %collective-permute-done.4.a2), channel_id=1, source_target_pairs={{0,1},{1,0},{2,3},{3,2},{4,5},{5,4},{6,7},{7,6},{8,9},{9,8},{10,11... | collective-permute-start | bytes 480008 | tf_op jit(solution)/shard_map/ppermute | solution.py:418
  17.2 7.4 %collective-permute-start.6 = (bf16[2,200,200]{2,1,0:T(8,128)(2,1)S(1)}, bf16[2,200,200]{2,1,0:T(8,128)(2,1)S(1)}, u32[]{:S(2)}, u32[]{:S(2)}) collective-permute-start(bf16[2,200,200]{2,1,0:T(8,128)(2,1)S(1)} %collective-permute-done.4.a2), channel_id=1, source_target_pairs={{0,8},{1,5},{2,10},{3,7},{4,0},{5,13},{6,2},{7,15},{8,16},{9,1},{1... | collective-permute-start | bytes 480008 | tf_op jit(solution)/shard_map/ppermute | solution.py:429
  17.2 7.4 %collective-permute-start.7 = (bf16[1,200,200]{2,1,0:T(8,128)(2,1)S(1)}, bf16[1,200,200]{2,1,0:T(8,128)(2,1)S(1)}, u32[]{:S(2)}, u32[]{:S(2)}) collective-permute-start(bf16[1,200,200]{2,1,0:T(8,128)(2,1)S(1)} %constant_dynamic-slice_fusion), channel_id=1, source_target_pairs={{0,16},{1,13},{2,18},{3,15},{4,8},{5,21},{6,10},{7,23},{8,24},{9,5... | collective-permute-start | bytes 240008 | tf_op jit(solution)/shard_map/ppermute | solution.py:429
  24.7 2.0 %collective-permute-start.12 = (bf16[200,512]{1,0:T(8,128)(2,1)S(1)}, bf16[200,512]{1,0:T(8,128)(2,1)S(1)}, u32[]{:S(2)}, u32[]{:S(2)}) collective-permute-start(bf16[200,512]{1,0:T(8,128)(2,1)S(1)} %collective-permute-done.9.mine), channel_id=1, source_target_pairs={{0,1},{1,0},{2,3},{3,2},{4,5},{5,4},{6,7},{7,6},{8,9},{9,8},{10,11... | collective-permute-start | bytes 614408 | tf_op jit(solution)/shard_map/ppermute | solution.py:418
  24.7 1.9 %collective-permute-start.11 = (bf16[2,200,200]{2,1,0:T(8,128)(2,1)S(1)}, bf16[2,200,200]{2,1,0:T(8,128)(2,1)S(1)}, u32[]{:S(2)}, u32[]{:S(2)}) collective-permute-start(bf16[2,200,200]{2,1,0:T(8,128)(2,1)S(1)} %collective-permute-done.6.a3), channel_id=1, source_target_pairs={{0,1},{1,0},{2,3},{3,2},{4,5},{5,4},{6,7},{7,6},{8,9},{9,8},{10,11... | collective-permute-start | bytes 480008 | tf_op jit(solution)/shard_map/ppermute | solution.py:418
  25.2 1.4 %collective-permute-start.10 = (bf16[1,200,200]{2,1,0:T(8,128)(2,1)S(1)}, bf16[1,200,200]{2,1,0:T(8,128)(2,1)S(1)}, u32[]{:S(2)}, u32[]{:S(2)}) collective-permute-start(bf16[1,200,200]{2,1,0:T(8,128)(2,1)S(1)} %collective-permute-done.7.a4), channel_id=1, source_target_pairs={{0,1},{1,0},{2,3},{3,2},{4,5},{5,4},{6,7},{7,6},{8,9},{9,8},{10,11... | collective-permute-start | bytes 240008 | tf_op jit(solution)/shard_map/ppermute | solution.py:418
  30.6 11.4 %collective-permute-start.13 = (bf16[320,128]{1,0:T(8,128)(2,1)S(1)}, bf16[320,128]{1,0:T(8,128)(2,1)S(1)}, u32[]{:S(2)}, u32[]{:S(2)}) collective-permute-start(bf16[320,128]{1,0:T(8,128)(2,1)S(1)} %get-tuple-element.69), channel_id=1, source_target_pairs={{0,20},{1,25},{2,30},{3,31},{4,28},{5,17},{6,26},{7,27},{8,12},{9,... | collective-permute-start | bytes 245768 | tf_op jit(solution)/shard_map/ppermute | solution.py:429
  32.4 9.6 %collective-permute-start.14 = (bf16[320,128]{1,0:T(8,128)(2,1)S(1)}, bf16[320,128]{1,0:T(8,128)(2,1)S(1)}, u32[]{:S(2)}, u32[]{:S(2)}) collective-permute-start(bf16[320,128]{1,0:T(8,128)(2,1)S(1)} %get-tuple-element.70), channel_id=1, source_target_pairs={{0,24},{1,21},{2,18},{3,15},{4,16},{5,29},{6,10},{7,23},{8,28},{9,... | collective-permute-start | bytes 245768 | tf_op jit(solution)/shard_map/ppermute | solution.py:429
  34.4 8.2 %collective-permute-start.15 = (bf16[320,128]{1,0:T(8,128)(2,1)S(1)}, bf16[320,128]{1,0:T(8,128)(2,1)S(1)}, u32[]{:S(2)}, u32[]{:S(2)}) collective-permute-start(bf16[320,128]{1,0:T(8,128)(2,1)S(1)} %get-tuple-element.71), channel_id=1, source_target_pairs={{0,12},{1,17},{2,6},{3,11},{4,20},{5,9},{6,14},{7,3},{8,4},{9,25},... | collective-permute-start | bytes 245768 | tf_op jit(solution)/shard_map/ppermute | solution.py:429
  34.6 7.9 %collective-permute-start.16 = (bf16[320,128]{1,0:T(8,128)(2,1)S(1)}, bf16[320,128]{1,0:T(8,128)(2,1)S(1)}, u32[]{:S(2)}, u32[]{:S(2)}) collective-permute-start(bf16[320,128]{1,0:T(8,128)(2,1)S(1)} %get-tuple-element.72), channel_id=1, source_target_pairs={{0,0},{1,1},{2,10},{3,7},{4,4},{5,5},{6,2},{7,15},{8,8},{9,9},{10,... | collective-permute-start | bytes 245768 | tf_op jit(solution)/shard_map/ppermute | solution.py:429
  36.5 12.7 %copy-start = (f32[1024,200]{0,1:T(8,128)S(1)}, f32[1024,200]{0,1:T(8,128)}, u32[]{:S(2)}) copy-start(f32[1024,200]{0,1:T(8,128)} %param.8) | copy-start | bytes 2457604
  36.5 12.7 %copy-start.3 = (f32[1024]{0:T(1024)S(1)}, f32[1024]{0:T(1024)}, u32[]{:S(2)}) copy-start(f32[1024]{0:T(1024)} %param.9) | copy-start | bytes 12292
  36.5 10.2 %collective-permute-start.19 = (bf16[200,512]{1,0:T(8,128)(2,1)S(1)}, bf16[200,512]{1,0:T(8,128)(2,1)S(1)}, u32[]{:S(2)}, u32[]{:S(2)}) collective-permute-start(bf16[200,512]{1,0:T(8,128)(2,1)S(1)} %targets.1), channel_id=1, source_target_pairs={{0,4},{4,8},{8,12},{12,16},{16,20},{20,24},{24,28},{28,0},{1,5},{5... | collective-permute-start | bytes 614408 | tf_op jit(solution)/shard_map/ppermute | solution.py:22
  42.0 8.6 %copy-start.1 = (f32[2,200,200]{2,1,0:T(8,128)S(1)}, f32[2,200,200]{2,1,0:T(8,128)}, u32[]{:S(2)}) copy-start(f32[2,200,200]{2,1,0:T(8,128)} %operators.1) | copy-start | bytes 960004
  42.6 6.5 %collective-permute-start.17 = (bf16[320,128]{1,0:T(8,128)(2,1)S(1)}, bf16[320,128]{1,0:T(8,128)(2,1)S(1)}, u32[]{:S(2)}, u32[]{:S(2)}) collective-permute-start(bf16[320,128]{1,0:T(8,128)(2,1)S(1)} %add_convert_fusion), channel_id=1, source_target_pairs={{0,2},{1,3},{2,0},{3,1},{4,6},{5,7},{6,4},{7,5},{8,10},{9,11},{10,... | collective-permute-start | bytes 245768 | tf_op jit(solution)/shard_map/ppermute | solution.py:418
  46.7 2.5 %collective-permute-start.20 = (bf16[200,512]{1,0:T(8,128)(2,1)S(1)}, bf16[200,512]{1,0:T(8,128)(2,1)S(1)}, u32[]{:S(2)}, u32[]{:S(2)}) collective-permute-start(bf16[200,512]{1,0:T(8,128)(2,1)S(1)} %collective-permute-done.19.mine), channel_id=1, source_target_pairs={{0,1},{1,0},{2,3},{3,2},{4,5},{5,4},{6,7},{7,6},{8,9},{9,8},{10,11... | collective-permute-start | bytes 614408 | tf_op jit(solution)/shard_map/ppermute | solution.py:418
  49.1 1.5 %collective-permute-start.18 = (f32[320,128]{1,0:T(8,128)S(1)}, f32[320,128]{1,0:T(8,128)S(1)}, u32[]{:S(2)}, u32[]{:S(2)}) collective-permute-start(f32[320,128]{1,0:T(8,128)S(1)} %convert_add_fusion.own), channel_id=1, source_target_pairs={{0,1},{1,0},{2,3},{3,2},{4,5},{5,4},{6,7},{7,6},{8,9},{9,8},{10,11... | collective-permute-start | bytes 491528 | tf_op jit(solution)/shard_map/ppermute | solution.py:418
  (1 other events, 8.6 us)

commit v8 on v7

--- a/solution.py
+++ b/solution.py
@@ -255,22 +255,38 @@
     moved[:, at] = dot(given, op).astype(bf16).reshape(reps, SLOTS, width)
 
 
-def ready_kernel(o0, a1, a2, b2, b1, slotted, rows, made_early, moved):
+def handed_places(core, me):
+    handed = []
+    for near, far in OFFSETS:
+        offset = jnp.where(me < CORES, near, far)
+        handed.append(2 * offset + jnp.where(offset == len(RING) // 2, 0, core))
+    return handed
+
+
+def ready_kernel(o0, a1, a2, b2, b1, slotted, rows, mine, made_early, target_early, turned, moved):
     reps, _, edges = rows.shape
     places, width = slotted.shape[1], slotted.shape[3]
+    core, me, *_ = position()
+    half = mine.shape[1]
+    aimed = []
     moved[:, LATE[0] : LATE[1]] = jnp.zeros((reps, LATE[1] - LATE[0], SLOTS, width), bf16)
     for place, op in enumerate(operator_list(o0, a1, a2, None, None, None, None, b2, b1)):
         if op is not None:
             transform(moved, slotted, place, place, op())
     for b in range(reps):
-        slot = rows[b].T[:, 2:3].astype(jnp.int32)
-        out_of = one_hot(lanes_of((edges, places * SLOTS)) == slot)
+        standing = rows[b].T.astype(jnp.int32)
+        out_of = one_hot(lanes_of((edges, places * SLOTS)) == standing[:, 2:3])
         made = dot(out_of, moved[b].reshape(places * SLOTS, width))
         made_early[b * edges : (b + 1) * edges] = made.astype(bf16)
+        aimed.append(lanes_of((edges, half)) + core * half == standing[:, 1:2])
+    target_early[...] = dot(one_hot(jnp.concatenate(aimed, axis=0)), mine[...], NT).astype(bf16)
+    for k, place in enumerate(handed_places(core, me)):
+        given = slotted[:, pl.ds(place, 1)].reshape(reps * SLOTS, width)
+        turned[k] = given.astype(f32).T.astype(bf16)
 
 
 def score_kernel(
-    negative_count, a3, a4, b4, b3, slotted, rows, counts, mine, other, made_early,
+    negative_count, a3, a4, b4, b3, slotted, rows, counts, mine, other, made_early, target_early, turned,
     s0, s1, s2, s3, weights, sides, query, table, moved, asking,
 ):
     core, me, *_ = position()
@@ -282,10 +298,7 @@
         if op is not None:
             transform(moved, slotted, place, place - LATE[0], op())
     sent = (s0, s1, s2, s3)
-    handed = []
-    for near, far in OFFSETS:
-        offset = jnp.where(me < CORES, near, far)
-        handed.append(2 * offset + jnp.where(offset == len(RING) // 2, 0, core))
+    handed = handed_places(core, me)
     lying = [rows[b] for b in range(reps)]
     standing = [block.T.astype(jnp.int32) for block in lying]
     made = []
@@ -295,18 +308,18 @@
         made.append(dot(out_of, moved[b].reshape(late, width)))
     made = jnp.concatenate(made, axis=0) + made_early[...].astype(f32)
     made_half = made.astype(bf16)
-    scores = dot(made_half, table[...])
-    aimed = lanes_of((reps * edges, entities)) == jnp.concatenate(
-        [block[:, 1:2] for block in standing], axis=0
-    )
-    positive = jnp.sum(jnp.where(aimed, scores, 0.0), axis=1, keepdims=True)
+    half = other.shape[1]
+    ends = jnp.concatenate([block[:, 1:2] for block in standing], axis=0)
+    far_aimed = one_hot(lanes_of((reps * edges, half)) + (1 - core) * half == ends)
+    target_rows = target_early[...].astype(f32) + dot(far_aimed, other[...], NT)
+    positive = jnp.sum(made * target_rows, axis=1, keepdims=True)
     positive_grad = -(0.5 * jnp.tanh(-0.5 * positive) + 0.5)
-    share = (0.5 * jnp.tanh(0.5 * scores) + 0.5) * (1.0 / negative_count)
-    share = share.astype(bf16).astype(f32)
+    scale = 0.5 / negative_count
+    share = jnp.tanh(dot((0.5 * made).astype(bf16), table[...])) * scale + scale
+    share = share.astype(bf16)
     weighted = jnp.concatenate(
-        [share[b * edges : (b + 1) * edges] * counts[b] for b in range(reps)], axis=0
-    ).astype(bf16)
-    target_rows = dot(one_hot(aimed), table[...], NT)
+        [share[b * edges : (b + 1) * edges] * counts[b].astype(bf16) for b in range(reps)], axis=0
+    )
     asked = (positive_grad * target_rows + dot(weighted, table[...], NT)).astype(bf16)
     push = positive_grad * made
     push_half = push.astype(bf16)
@@ -323,9 +336,8 @@
             [one_hot(rows_of((SLOTS, edges)) + place * SLOTS == slot) for place in handed], axis=0
         )
         asking[b] = dot(into, asked[at]).astype(bf16).reshape(len(sent), SLOTS, width)
-    for k, place in enumerate(handed):
-        given = slotted[:, pl.ds(place, 1)].reshape(reps * SLOTS, width)
-        sent[k][...] = packed(dot(given, asking[:, k].reshape(reps * SLOTS, width), TN)).astype(bf16)
+    for k in range(len(sent)):
+        sent[k][...] = packed(dot(turned[k], asking[:, k].reshape(reps * SLOTS, width))).astype(bf16)
 
 
 def packed(matrix):
@@ -483,10 +495,11 @@
     other = rep_swapped(mine, 1)
     b3 = rep_swapped(a3, 1)
     b4 = rep_swapped(a4, 1)
-    (made_early,) = call(
+    early = call(
         ready_kernel,
-        [jax.ShapeDtypeStruct((reps * edges, width), bf16)],
-        "ready", 10**8, 10**6, (operators_half, a1, a2, b2, b1, slotted, rows),
+        [jax.ShapeDtypeStruct((reps * edges, width), bf16)] * 2
+        + [jax.ShapeDtypeStruct((len(OFFSETS), width, reps * SLOTS), bf16)],
+        "ready", 10**8, 10**6, (operators_half, a1, a2, b2, b1, slotted, rows, mine),
         scratch=[VMEM((reps, places, SLOTS, width), bf16)],
     )
     gathered = (operators_half, a1, a2, a3, a4, b4, b3, b2, b1)
@@ -498,7 +511,7 @@
     ]
     *handed, weights, sides, query = call(
         functools.partial(score_kernel, negatives.shape[1]), score_out, "scores", 10**9, 10**6,
-        (a3, a4, b4, b3, slotted, rows, counts, mine, other, made_early),
+        (a3, a4, b4, b3, slotted, rows, counts, mine, other, *early),
         scratch=[
             VMEM((width, entities), bf16),
             VMEM((reps, LATE[1] - LATE[0], SLOTS, width), bf16),

time: 52.4 us -> 51.5 us (0.983)
  transfers between devices with their start and end apart: 21 -> 21, of which waited for: 8 -> 9; matrix products, arithmetic and copies ran while one was open for 6% -> 6% of each run, Pallas kernels for 16% -> 17%
where the time goes in v8:
time: 51.5 us; the launch traced here: 50.8 us
  starting transfers between devices  24.5 us (48%)
  Pallas kernels  12.9 us (25%)
  waiting for transfers between devices  8.43 us (16%)
  other arithmetic  2.29 us (4%)
  local copies, waits for them, and re-layouts  1.88 us (4%)
  between operations  0.8 us (2%)
    pallas_call x7, Pallas kernels, call(): pl.pallas_call(body, out_shape=outs, in_specs=[whole] * len(operands), ou...  12.9 us
    ppermute x8, starting transfers between devices, along_ring(): return lax.ppermute(array, ('ent', 'rep'), pairs)  11.5 us
    ppermute x11, starting transfers between devices, rep_swapped(): return lax.ppermute(array, 'rep', [(i, i ^ by) for i in range(peers)])  7.11 us
    ppermute x2, starting transfers between devices, passed_along(): lax.ppermute(array, axis, [(i, (i + by) % peers) for i in range(peers)])  5.87 us
    ppermute x8, waiting for transfers between devices, along_ring(): return lax.ppermute(array, ('ent', 'rep'), pairs)  4.9 us
    ppermute x11, waiting for transfers between devices, rep_swapped(): return lax.ppermute(array, 'rep', [(i, i ^ by) for i in range(peers)])  3.43 us
    convert_element_type x1, other arithmetic, gathered_shards(): table_half = late_table.astype(bf16)  1.2 us
  transfers between devices with their start and end apart: 21, of which 9 were waited for; matrix products, arithmetic and copies ran while one was open for 6% of the time, Pallas kernels for 17%

profile of v8, /device:TPU:0, one launch (start us, length us, event | category | flops | bytes accessed | tf_op | source)
XLA Modules:
  0.0 50.8 jit_solution(9873823660711310467)
XLA Ops:
  0.6 1.0 %convert_element_type.33.o0 = bf16[2,200,200]{2,1,0:T(8,128)(2,1)S(1)} convert(f32[2,200,200]{2,1,0:T(8,128)} %operators.1) | non-fusion elementwise | flops 80000 | bytes 480000 | tf_op jit(solution)/shard_map/convert_element_type | solution.py:462
  1.7 3.1 %collective-permute-start = (bf16[2,200,200]{2,1,0:T(8,128)(2,1)S(1)}, bf16[2,200,200]{2,1,0:T(8,128)(2,1)S(1)}, u32[]{:S(2)}, u32[]{:S(2)}) collective-permute-start(bf16[2,200,200]{2,1,0:T(8,128)(2,1)S(1)} %convert_element_type.33.o0), channel_id=1, source_target_pairs={{0,8},{1,5},{2,10},{3,7},{4,0},{5,13},{6,2},{7,15},{8,16},{9,1},{1... | collective-permute-start | bytes 480008 | tf_op jit(solution)/shard_map/ppermute | solution.py:441
  6.1 1.0 %collective-permute-start.2 = (s32[8,256]{1,0:T(8,128)S(1)}, s32[8,256]{1,0:T(8,128)S(1)}, u32[]{:S(2)}, u32[]{:S(2)}) collective-permute-start(s32[8,256]{1,0:T(8,128)S(1)} %reshape.17.own), channel_id=1, source_target_pairs={{0,2},{1,3},{2,0},{3,1},{4,6},{5,7},{6,4},{7,5},{8,10},{9,11},{10,... | collective-permute-start | bytes 24584 | tf_op jit(solution)/shard_map/ppermute | solution.py:430
  7.4 1.0 %fusion = bf16[200,512]{1,0:T(8,128)(2,1)S(1)} fusion(f32[1024,200]{0,1:T(8,128)} %param.8, s32[]{:T(128)S(6)} %select_n.14), kind=kLoop, calls=%fused_computation.1 | loop fusion | bytes 409604 | tf_op jit(solution)/shard_map/convert_element_type | solution.py:481
  8.6 1.2 %collective-permute-done.2.far = s32[8,256]{1,0:T(8,128)S(1)} collective-permute-done((s32[8,256]{1,0:T(8,128)S(1)}, s32[8,256]{1,0:T(8,128)S(1)}, u32[]{:S(2)}, u32[]{:S(2)}) %collective-permute-start.2) | collective-permute-done | bytes 8224 | tf_op jit(solution)/shard_map/ppermute | solution.py:430
  9.9 1.3 %collective-permute-start.4 = (bf16[2,200,200]{2,1,0:T(8,128)(2,1)S(1)}, bf16[2,200,200]{2,1,0:T(8,128)(2,1)S(1)}, u32[]{:S(2)}, u32[]{:S(2)}) collective-permute-start(bf16[2,200,200]{2,1,0:T(8,128)(2,1)S(1)} %collective-permute-done.a1), channel_id=1, source_target_pairs={{0,8},{1,5},{2,10},{3,7},{4,0},{5,13},{6,2},{7,15},{8,16},{9,1},{1... | collective-permute-start | bytes 480008 | tf_op jit(solution)/shard_map/ppermute | solution.py:441
  11.3 3.7 %collective-permute-start.9 = (bf16[200,512]{1,0:T(8,128)(2,1)S(1)}, bf16[200,512]{1,0:T(8,128)(2,1)S(1)}, u32[]{:S(2)}, u32[]{:S(2)}) collective-permute-start(bf16[200,512]{1,0:T(8,128)(2,1)S(1)} %fusion), channel_id=1, source_target_pairs={{0,28},{4,0},{8,4},{12,8},{16,12},{20,16},{24,20},{28,24},{1,29},{... | collective-permute-start | bytes 614408 | tf_op jit(solution)/shard_map/ppermute | solution.py:22
  14.9 2.3 %collective-permute-done.4.a2 = bf16[2,200,200]{2,1,0:T(8,128)(2,1)S(1)} collective-permute-done((bf16[2,200,200]{2,1,0:T(8,128)(2,1)S(1)}, bf16[2,200,200]{2,1,0:T(8,128)(2,1)S(1)}, u32[]{:S(2)}, u32[]{:S(2)}) %collective-permute-start.4) | collective-permute-done | bytes 160032 | tf_op jit(solution)/shard_map/ppermute | solution.py:441
  17.2 2.4 %collective-permute-start.7 = (bf16[1,200,200]{2,1,0:T(8,128)(2,1)S(1)}, bf16[1,200,200]{2,1,0:T(8,128)(2,1)S(1)}, u32[]{:S(2)}, u32[]{:S(2)}) collective-permute-start(bf16[1,200,200]{2,1,0:T(8,128)(2,1)S(1)} %constant_dynamic-slice_fusion), channel_id=1, source_target_pairs={{0,16},{1,13},{2,18},{3,15},{4,8},{5,21},{6,10},{7,23},{8,24},{9,5... | collective-permute-start | bytes 240008 | tf_op jit(solution)/shard_map/ppermute | solution.py:441
  19.6 1.2 %convert_element_type.36.table = bf16[200,1024]{1,0:T(8,128)(2,1)S(1)} convert(f32[200,1024]{1,0:T(8,128)} %bitcast.8) | non-fusion elementwise | flops 204800 | bytes 1228800 | tf_op jit(solution)/shard_map/convert_element_type | solution.py:491
  20.8 2.0 %slots.1 = (bf16[4,16,32,200]{3,2,1,0:T(8,128)(2,1)S(1)}, f32[4,8,256]{2,1,0:T(8,128)S(1)}, f32[4,1,1024]{2,1,0:T(1,128)S(1)}) custom-call(s32[8,256]{1,0:T(8,128)S(1)} %reshape.17.own, s32[8,256]{1,0:T(8,128)S(1)} %collective-permute-done.1.near, s32[8,256]{1,0:T(8,128)S(1)} %collective-permute-done.2.far, s32[8,256]{1,0:T(8,128)S(1)} %collective-permute-done.3.across, ...), custom_call_target="tpu_custom_call" | custom-call | flops 100000000 | bytes 1000000 | tf_op jit(solution)/shard_map/slots/pallas_call | solution.py:166
  22.9 1.8 %collective-permute-done.7.a4 = bf16[1,200,200]{2,1,0:T(8,128)(2,1)S(1)} collective-permute-done((bf16[1,200,200]{2,1,0:T(8,128)(2,1)S(1)}, bf16[1,200,200]{2,1,0:T(8,128)(2,1)S(1)}, u32[]{:S(2)}, u32[]{:S(2)}) %collective-permute-start.7) | collective-permute-done | bytes 80032 | tf_op jit(solution)/shard_map/ppermute | solution.py:441
  25.3 1.1 %ready.1 = (bf16[1024,200]{1,0:T(8,128)(2,1)S(1)}, bf16[1024,200]{1,0:T(8,128)(2,1)S(1)}, bf16[4,200,128]{2,1,0:T(8,128)(2,1)S(1)}) custom-call(bf16[2,200,200]{2,1,0:T(8,128)(2,1)S(1)} %convert_element_type.33.o0, bf16[2,200,200]{2,1,0:T(8,128)(2,1)S(1)} %collective-permute-done.a1, bf16[2,200,200]{2,1,0:T(8,128)(2,1)S(1)} %collective-permute-done.4.a2, ...), custom_call_target="tpu_custom_call" | custom-call | flops 100000000 | bytes 1000000 | tf_op jit(solution)/shard_map/ready/pallas_call | solution.py:166
  26.6 3.1 %scores.1 = (bf16[320,128]{1,0:T(8,128)(2,1)S(1)}, bf16[320,128]{1,0:T(8,128)(2,1)S(1)}, bf16[320,128]{1,0:T(8,128)(2,1)S(1)}, bf16[320,128]{1,0:T(8,128)(2,1)S(...) custom-call(bf16[2,200,200]{2,1,0:T(8,128)(2,1)S(1)} %collective-permute-d, ...), custom_call_target="tpu_custom_call" | custom-call | flops 1000000000 | bytes 1000000 | tf_op jit(solution)/shard_map/scores/pallas_call | solution.py:166
  29.8 1.9 %collective-permute-start.13 = (bf16[320,128]{1,0:T(8,128)(2,1)S(1)}, bf16[320,128]{1,0:T(8,128)(2,1)S(1)}, u32[]{:S(2)}, u32[]{:S(2)}) collective-permute-start(bf16[320,128]{1,0:T(8,128)(2,1)S(1)} %get-tuple-element.75), channel_id=1, source_target_pairs={{0,20},{1,25},{2,30},{3,31},{4,28},{5,17},{6,26},{7,27},{8,12},{9,... | collective-permute-start | bytes 245768 | tf_op jit(solution)/shard_map/ppermute | solution.py:441
  31.6 2.0 %collective-permute-start.14 = (bf16[320,128]{1,0:T(8,128)(2,1)S(1)}, bf16[320,128]{1,0:T(8,128)(2,1)S(1)}, u32[]{:S(2)}, u32[]{:S(2)}) collective-permute-start(bf16[320,128]{1,0:T(8,128)(2,1)S(1)} %get-tuple-element.76), channel_id=1, source_target_pairs={{0,24},{1,21},{2,18},{3,15},{4,16},{5,29},{6,10},{7,23},{8,28},{9,... | collective-permute-start | bytes 245768 | tf_op jit(solution)/shard_map/ppermute | solution.py:441
  34.5 1.2 %targets.1 = bf16[200,512]{1,0:T(8,128)(2,1)S(1)} custom-call(f32[4,8,256]{2,1,0:T(8,128)S(1)} %get-tuple-element.64.rows, bf16[4,256,1024]{2,1,0:T(8,128)(2,1)S(1)} %get-tuple-element.72.weights, bf16[4,768,200]{2,1,0:T(8,128)(2,1)S(1)} %get-tuple-element.73.sides), custom_call_target="tpu_custom_call" | custom-call | flops 100000000 | bytes 1000000 | tf_op jit(solution)/shard_map/targets/pallas_call | solution.py:166
  35.7 2.2 %collective-permute-start.19 = (bf16[200,512]{1,0:T(8,128)(2,1)S(1)}, bf16[200,512]{1,0:T(8,128)(2,1)S(1)}, u32[]{:S(2)}, u32[]{:S(2)}) collective-permute-start(bf16[200,512]{1,0:T(8,128)(2,1)S(1)} %targets.1), channel_id=1, source_target_pairs={{0,4},{4,8},{8,12},{12,16},{16,20},{20,24},{24,28},{28,0},{1,5},{5... | collective-permute-start | bytes 614408 | tf_op jit(solution)/shard_map/ppermute | solution.py:22
  37.9 3.1 %sources.1.source_total = f32[200,1024]{1,0:T(8,128)S(1)} custom-call(bf16[2,200,200]{2,1,0:T(8,128)(2,1)S(1)} %convert_element_type.33.o0, bf16[2,200,200]{2,1,0:T(8,128)(2,1)S(1)} %collective-permute-done.a1, bf16[2,200,200]{2,1,0:T(8,128)(2,1)S(1)} %collective-permute-done.4.a2, bf16[2,200,200]{2,1,0:T(8,128)(2,1)S(1)} %collective-permute-done.6.a3, ...), custom_call_target="tpu_custom_call" | custom-call | flops 100000000 | bytes 1000000 | tf_op jit(solution)/shard_map/sources/pallas_call | solution.py:166
  41.0 0.8 %collective-permute-done.15 = bf16[320,128]{1,0:T(8,128)(2,1)S(1)} collective-permute-done((bf16[320,128]{1,0:T(8,128)(2,1)S(1)}, bf16[320,128]{1,0:T(8,128)(2,1)S(1)}, u32[]{:S(2)}, u32[]{:S(2)}) %collective-permute-start.15) | collective-permute-done | bytes 81952 | tf_op jit(solution)/shard_map/ppermute | solution.py:441
  41.9 3.8 %collective-permute-start.17 = (bf16[320,128]{1,0:T(8,128)(2,1)S(1)}, bf16[320,128]{1,0:T(8,128)(2,1)S(1)}, u32[]{:S(2)}, u32[]{:S(2)}) collective-permute-start(bf16[320,128]{1,0:T(8,128)(2,1)S(1)} %add_convert_fusion), channel_id=1, source_target_pairs={{0,2},{1,3},{2,0},{3,1},{4,6},{5,7},{6,4},{7,5},{8,10},{9,11},{10,... | collective-permute-start | bytes 245768 | tf_op jit(solution)/shard_map/ppermute | solution.py:430
  46.4 1.7 %collective-permute-done.17 = bf16[320,128]{1,0:T(8,128)(2,1)S(1)} collective-permute-done((bf16[320,128]{1,0:T(8,128)(2,1)S(1)}, bf16[320,128]{1,0:T(8,128)(2,1)S(1)}, u32[]{:S(2)}, u32[]{:S(2)}) %collective-permute-start.17) | collective-permute-done | bytes 81952 | tf_op jit(solution)/shard_map/ppermute | solution.py:430
  48.2 1.2 %entity_update.1 = (f32[200,1024]{1,0:T(8,128)}, f32[1,1024]{1,0:T(1,128)}) custom-call(f32[200,1024]{1,0:T(8,128)S(1)} %sources.1.source_total, bf16[200,512]{1,0:T(8,128)(2,1)S(1)} %collective-permute-done.19.mine, bf16[200,512]{1,0:T(8,128)(2,1)S(1)} %collective-permute-done.20.other, f32[200,1024]{1,0:T(8,128)S(1)} %bitcast.9, f32[1,1024]{1,0:T(1,128)S(1)} %bitcast.10), custom_call_target="tpu_custom_call" | custom-call | flops 1000000 | bytes 1000000 | tf_op jit(solution)/shard_map/entity_update/pallas_call | solution.py:166
  49.6 1.2 %operator_update.1 = (f32[2,200,200]{2,1,0:T(8,128)}, f32[2,200,200]{2,1,0:T(8,128)}) custom-call(f32[320,128]{1,0:T(8,128)S(1)} %convert_add_fusion.own, f32[320,128]{1,0:T(8,128)S(1)} %collective-permute-done.18.other, f32[2,200,200]{2,1,0:T(8,128)S(1)} %copy-done.1, f32[2,200,200]{2,1,0:T(8,128)S(1)} %copy-done.2), custom_call_target="tpu_custom_call" | custom-call | flops 1000000 | bytes 1000000 | tf_op jit(solution)/shard_map/operator_update/pallas_call | solution.py:166
  (42 shorter events, 4.9 us)
Async XLA Ops:
  1.7 8.2 %collective-permute-start = (bf16[2,200,200]{2,1,0:T(8,128)(2,1)S(1)}, bf16[2,200,200]{2,1,0:T(8,128)(2,1)S(1)}, u32[]{:S(2)}, u32[]{:S(2)}) collective-permute-start(bf16[2,200,200]{2,1,0:T(8,128)(2,1)S(1)} %convert_element_type.33.o0), channel_id=1, source_target_pairs={{0,8},{1,5},{2,10},{3,7},{4,0},{5,13},{6,2},{7,15},{8,16},{9,1},{1... | collective-permute-start | bytes 480008 | tf_op jit(solution)/shard_map/ppermute | solution.py:441
  5.6 3.1 %collective-permute-start.3 = (s32[8,256]{1,0:T(8,128)S(1)}, s32[8,256]{1,0:T(8,128)S(1)}, u32[]{:S(2)}, u32[]{:S(2)}) collective-permute-start(s32[8,256]{1,0:T(8,128)S(1)} %reshape.17.own), channel_id=1, source_target_pairs={{0,3},{1,2},{2,1},{3,0},{4,7},{5,6},{6,5},{7,4},{8,11},{9,10},{10,... | collective-permute-start | bytes 24584 | tf_op jit(solution)/shard_map/ppermute | solution.py:430
  6.1 3.7 %collective-permute-start.2 = (s32[8,256]{1,0:T(8,128)S(1)}, s32[8,256]{1,0:T(8,128)S(1)}, u32[]{:S(2)}, u32[]{:S(2)}) collective-permute-start(s32[8,256]{1,0:T(8,128)S(1)} %reshape.17.own), channel_id=1, source_target_pairs={{0,2},{1,3},{2,0},{3,1},{4,6},{5,7},{6,4},{7,5},{8,10},{9,11},{10,... | collective-permute-start | bytes 24584 | tf_op jit(solution)/shard_map/ppermute | solution.py:430
  7.1 2.7 %collective-permute-start.1 = (s32[8,256]{1,0:T(8,128)S(1)}, s32[8,256]{1,0:T(8,128)S(1)}, u32[]{:S(2)}, u32[]{:S(2)}) collective-permute-start(s32[8,256]{1,0:T(8,128)S(1)} %reshape.17.own), channel_id=1, source_target_pairs={{0,1},{1,0},{2,3},{3,2},{4,5},{5,4},{6,7},{7,6},{8,9},{9,8},{10,11... | collective-permute-start | bytes 24584 | tf_op jit(solution)/shard_map/ppermute | solution.py:430
  9.8 1.5 %collective-permute-start.5 = (bf16[2,200,200]{2,1,0:T(8,128)(2,1)S(1)}, bf16[2,200,200]{2,1,0:T(8,128)(2,1)S(1)}, u32[]{:S(2)}, u32[]{:S(2)}) collective-permute-start(bf16[2,200,200]{2,1,0:T(8,128)(2,1)S(1)} %collective-permute-done.a1), channel_id=1, source_target_pairs={{0,1},{1,0},{2,3},{3,2},{4,5},{5,4},{6,7},{7,6},{8,9},{9,8},{10,11... | collective-permute-start | bytes 480008 | tf_op jit(solution)/shard_map/ppermute | solution.py:430
  9.9 7.3 %collective-permute-start.4 = (bf16[2,200,200]{2,1,0:T(8,128)(2,1)S(1)}, bf16[2,200,200]{2,1,0:T(8,128)(2,1)S(1)}, u32[]{:S(2)}, u32[]{:S(2)}) collective-permute-start(bf16[2,200,200]{2,1,0:T(8,128)(2,1)S(1)} %collective-permute-done.a1), channel_id=1, source_target_pairs={{0,8},{1,5},{2,10},{3,7},{4,0},{5,13},{6,2},{7,15},{8,16},{9,1},{1... | collective-permute-start | bytes 480008 | tf_op jit(solution)/shard_map/ppermute | solution.py:441
  11.3 13.4 %collective-permute-start.9 = (bf16[200,512]{1,0:T(8,128)(2,1)S(1)}, bf16[200,512]{1,0:T(8,128)(2,1)S(1)}, u32[]{:S(2)}, u32[]{:S(2)}) collective-permute-start(bf16[200,512]{1,0:T(8,128)(2,1)S(1)} %fusion), channel_id=1, source_target_pairs={{0,28},{4,0},{8,4},{12,8},{16,12},{20,16},{24,20},{28,24},{1,29},{... | collective-permute-start | bytes 614408 | tf_op jit(solution)/shard_map/ppermute | solution.py:22
  17.2 7.4 %collective-permute-start.8 = (bf16[2,200,200]{2,1,0:T(8,128)(2,1)S(1)}, bf16[2,200,200]{2,1,0:T(8,128)(2,1)S(1)}, u32[]{:S(2)}, u32[]{:S(2)}) collective-permute-start(bf16[2,200,200]{2,1,0:T(8,128)(2,1)S(1)} %collective-permute-done.4.a2), channel_id=1, source_target_pairs={{0,1},{1,0},{2,3},{3,2},{4,5},{5,4},{6,7},{7,6},{8,9},{9,8},{10,11... | collective-permute-start | bytes 480008 | tf_op jit(solution)/shard_map/ppermute | solution.py:430
  17.2 7.4 %collective-permute-start.6 = (bf16[2,200,200]{2,1,0:T(8,128)(2,1)S(1)}, bf16[2,200,200]{2,1,0:T(8,128)(2,1)S(1)}, u32[]{:S(2)}, u32[]{:S(2)}) collective-permute-start(bf16[2,200,200]{2,1,0:T(8,128)(2,1)S(1)} %collective-permute-done.4.a2), channel_id=1, source_target_pairs={{0,8},{1,5},{2,10},{3,7},{4,0},{5,13},{6,2},{7,15},{8,16},{9,1},{1... | collective-permute-start | bytes 480008 | tf_op jit(solution)/shard_map/ppermute | solution.py:441
  17.2 7.4 %collective-permute-start.7 = (bf16[1,200,200]{2,1,0:T(8,128)(2,1)S(1)}, bf16[1,200,200]{2,1,0:T(8,128)(2,1)S(1)}, u32[]{:S(2)}, u32[]{:S(2)}) collective-permute-start(bf16[1,200,200]{2,1,0:T(8,128)(2,1)S(1)} %constant_dynamic-slice_fusion), channel_id=1, source_target_pairs={{0,16},{1,13},{2,18},{3,15},{4,8},{5,21},{6,10},{7,23},{8,24},{9,5... | collective-permute-start | bytes 240008 | tf_op jit(solution)/shard_map/ppermute | solution.py:441
  24.7 2.0 %collective-permute-start.12 = (bf16[200,512]{1,0:T(8,128)(2,1)S(1)}, bf16[200,512]{1,0:T(8,128)(2,1)S(1)}, u32[]{:S(2)}, u32[]{:S(2)}) collective-permute-start(bf16[200,512]{1,0:T(8,128)(2,1)S(1)} %collective-permute-done.9.mine), channel_id=1, source_target_pairs={{0,1},{1,0},{2,3},{3,2},{4,5},{5,4},{6,7},{7,6},{8,9},{9,8},{10,11... | collective-permute-start | bytes 614408 | tf_op jit(solution)/shard_map/ppermute | solution.py:430
  24.7 1.9 %collective-permute-start.11 = (bf16[2,200,200]{2,1,0:T(8,128)(2,1)S(1)}, bf16[2,200,200]{2,1,0:T(8,128)(2,1)S(1)}, u32[]{:S(2)}, u32[]{:S(2)}) collective-permute-start(bf16[2,200,200]{2,1,0:T(8,128)(2,1)S(1)} %collective-permute-done.6.a3), channel_id=1, source_target_pairs={{0,1},{1,0},{2,3},{3,2},{4,5},{5,4},{6,7},{7,6},{8,9},{9,8},{10,11... | collective-permute-start | bytes 480008 | tf_op jit(solution)/shard_map/ppermute | solution.py:430
  25.2 1.4 %collective-permute-start.10 = (bf16[1,200,200]{2,1,0:T(8,128)(2,1)S(1)}, bf16[1,200,200]{2,1,0:T(8,128)(2,1)S(1)}, u32[]{:S(2)}, u32[]{:S(2)}) collective-permute-start(bf16[1,200,200]{2,1,0:T(8,128)(2,1)S(1)} %collective-permute-done.7.a4), channel_id=1, source_target_pairs={{0,1},{1,0},{2,3},{3,2},{4,5},{5,4},{6,7},{7,6},{8,9},{9,8},{10,11... | collective-permute-start | bytes 240008 | tf_op jit(solution)/shard_map/ppermute | solution.py:430
  29.8 11.3 %collective-permute-start.13 = (bf16[320,128]{1,0:T(8,128)(2,1)S(1)}, bf16[320,128]{1,0:T(8,128)(2,1)S(1)}, u32[]{:S(2)}, u32[]{:S(2)}) collective-permute-start(bf16[320,128]{1,0:T(8,128)(2,1)S(1)} %get-tuple-element.75), channel_id=1, source_target_pairs={{0,20},{1,25},{2,30},{3,31},{4,28},{5,17},{6,26},{7,27},{8,12},{9,... | collective-permute-start | bytes 245768 | tf_op jit(solution)/shard_map/ppermute | solution.py:441
  31.6 9.4 %collective-permute-start.14 = (bf16[320,128]{1,0:T(8,128)(2,1)S(1)}, bf16[320,128]{1,0:T(8,128)(2,1)S(1)}, u32[]{:S(2)}, u32[]{:S(2)}) collective-permute-start(bf16[320,128]{1,0:T(8,128)(2,1)S(1)} %get-tuple-element.76), channel_id=1, source_target_pairs={{0,24},{1,21},{2,18},{3,15},{4,16},{5,29},{6,10},{7,23},{8,28},{9,... | collective-permute-start | bytes 245768 | tf_op jit(solution)/shard_map/ppermute | solution.py:441
  33.6 8.2 %collective-permute-start.15 = (bf16[320,128]{1,0:T(8,128)(2,1)S(1)}, bf16[320,128]{1,0:T(8,128)(2,1)S(1)}, u32[]{:S(2)}, u32[]{:S(2)}) collective-permute-start(bf16[320,128]{1,0:T(8,128)(2,1)S(1)} %get-tuple-element.77), channel_id=1, source_target_pairs={{0,12},{1,17},{2,6},{3,11},{4,20},{5,9},{6,14},{7,3},{8,4},{9,25},... | collective-permute-start | bytes 245768 | tf_op jit(solution)/shard_map/ppermute | solution.py:441
  33.8 8.0 %collective-permute-start.16 = (bf16[320,128]{1,0:T(8,128)(2,1)S(1)}, bf16[320,128]{1,0:T(8,128)(2,1)S(1)}, u32[]{:S(2)}, u32[]{:S(2)}) collective-permute-start(bf16[320,128]{1,0:T(8,128)(2,1)S(1)} %get-tuple-element.78), channel_id=1, source_target_pairs={{0,0},{1,1},{2,10},{3,7},{4,4},{5,5},{6,2},{7,15},{8,8},{9,9},{10,... | collective-permute-start | bytes 245768 | tf_op jit(solution)/shard_map/ppermute | solution.py:441
  35.7 12.5 %copy-start = (f32[1024,200]{0,1:T(8,128)S(1)}, f32[1024,200]{0,1:T(8,128)}, u32[]{:S(2)}) copy-start(f32[1024,200]{0,1:T(8,128)} %param.8) | copy-start | bytes 2457604
  35.7 12.5 %copy-start.3 = (f32[1024]{0:T(1024)S(1)}, f32[1024]{0:T(1024)}, u32[]{:S(2)}) copy-start(f32[1024]{0:T(1024)} %param.9) | copy-start | bytes 12292
  35.7 10.1 %collective-permute-start.19 = (bf16[200,512]{1,0:T(8,128)(2,1)S(1)}, bf16[200,512]{1,0:T(8,128)(2,1)S(1)}, u32[]{:S(2)}, u32[]{:S(2)}) collective-permute-start(bf16[200,512]{1,0:T(8,128)(2,1)S(1)} %targets.1), channel_id=1, source_target_pairs={{0,4},{4,8},{8,12},{12,16},{16,20},{20,24},{24,28},{28,0},{1,5},{5... | collective-permute-start | bytes 614408 | tf_op jit(solution)/shard_map/ppermute | solution.py:22
  41.0 8.6 %copy-start.1 = (f32[2,200,200]{2,1,0:T(8,128)S(1)}, f32[2,200,200]{2,1,0:T(8,128)}, u32[]{:S(2)}) copy-start(f32[2,200,200]{2,1,0:T(8,128)} %operators.1) | copy-start | bytes 960004
  41.9 6.2 %collective-permute-start.17 = (bf16[320,128]{1,0:T(8,128)(2,1)S(1)}, bf16[320,128]{1,0:T(8,128)(2,1)S(1)}, u32[]{:S(2)}, u32[]{:S(2)}) collective-permute-start(bf16[320,128]{1,0:T(8,128)(2,1)S(1)} %add_convert_fusion), channel_id=1, source_target_pairs={{0,2},{1,3},{2,0},{3,1},{4,6},{5,7},{6,4},{7,5},{8,10},{9,11},{10,... | collective-permute-start | bytes 245768 | tf_op jit(solution)/shard_map/ppermute | solution.py:430
  45.8 2.4 %collective-permute-start.20 = (bf16[200,512]{1,0:T(8,128)(2,1)S(1)}, bf16[200,512]{1,0:T(8,128)(2,1)S(1)}, u32[]{:S(2)}, u32[]{:S(2)}) collective-permute-start(bf16[200,512]{1,0:T(8,128)(2,1)S(1)} %collective-permute-done.19.mine), channel_id=1, source_target_pairs={{0,1},{1,0},{2,3},{3,2},{4,5},{5,4},{6,7},{7,6},{8,9},{9,8},{10,11... | collective-permute-start | bytes 614408 | tf_op jit(solution)/shard_map/ppermute | solution.py:430
  48.1 1.5 %collective-permute-start.18 = (f32[320,128]{1,0:T(8,128)S(1)}, f32[320,128]{1,0:T(8,128)S(1)}, u32[]{:S(2)}, u32[]{:S(2)}) collective-permute-start(f32[320,128]{1,0:T(8,128)S(1)} %convert_add_fusion.own), channel_id=1, source_target_pairs={{0,1},{1,0},{2,3},{3,2},{4,5},{5,4},{6,7},{7,6},{8,9},{9,8},{10,11... | collective-permute-start | bytes 491528 | tf_op jit(solution)/shard_map/ppermute | solution.py:430
  (1 other events, 8.6 us)
